TPU v7x, 32 devices: a whole 2x2x4 slice. The times are simulated.
32 devices in a mesh: batch: 8 (over y, x, core), expert: 4 (over z).
Axes of the slice: x: 2, y: 2, z: 4, core: 2. Of those that a mesh axis runs over, the one named last changes fastest.
Arguments:
- dense_feats: float32 [32768, 13], P(('batch', 'expert')), may hold values from -6 to 6
- picks: int32 [32768, 26], P(('batch', 'expert')), may hold values from 0 to 16383, as said below
- labels: int32 [32768, 2], P(('batch', 'expert')), may hold values from 0 to 1
- label_mask: int32 [32768, 2], P(('batch', 'expert')), may hold values from 0 to 1
- requests: int32 [32, 8, 4, 512], P(('batch', 'expert')), may hold values from 0 to 4095
- table: float32 [131072, 16], P(('batch', 'expert')), may hold values from -6 to 6
- table_m: float32 [131072, 16], P(('batch', 'expert')), may hold values from -9.536743e-06 to 9.536743e-06
- table_v: float32 [131072, 16], P(('batch', 'expert')), may hold values from 3.7252902e-14 to 1.4901161e-13
- first_w: float32 [4, 512, 256], P('expert', 'batch'), may hold values from -1 to 1
- first_m: float32 [4, 512, 256], P('expert', 'batch'), may hold values from -0.00024414062 to 0.00024414062
- first_v: float32 [4, 512, 256], P('expert', 'batch'), may hold values from 2.746582e-11 to 1.0986328e-10
- second_w: float32 [4, 256, 128], P('expert', 'batch'), may hold values from -1.25 to 1.25
- second_m: float32 [4, 256, 128], P('expert', 'batch'), may hold values from -0.00024414062 to 0.00024414062
- second_v: float32 [4, 256, 128], P('expert', 'batch'), may hold values from 2.746582e-11 to 4.394531e-10
- small: float32 [23626], replicated
- small_m: float32 [23626], replicated, may hold values from -0.0024414062 to 0.0024414062
- small_v: float32 [23626], replicated, may hold values from 2.746582e-09 to 4.3945313e-08
Outputs:
- loss: float32 [], replicated
- new_table: float32 [131072, 16], P(('batch', 'expert'))
- new_table_m: float32 [131072, 16], P(('batch', 'expert'))
- new_table_v: float32 [131072, 16], P(('batch', 'expert'))
- new_first: float32 [4, 512, 256], P('expert', 'batch')
- new_first_m: float32 [4, 512, 256], P('expert', 'batch')
- new_first_v: float32 [4, 512, 256], P('expert', 'batch')
- new_second: float32 [4, 256, 128], P('expert', 'batch')
- new_second_m: float32 [4, 256, 128], P('expert', 'batch')
- new_second_v: float32 [4, 256, 128], P('expert', 'batch')
- new_small: float32 [23626], replicated
- new_small_m: float32 [23626], replicated
- new_small_v: float32 [23626], replicated
Inputs may be any that keep to these rules, and one draw needn't show every extreme that they name: `picks`: slot of the impression's own device's request buffer; an impression t with b = (t % 1024) // 64 asks only slots s with (s % 512) // 32 == b. `requests`: row within the owner's 4096 rows.
All inputs are finite; a program needn't handle non-finite values.
Results may differ from a plain program's by a relative error of at most 0.018.
Values may be sent and summed in bfloat16 or wider, within the bound.
A program may use at most 128 MiB of HBM per device.

v0:
```python
import jax
import jax.numpy as jnp
from jax import lax
from jax.sharding import PartitionSpec as P

FIELDS = 26
EMB = 16
DENSE = 13
DOUT = 96
HID = 256
OUT = 128
TOWER = 64
TASKS = 2
STEP = 5
GROUP_TOK = 64
INPUT = 512


HI = lax.Precision.HIGHEST


def unpack(flat, experts):
    shapes = [
        (experts, HID),
        (experts, OUT),
        (DENSE + 1, DOUT),
        (INPUT + 1, TASKS * experts),
        (TASKS, OUT + 1, TOWER),
        (TASKS, TOWER + 1),
    ]
    parts = []
    offset = 0
    for shape in shapes:
        length = 1
        for extent in shape:
            length = length * extent
        parts.append(flat[offset : offset + length].reshape(shape))
        offset = offset + length
    return parts


def adamw(weight, first, second, grad, rate):
    first = 0.9 * first + 0.1 * grad
    second = 0.999 * second + 0.001 * grad * grad
    fix_one = 1.0 - 0.9**STEP
    fix_two = 1.0 - 0.999**STEP
    weight = weight - rate * (
        first / fix_one / (jnp.sqrt(second / fix_two) + 1e-08) + 0.01 * weight
    )
    return (weight, first, second)


def silu_slope(value):
    sig = jax.nn.sigmoid(value)
    return sig * (1.0 + value * (1.0 - sig))


def split_three(values):
    upper = values.astype(jnp.bfloat16)
    rest = values - upper.astype(jnp.float32)
    middle = rest.astype(jnp.bfloat16)
    lower_part = (rest - middle.astype(jnp.float32)).astype(jnp.bfloat16)
    return jnp.concatenate([upper, middle, lower_part], -1)


def join_three(values):
    return values[:, :EMB] + values[:, EMB : 2 * EMB] + values[:, 2 * EMB :]


def one_hot(index, extent):
    return (index[:, None] == jnp.arange(extent, dtype=jnp.int32)[None, :]).astype(jnp.bfloat16)


def pick_rows(index, source):
    return jnp.dot(
        one_hot(index, source.shape[0]), source, preferred_element_type=jnp.float32
    ).astype(jnp.bfloat16)


def add_rows(index, values, extent):
    spread = lax.dot_general(
        one_hot(index, extent),
        split_three(values),
        (((0,), (0,)), ((), ())),
        preferred_element_type=jnp.float32,
    )
    return join_three(spread)


def expert_forward(inputs, first_w, second_w, first_b, second_b):
    pre_one = (
        jnp.einsum("ti,eih->teh", inputs, first_w, preferred_element_type=jnp.float32)
        + first_b[None]
    )
    hidden = jax.nn.silu(pre_one).astype(jnp.bfloat16)
    pre_two = (
        jnp.einsum("teh,eho->teo", hidden, second_w, preferred_element_type=jnp.float32)
        + second_b[None]
    )
    return (pre_one, hidden, pre_two, jax.nn.silu(pre_two))


def expert_backward(inputs, first_w, second_w, pre_one, hidden, pre_two, d_out):
    d_two = (silu_slope(pre_two) * d_out).astype(jnp.bfloat16)
    d_second_w = jnp.einsum("teh,teo->eho", hidden, d_two, preferred_element_type=jnp.float32)
    d_second_b = jnp.sum(d_two, 0, dtype=jnp.float32)
    d_hidden = jnp.einsum("teo,eho->teh", d_two, second_w, preferred_element_type=jnp.float32)
    d_one = (silu_slope(pre_one) * d_hidden).astype(jnp.bfloat16)
    d_first_w = jnp.einsum("ti,teh->eih", inputs, d_one, preferred_element_type=jnp.float32)
    d_first_b = jnp.sum(d_one, 0, dtype=jnp.float32)
    d_inputs = jnp.einsum("teh,eih->ti", d_one, first_w, preferred_element_type=jnp.float32)
    return (d_first_w, d_second_w, d_first_b, d_second_b, d_inputs)


def local(
    dense_feats,
    picks,
    labels,
    label_mask,
    requests,
    table,
    table_m,
    table_v,
    first_w,
    first_m,
    first_v,
    second_w,
    second_m,
    second_v,
    small,
    small_m,
    small_v,
):
    groups = lax.axis_size("batch")
    experts = lax.axis_size("expert")
    devices = groups * experts
    expert_idx = lax.axis_index("expert")
    tokens = dense_feats.shape[0]
    slots = requests.shape[-1]
    rows_dev = table.shape[0]
    tok_groups = tokens // GROUP_TOK
    sub_slots = slots // tok_groups
    group_slots = devices * sub_slots
    total_asked = devices * slots
    ask_block = min(1024, total_asked)
    bias_one, bias_two, dense_w, gate_w, tower_w, head_w = unpack(small, experts)
    first_full, second_full = (
        lax.all_gather(first_w.astype(jnp.bfloat16), "batch", axis=1, tiled=True),
        lax.all_gather(second_w.astype(jnp.bfloat16), "batch", axis=1, tiled=True),
    )
    asked = lax.all_to_all(
        lax.all_to_all(requests[0], "batch", split_axis=0, concat_axis=0, tiled=True),
        "expert",
        split_axis=1,
        concat_axis=1,
        tiled=True,
    )
    asked_blocks = asked.reshape(total_asked // ask_block, ask_block)
    table_low = table.astype(jnp.bfloat16)
    sent_rows = lax.map(lambda index: pick_rows(index, table_low), asked_blocks)
    sent_rows = sent_rows.reshape(groups, experts, slots * EMB)
    got_rows = lax.all_to_all(
        lax.all_to_all(sent_rows, "batch", split_axis=0, concat_axis=0, tiled=True),
        "expert",
        split_axis=1,
        concat_axis=1,
        tiled=True,
    )
    by_group = (
        got_rows.reshape(devices, tok_groups, sub_slots, EMB)
        .transpose(1, 0, 2, 3)
        .reshape(tok_groups, group_slots, EMB)
    )
    local_pick = (picks // slots * sub_slots + picks % sub_slots).reshape(
        tok_groups, GROUP_TOK * FIELDS
    )
    emb = lax.map(lambda item: pick_rows(item[0], item[1]), (local_pick, by_group)).reshape(
        tokens, FIELDS * EMB
    )
    dense_proj = jnp.dot(dense_feats, dense_w[:DENSE], precision=HI) + dense_w[DENSE]
    inputs = jnp.concatenate([emb, dense_proj.astype(jnp.bfloat16)], 1)
    gate_low = gate_w[:INPUT].astype(jnp.bfloat16)
    gate_logits = jnp.dot(inputs, gate_low, preferred_element_type=jnp.float32) + gate_w[INPUT]
    probs = jax.nn.softmax(gate_logits.reshape(tokens, TASKS, experts), axis=-1)
    gates = probs.astype(jnp.bfloat16)
    all_inputs, all_gates = (
        lax.all_gather(inputs, "expert", axis=0, tiled=True),
        lax.all_gather(gates.reshape(tokens, TASKS * experts), "expert", axis=0, tiled=True),
    )
    own_gates = lax.dynamic_slice_in_dim(
        all_gates.reshape(-1, TASKS, experts), expert_idx, 1, 2
    ).astype(jnp.float32)
    first_use, second_use = (first_full, second_full)
    first_b = lax.dynamic_slice_in_dim(bias_one, expert_idx, 1, 0)
    second_b = lax.dynamic_slice_in_dim(bias_two, expert_idx, 1, 0)
    pre_one, hidden, pre_two, expert_out = expert_forward(
        all_inputs, first_use, second_use, first_b, second_b
    )
    terms = jnp.einsum("tke,teo->tko", own_gates, expert_out, precision=HI).reshape(-1, TASKS * OUT)
    mixed = lax.psum_scatter(terms.astype(jnp.bfloat16), "expert", scatter_dimension=0, tiled=True)
    mask = label_mask.astype(jnp.float32)
    target = labels.astype(jnp.float32)
    counts = jnp.maximum(lax.psum(jnp.sum(mask, 0), ("batch", "expert")), 1.0)
    mixed_low = mixed.reshape(tokens, TASKS, OUT)
    tower_low = tower_w[:, :OUT].astype(jnp.bfloat16)
    tower_pre = (
        jnp.einsum("tko,koh->tkh", mixed_low, tower_low, preferred_element_type=jnp.float32)
        + tower_w[:, OUT][None]
    )
    tower_act = jax.nn.silu(tower_pre)
    logits = jnp.einsum("tkh,kh->tk", tower_act, head_w[:, :TOWER], precision=HI) + head_w[:, TOWER]
    loss_local = jnp.sum(mask * (jax.nn.softplus(logits) - target * logits) / counts)
    d_logits = mask * (jax.nn.sigmoid(logits) - target) / counts
    d_head = jnp.concatenate(
        [
            jnp.einsum("tkh,tk->kh", tower_act, d_logits, precision=HI),
            jnp.sum(d_logits, 0)[:, None],
        ],
        1,
    )
    d_act = d_logits[:, :, None] * head_w[None, :, :TOWER]
    d_tower_pre = (silu_slope(tower_pre) * d_act).astype(jnp.bfloat16)
    d_tower = jnp.concatenate(
        [
            jnp.einsum("tko,tkh->koh", mixed_low, d_tower_pre, preferred_element_type=jnp.float32),
            jnp.sum(d_tower_pre, 0, dtype=jnp.float32)[:, None, :],
        ],
        1,
    )
    d_mixed = jnp.einsum(
        "tkh,koh->tko", d_tower_pre, tower_low, preferred_element_type=jnp.float32
    ).astype(jnp.bfloat16)
    all_d_mixed = (
        lax.all_gather(d_mixed.reshape(tokens, TASKS * OUT), "expert", axis=0, tiled=True)
        .reshape(-1, TASKS, OUT)
        .astype(jnp.float32)
    )
    d_out = jnp.einsum("tke,tko->teo", own_gates, all_d_mixed, precision=HI)
    d_gate_col = jnp.einsum("teo,tko->tke", expert_out, all_d_mixed, precision=HI)
    d_first_w, d_second_w, d_first_b, d_second_b, d_rows = expert_backward(
        all_inputs, first_use, second_use, pre_one, hidden, pre_two, d_out
    )
    onehot = (jnp.arange(experts) == expert_idx).astype(jnp.float32)
    d_gate_full = (d_gate_col * onehot[None, None, :]).reshape(-1, TASKS * experts)
    d_inputs, d_gates = (
        lax.psum_scatter(
            d_rows.astype(jnp.bfloat16), "expert", scatter_dimension=0, tiled=True
        ).astype(jnp.float32),
        lax.psum_scatter(
            d_gate_full.astype(jnp.bfloat16), "expert", scatter_dimension=0, tiled=True
        ).astype(jnp.float32),
    )
    d_gates = d_gates.reshape(tokens, TASKS, experts)
    d_first_b = onehot[:, None] * d_first_b
    d_second_b = onehot[:, None] * d_second_b
    d_gate_logits = (
        (probs * (d_gates - jnp.sum(probs * d_gates, -1, keepdims=True)))
        .astype(jnp.bfloat16)
        .reshape(tokens, TASKS * experts)
    )
    d_gate_w = jnp.concatenate(
        [
            jnp.dot(inputs.T, d_gate_logits, preferred_element_type=jnp.float32),
            jnp.sum(d_gate_logits, 0, dtype=jnp.float32)[None],
        ],
        0,
    )
    d_x = d_inputs + jnp.dot(d_gate_logits, gate_low.T, preferred_element_type=jnp.float32)
    d_dense = d_x[:, FIELDS * EMB :]
    d_dense_w = jnp.concatenate(
        [jnp.dot(dense_feats.T, d_dense, precision=HI), jnp.sum(d_dense, 0)[None]], 0
    )
    d_emb = d_x[:, : FIELDS * EMB].reshape(tok_groups, GROUP_TOK * FIELDS, EMB)
    slot_grads = lax.map(lambda item: add_rows(item[0], item[1], group_slots), (local_pick, d_emb))
    slot_grads = (
        slot_grads.reshape(tok_groups, devices, sub_slots, EMB)
        .transpose(1, 0, 2, 3)
        .reshape(groups, experts, slots * EMB)
    )
    owner_grads = lax.all_to_all(
        lax.all_to_all(
            slot_grads.astype(jnp.bfloat16), "batch", split_axis=0, concat_axis=0, tiled=True
        ),
        "expert",
        split_axis=1,
        concat_axis=1,
        tiled=True,
    ).astype(slot_grads.dtype)
    owner_blocks = owner_grads.reshape(total_asked // ask_block, ask_block, EMB)

    def add_block(total, item):
        return (total + add_rows(item[0], item[1], rows_dev), None)

    table_grad, unused = lax.scan(
        add_block, jnp.zeros((rows_dev, EMB), jnp.float32), (asked_blocks, owner_blocks)
    )
    grad_first, grad_second = (
        lax.psum_scatter(
            d_first_w.astype(jnp.bfloat16), "batch", scatter_dimension=1, tiled=True
        ).astype(jnp.float32),
        lax.psum_scatter(
            d_second_w.astype(jnp.bfloat16), "batch", scatter_dimension=1, tiled=True
        ).astype(jnp.float32),
    )
    flat_grads = jnp.concatenate(
        [
            d_first_b.reshape(-1),
            d_second_b.reshape(-1),
            d_dense_w.reshape(-1),
            d_gate_w.reshape(-1),
            d_tower.reshape(-1),
            d_head.reshape(-1),
        ]
    )
    grad_small, loss = lax.psum((flat_grads, loss_local), ("batch", "expert"))
    new_table, new_table_m, new_table_v = adamw(table, table_m, table_v, table_grad, 0.3)
    new_first, new_first_m, new_first_v = adamw(first_w, first_m, first_v, grad_first, 0.15)
    new_second, new_second_m, new_second_v = adamw(second_w, second_m, second_v, grad_second, 0.15)
    new_small, new_small_m, new_small_v = adamw(small, small_m, small_v, grad_small, 0.15)
    return (
        loss,
        new_table,
        new_table_m,
        new_table_v,
        new_first,
        new_first_m,
        new_first_v,
        new_second,
        new_second_m,
        new_second_v,
        new_small,
        new_small_m,
        new_small_v,
    )


def solution(mesh):
    return jax.shard_map(
        local,
        mesh=mesh,
        in_specs=(
            P(("batch", "expert"), None),
            P(("batch", "expert"), None),
            P(("batch", "expert"), None),
            P(("batch", "expert"), None),
            P(("batch", "expert"), None, None, None),
            P(("batch", "expert"), None),
            P(("batch", "expert"), None),
            P(("batch", "expert"), None),
            P("expert", "batch", None),
            P("expert", "batch", None),
            P("expert", "batch", None),
            P("expert", "batch", None),
            P("expert", "batch", None),
            P("expert", "batch", None),
            P(),
            P(),
            P(),
        ),
        out_specs=(
            P(),
            P(("batch", "expert"), None),
            P(("batch", "expert"), None),
            P(("batch", "expert"), None),
            P("expert", "batch", None),
            P("expert", "batch", None),
            P("expert", "batch", None),
            P("expert", "batch", None),
            P("expert", "batch", None),
            P("expert", "batch", None),
            P(),
            P(),
            P(),
        ),
        check_vma=False,
    )
```

profile of v0, /device:TPU:0, one launch (start us, length us, event | category | flops | bytes accessed | tf_op | source)
XLA Modules:
  0.0 857.6 jit_solution(4808666217549866992)
XLA Ops:
  7.2 10.3 %all_to_all.30 = s32[8,4,512]{2,1,0:T(4,128)S(1)} all-to-all(s32[8,4,512]{2,1,0:T(4,128)} %bitcast.261), channel_id=1, replica_groups=mesh['batch'=8,'expert'=4] {'batch'}, dimensions={0} | all-to-all | bytes 131072 | tf_op jit(solution)/shard_map/all_to_all | solution.py:152
  18.2 4.9 all-to-all-start.1
  24.0 4.8 all-to-all-done.1
  28.9 49.9 %while.41 = (s32[]{:T(128)}, bf16[16,1024,16]{1,2,0:T(8,128)(2,1)S(1)}, s32[16,1024]{1,0:T(8,128)S(1)}, bf16[4096,16]{0,1:T(8,128)(2,1)S(1)}, s32[]{:T(128)}) while((s32[]{:T(128)}, bf16[16,1024,16]{1,2,0:T(8,128)(2,1)S(1)}, s32[16,1024]{1,0:T(8,128)S(1)}, bf16[4096,16]{0,1:T(8,128)(2,1)S(1)}, s32[]{:T(128)}) %tuple.107), condition=%wide.region_1.2_spmd, body=%wide.region_0.1_spmd.sunk | while | flops 138428416 | bytes 176205 | solution.py:160
  81.9 6.1 reshape.219
  88.0 12.3 %all_to_all.31 = bf16[8,4,8192]{2,1,0:T(4,128)(2,1)S(1)} all-to-all(bf16[8,4,8192]{2,1,0:T(4,128)(2,1)S(1)} %reshape.219), channel_id=1, replica_groups=mesh['batch'=8,'expert'=4] {'batch'}, dimensions={0} | all-to-all | bytes 1048576 | tf_op jit(solution)/shard_map/all_to_all | solution.py:163
  101.4 3.5 all-to-all-start.3
  106.5 12.4 %all-to-all-done.3 = bf16[8,4,8192]{2,0,1:T(8,128)(2,1)S(1)} async-done(((bf16[8,4,8192]{2,0,1:T(8,128)(2,1)}), bf16[8,4,8192]{2,0,1:T(8,128)(2,1)S(1)}, u32[]{:S(2)}, u32[]{:S(2)}) %all-to-all-start.3) | async-done | bytes 524320 | tf_op jit(solution)/shard_map/all_to_all | solution.py:162
  119.3 4.3 reshape.220
  123.6 5.1 copy.198
  131.7 34.4 %while.42 = (s32[]{:T(128)}, bf16[16,1664,16]{1,2,0:T(8,128)(2,1)S(1)}, s32[16,1664]{1,0:T(8,128)S(1)}, bf16[16,1024,16]{1,2,0:T(8,128)(2,1)}, s32[]{:T(128)}) while((s32[]{:T(128)}, bf16[16,1664,16]{1,2,0:T(8,128)(2,1)S(1)}, s32[16,1664]{1,0:T(8,128)S(1)}, bf16[16,1024,16]{1,2,0:T(8,128)(2,1)}, s32[]{:T(128)}) %tuple.110), condition=%wide.region_3.4_spmd, body=%wide.region_2.3_spmd.sunk | while | flops 56256512 | bytes 108617 | solution.py:177
  166.1 4.7 copy.199
  170.8 7.6 reshape.222
  180.2 9.0 %all_gather.18 = bf16[1,256,128]{2,1,0:T(8,128)(2,1)S(1)} all-gather(bf16[1,32,128]{2,1,0:T(8,128)(2,1)S(1)} %convert_element_type.174), channel_id=1, replica_groups=mesh['batch'=8,'expert'=4] {'batch'}, dimensions={1}, use_global_device_ids=true | all-gather | bytes 73728 | tf_op jit(solution)/shard_map/all_gather | solution.py:149
  189.2 8.5 all_gather.17
  200.3 14.1 %all_gather.15 = bf16[4096,8]{0,1:T(8,128)(2,1)S(1)} all-gather(bf16[1024,8]{0,1:T(8,128)(2,1)S(1)} %fusion.95), channel_id=1, replica_groups=mesh['batch'=8,'expert'=4] {'expert'}, dimensions={0}, use_global_device_ids=true | all-gather | bytes 81920 | tf_op jit(solution)/shard_map/all_gather | solution.py:188
  214.5 45.1 %all-gather.3.cloned.1.call-done = bf16[4096,512]{1,0:T(8,128)(2,1)} async-done(((bf16[1024,512]{1,0:T(8,128)(2,1)}), bf16[4096,512]{1,0:T(8,128)(2,1)}) %all-gather.3.cloned.1.call-update) | async-done | bytes 4194320 | tf_op jit(solution)/shard_map/all_gather | solution.py:187
  259.6 5.4 multiply_convert_fusion.1
  275.3 43.1 %psum.21 = f32[2]{0:T(128)S(1)} all-reduce(f32[2]{0:T(128)S(1)} %convert_reduce_fusion.4), channel_id=1, replica_groups=mesh['batch'=8,'expert'=4] {'batch','expert'}, use_global_device_ids=true, to_apply=%region_8.9 | all-reduce | flops 2 | bytes 16 | tf_op jit(solution)/shard_map/psum | solution.py:203
  324.3 45.0 %all-gather.5.cloned.1.call-done = bf16[4096,256]{0,1:T(8,128)(2,1)} async-done(((bf16[1024,256]{0,1:T(8,128)(2,1)}), bf16[4096,256]{0,1:T(8,128)(2,1)}) %all-gather.5.cloned.1.call-update) | async-done | bytes 2097168 | tf_op jit(solution)/shard_map/all_gather | solution.py:234
  369.3 3.6 multiply_reduce_fusion.1
  384.0 4.5 convert_reduce_fusion
  388.6 3.5 fusion.48
  396.8 39.4 %psum.22 = f32[]{:T(128)} all-reduce(f32[]{:T(128)} %get-tuple-element.308), channel_id=1, replica_groups=mesh['batch'=8,'expert'=4] {'batch','expert'}, use_global_device_ids=true, to_apply=%region_10.11 | all-reduce | flops 1 | bytes 8 | tf_op jit(solution)/shard_map/psum | solution.py:315
  442.2 27.4 %reduce-scatter.16.cloned.1.call-done = bf16[64,256]{1,0:T(8,128)(2,1)} async-done(((bf16[512,256]{1,0:T(8,128)(2,1)}), bf16[64,256]{1,0:T(8,128)(2,1)}) %reduce-scatter.16.cloned.1.call-update) | async-done | bytes 32784
  470.5 78.3 %reduce-scatter.10.cloned.1.call-done = bf16[1024,512]{1,0:T(8,128)(2,1)} async-done(((bf16[4096,512]{1,0:T(8,128)(2,1)}), bf16[1024,512]{1,0:T(8,128)(2,1)}) %reduce-scatter.10.cloned.1.call-update) | async-done | bytes 1048592 | tf_op jit(solution)/shard_map/reduce_scatter | solution.py:246
  550.5 7.9 reshape.239
  558.3 9.1 %copy.206 = f32[16,1664,16]{1,2,0:T(8,128)} copy(f32[16,1664,16]{2,1,0:T(8,128)} %reshape.239) | data formatting | bytes 3407872 | tf_op jit(solution)/shard_map/while | solution.py:274
  567.5 49.3 %while.43 = (s32[]{:T(128)}, bf16[16,1024,16]{1,2,0:T(8,128)(2,1)S(1)}, s32[16,1664]{1,0:T(8,128)}, f32[16,1664,16]{1,2,0:T(8,128)}, s32[]{:T(128)}) while((s32[]{:T(128)}, bf16[16,1024,16]{1,2,0:T(8,128)(2,1)S(1)}, s32[16,1664]{1,0:T(8,128)}, f32[16,1664,16]{1,2,0:T(8,128)}, s32[]{:T(128)}) %tuple.136), condition=%wide.region_15.16_spmd, body=%wide.region_14.15_spmd.sunk | while | flops 165953536 | bytes 958033 | solution.py:274
  619.4 5.0 copy.207
  624.4 6.8 convert_element_type.192
  631.1 3.8 all-to-all-start.4
  636.6 8.1 all-to-all-done.4
  645.8 4.5 all-to-all-start.5
  651.0 117.7 %all-reduce.2.cloned.1.call-done = f32[23626]{0:T(1024)} async-done(((f32[23626]{0:T(1024)}), f32[23626]{0:T(1024)}) %all-reduce.2.cloned.1.call-update) | async-done | bytes 94520 | tf_op jit(solution)/shard_map/psum | solution.py:315
  770.7 4.8 reshape.247
  775.5 5.1 copy.210
  780.6 68.6 %while.44 = (s32[]{:T(128)}, f32[4096,16]{0,1:T(8,128)S(1)}, s32[16,1024]{1,0:T(8,128)}, f32[16,1024,16]{1,2,0:T(8,128)S(1)}, s32[]{:T(128)}, /*index=5*/s32[]{:T(128)}) while((s32[]{:T(128)}, f32[4096,16]{0,1:T(8,128)S(1)}, s32[16,1024]{1,0:T(8,128)}, f32[16,1024,16]{1,2,0:T(8,128)S(1)}, s32[]{:T(128)}, ...), condition=%wide.region_17.18_spmd.clone, body=%wide.region_16.17_spmd.clone.sunk | while | flops 407502848 | bytes 2404447 | solution.py:294
  781.5 3.4 fusion.148
  785.8 3.4 fusion.148
  790.1 3.4 fusion.148
  798.6 3.4 fusion.148
  802.9 3.4 fusion.148
  807.2 3.4 fusion.148
  811.5 3.4 fusion.148
  815.8 3.4 fusion.148
  820.0 3.4 fusion.148
  824.3 3.4 fusion.148
  (407 shorter events, 231.5 us)
Async XLA Ops:
  7.2 98.1 %copy-start = (f32[1024,13]{0,1:T(8,128)S(1)}, f32[1024,13]{0,1:T(8,128)}, u32[]{:S(2)}) copy-start(f32[1024,13]{0,1:T(8,128)} %param.25) | copy-start | bytes 159748
  18.2 10.6 %all-to-all-start.1 = ((s32[8,4,512]{2,0,1:T(8,128)}), s32[8,4,512]{2,0,1:T(8,128)S(1)}, u32[]{:S(2)}, u32[]{:S(2)}) async-start(s32[8,4,512]{2,0,1:T(8,128)} %copy.193), calls=%async_computation.1 | async-start | bytes 131072 | tf_op jit(solution)/shard_map/all_to_all | solution.py:151
  88.0 17.1 %copy-start.14 = (f32[23626]{0:T(1024)S(1)}, f32[23626]{0:T(1024)}, u32[]{:S(2)}) copy-start(f32[23626]{0:T(1024)} %param.39) | copy-start | bytes 283516
  88.0 18.0 %copy-start.27 = (s32[1024,26]{0,1:T(8,128)S(1)}, s32[1024,26]{0,1:T(8,128)}, u32[]{:S(2)}) copy-start(s32[1024,26]{0,1:T(8,128)} %param.26) | copy-start | bytes 319492
  101.4 17.6 %all-to-all-start.3 = ((bf16[8,4,8192]{2,0,1:T(8,128)(2,1)}), bf16[8,4,8192]{2,0,1:T(8,128)(2,1)S(1)}, u32[]{:S(2)}, u32[]{:S(2)}) async-start(bf16[8,4,8192]{2,0,1:T(8,128)(2,1)} %copy.196), calls=%async_computation.3 | async-start | bytes 1048576 | tf_op jit(solution)/shard_map/all_to_all | solution.py:162
  104.8 154.7 %all-gather.3.cloned.1.call-start = ((), (), s32[]{:S(2)}) async-start(), calls=%async_computation.11 | async-start | bytes 5242880 | tf_op jit(solution)/shard_map/all_gather | solution.py:187
  166.1 4.7 copy-start.20
  179.7 139.3 %reduce-scatter.8.cloned.1.call-start = ((), (), s32[]{:S(2)}) async-start(), calls=%async_computation.12 | async-start | bytes 2621440 | tf_op jit(solution)/shard_map/reduce_scatter | solution.py:200
  180.2 84.9 %copy-start.8 = (bf16[512,8]{1,0:T(8,128)(2,1)}, bf16[512,8]{1,0:T(8,128)(2,1)S(1)}, u32[]{:S(2)}) copy-start(bf16[512,8]{1,0:T(8,128)(2,1)S(1)} %convert_element_type.170) | copy-start | bytes 24580
  189.2 75.8 %copy-start.21 = (bf16[1,256,128]{2,1,0:T(8,128)(2,1)}, bf16[1,256,128]{2,1,0:T(8,128)(2,1)S(1)}, u32[]{:S(2)}) copy-start(bf16[1,256,128]{2,1,0:T(8,128)(2,1)S(1)} %all_gather.18) | copy-start | bytes 196612
  197.7 67.3 %copy-start.11 = (bf16[1,512,256]{2,1,0:T(8,128)(2,1)}, bf16[1,512,256]{2,1,0:T(8,128)(2,1)S(1)}, u32[]{:S(2)}) copy-start(bf16[1,512,256]{2,1,0:T(8,128)(2,1)S(1)} %all_gather.17) | copy-start | bytes 786436
  200.2 64.8 %copy-start.16 = (f32[1024,8]{0,1:T(8,128)}, f32[1024,8]{0,1:T(8,128)S(1)}, u32[]{:S(2)}) copy-start(f32[1024,8]{0,1:T(8,128)S(1)} %sub.73) | copy-start | bytes 98308
  274.5 46.3 %copy-start.39 = (s32[1024,2]{0,1:T(2,128)S(1)}, s32[1024,2]{0,1:T(2,128)}, u32[]{:S(2)}) copy-start(s32[1024,2]{0,1:T(2,128)} %param.27) | copy-start | bytes 24580
  274.5 94.8 %all-gather.5.cloned.1.call-start = ((), (), s32[]{:S(2)}) async-start(), calls=%async_computation.13 | async-start | bytes 2621440 | tf_op jit(solution)/shard_map/all_gather | solution.py:234
  323.6 115.0 %reduce-scatter.14.cloned.1.call-start = ((), (), s32[]{:S(2)}) async-start(), calls=%async_computation.16 | async-start | bytes 73728 | tf_op jit(solution)/shard_map/reduce_scatter | solution.py:301
  323.7 49.2 %copy-start.42 = (f32[4]{0:T(128)}, f32[4]{0:T(128)S(1)}, u32[]{:S(2)}) copy-start(f32[4]{0:T(128)S(1)} %compare_convert_fusion) | copy-start | bytes 52
  380.3 59.6 %reduce-scatter.12.cloned.1.call-start = ((), (), s32[]{:S(2)}) async-start(), calls=%async_computation.15 | async-start | bytes 81920 | tf_op jit(solution)/shard_map/reduce_scatter | solution.py:249
  388.6 81.1 %reduce-scatter.16.cloned.1.call-start = ((), (), s32[]{:S(2)}) async-start(), calls=%async_computation.18 | async-start | bytes 294912
  388.6 4.8 copy-start.12
  393.4 155.4 %reduce-scatter.10.cloned.1.call-start = ((), (), s32[]{:S(2)}) async-start(), calls=%async_computation.14 | async-start | bytes 5242880 | tf_op jit(solution)/shard_map/reduce_scatter | solution.py:246
  396.7 39.6 %copy-start.46 = (f32[2]{0:T(128)S(1)}, f32[2]{0:T(128)}, u32[]{:S(2)}) copy-start(f32[2]{0:T(128)} %get-tuple-element.291) | copy-start | bytes 28
  396.7 39.7 %copy-start.6 = (f32[1024,2,64]{0,2,1:T(8,128)S(1)}, f32[1024,2,64]{0,2,1:T(8,128)}, u32[]{:S(2)}) copy-start(f32[1024,2,64]{0,2,1:T(8,128)} %copy-done.5) | copy-start | bytes 1572868
  396.7 41.1 %copy-start.40 = (f32[2,64]{1,0:T(2,128)S(1)}, f32[2,64]{1,0:T(2,128)}, u32[]{:S(2)}) copy-start(f32[2,64]{1,0:T(2,128)} %get-tuple-element.293) | copy-start | bytes 1540
  396.7 41.2 %copy-start.7 = (bf16[1024,256]{0,1:T(8,128)(2,1)S(1)}, bf16[1024,256]{0,1:T(8,128)(2,1)}, u32[]{:S(2)}) copy-start(bf16[1024,256]{0,1:T(8,128)(2,1)} %reduce-scatter.8.cloned.1.call-done) | copy-start | bytes 1572868
  396.7 41.7 %copy-start.43 = (f32[4]{0:T(128)S(1)}, f32[4]{0:T(128)}, u32[]{:S(2)}) copy-start(f32[4]{0:T(128)} %copy-done.42) | copy-start | bytes 52
  396.7 41.7 %copy-start.45 = (f32[256]{0:T(256)S(1)}, f32[256]{0:T(256)}, u32[]{:S(2)}) copy-start(f32[256]{0:T(256)} %get-tuple-element.311) | copy-start | bytes 3076
  396.7 41.8 %copy-start.44 = (f32[128]{0:T(128)S(1)}, f32[128]{0:T(128)}, u32[]{:S(2)}) copy-start(f32[128]{0:T(128)} %get-tuple-element.297) | copy-start | bytes 1540
  396.7 41.8 %copy-start.33 = (f32[1,32,128]{2,1,0:T(8,128)S(1)}, f32[1,32,128]{2,1,0:T(8,128)}, u32[]{:S(2)}) copy-start(f32[1,32,128]{2,1,0:T(8,128)} %param.36) | copy-start | bytes 49156
  396.8 41.8 %copy-start.37 = (f32[1,32,128]{2,1,0:T(8,128)S(1)}, f32[1,32,128]{2,1,0:T(8,128)}, u32[]{:S(2)}) copy-start(f32[1,32,128]{2,1,0:T(8,128)} %param.37) | copy-start | bytes 49156
  396.8 41.8 %copy-start.38 = (f32[1,32,128]{2,1,0:T(8,128)S(1)}, f32[1,32,128]{2,1,0:T(8,128)}, u32[]{:S(2)}) copy-start(f32[1,32,128]{2,1,0:T(8,128)} %param.38) | copy-start | bytes 49156
  396.8 43.9 %copy-start.19 = (f32[1024,2,4]{0,2,1:T(4,128)S(1)}, f32[1024,2,4]{0,2,1:T(4,128)}, u32[]{:S(2)}) copy-start(f32[1024,2,4]{0,2,1:T(4,128)} %copy-done.18) | copy-start | bytes 98308
  396.8 43.9 %copy-start.36 = (f32[1024,2]{0,1:T(2,128)S(1)}, f32[1024,2]{0,1:T(2,128)}, u32[]{:S(2)}) copy-start(f32[1024,2]{0,1:T(2,128)} %copy-done.35) | copy-start | bytes 24580
  436.4 5.3 copy-start.4
  437.8 111.0 %copy-start.9 = (bf16[512,8]{1,0:T(8,128)(2,1)S(1)}, bf16[512,8]{1,0:T(8,128)(2,1)}, u32[]{:S(2)}) copy-start(bf16[512,8]{1,0:T(8,128)(2,1)} %copy-done.8) | copy-start | bytes 24580
  558.3 9.1 %copy-start.13 = (bf16[16,1024,16]{1,2,0:T(8,128)(2,1)S(1)}, bf16[16,1024,16]{1,2,0:T(8,128)(2,1)}, u32[]{:S(2)}) copy-start(bf16[16,1024,16]{1,2,0:T(8,128)(2,1)} %custom-call.3) | copy-start | bytes 1572868
  631.1 4.7 copy-start.41
  631.1 19.1 %copy-start.25 = (f32[1,64,256]{2,1,0:T(8,128)S(1)}, f32[1,64,256]{2,1,0:T(8,128)}, u32[]{:S(2)}) copy-start(f32[1,64,256]{2,1,0:T(8,128)} %param.33) | copy-start | bytes 196612
  631.1 19.1 %copy-start.30 = (f32[1,64,256]{2,1,0:T(8,128)S(1)}, f32[1,64,256]{2,1,0:T(8,128)}, u32[]{:S(2)}) copy-start(f32[1,64,256]{2,1,0:T(8,128)} %param.34) | copy-start | bytes 196612
  631.1 13.5 %all-to-all-start.4 = ((bf16[8,4,8192]{2,1,0:T(4,128)(2,1)}), bf16[8,4,8192]{2,1,0:T(4,128)(2,1)S(1)}, u32[]{:S(2)}, u32[]{:S(2)}) async-start(bf16[8,4,8192]{2,1,0:T(4,128)(2,1)} %convert_element_type.192), calls=%async_computation.7 | async-start | bytes 1048576 | tf_op jit(solution)/shard_map/all_to_all | solution.py:281
  634.9 133.7 %copy-start.15 = (f32[23626]{0:T(1024)S(1)}, f32[23626]{0:T(1024)}, u32[]{:S(2)}) copy-start(f32[23626]{0:T(1024)} %param.39) | copy-start | bytes 283516
  634.9 133.7 %copy-start.28 = (f32[23626]{0:T(1024)S(1)}, f32[23626]{0:T(1024)}, u32[]{:S(2)}) copy-start(f32[23626]{0:T(1024)} %param.40) | copy-start | bytes 283516
  634.9 133.7 %copy-start.29 = (f32[23626]{0:T(1024)S(1)}, f32[23626]{0:T(1024)}, u32[]{:S(2)}) copy-start(f32[23626]{0:T(1024)} %param.41) | copy-start | bytes 283516
  635.0 133.7 %all-reduce.2.cloned.1.call-start = ((), (), s32[]{:S(2)}) async-start(), calls=%async_computation.17 | async-start | bytes 196608 | tf_op jit(solution)/shard_map/psum | solution.py:315
  635.7 14.6 %copy-start.31 = (f32[1,64,256]{2,1,0:T(8,128)S(1)}, f32[1,64,256]{2,1,0:T(8,128)}, u32[]{:S(2)}) copy-start(f32[1,64,256]{2,1,0:T(8,128)} %param.35) | copy-start | bytes 196612
  645.8 124.5 %all-to-all-start.5 = ((bf16[8,4,8192]{2,0,1:T(8,128)(2,1)}), bf16[8,4,8192]{2,0,1:T(8,128)(2,1)S(1)}, u32[]{:S(2)}, u32[]{:S(2)}) async-start(bf16[8,4,8192]{2,0,1:T(8,128)(2,1)} %copy.208), calls=%async_computation.8 | async-start | bytes 1048576 | tf_op jit(solution)/shard_map/all_to_all | solution.py:280
  780.6 68.6 %copy-start.10 = (f32[4096,16]{0,1:T(8,128)S(1)}, f32[4096,16]{0,1:T(8,128)}, u32[]{:S(2)}) copy-start(f32[4096,16]{0,1:T(8,128)} %param.30) | copy-start | bytes 786436
  780.6 68.6 %copy-start.22 = (f32[4096,16]{0,1:T(8,128)S(1)}, f32[4096,16]{0,1:T(8,128)}, u32[]{:S(2)}) copy-start(f32[4096,16]{0,1:T(8,128)} %param.31) | copy-start | bytes 786436
  780.6 68.6 %copy-start.23 = (f32[4096,16]{0,1:T(8,128)S(1)}, f32[4096,16]{0,1:T(8,128)}, u32[]{:S(2)}) copy-start(f32[4096,16]{0,1:T(8,128)} %param.32) | copy-start | bytes 786436
  (12 other events, 23.1 us)
Sparse Core Ops, SparseCore 0:
  179.8 79.6 all-gather.2
  274.6 43.4 reduce-scatter.7
  323.7 45.5 all-gather.4
  380.4 31.8 reduce-scatter.13
  415.0 19.0 reduce-scatter.11
  437.8 31.7 reduce-scatter.15
  472.0 76.7 reduce-scatter.9
  642.9 125.7 all-reduce.1
where the time goes:
time: 868 us; the launch traced here: 858 us
  waiting for transfers between devices  339 us (39%)
  matrix products  184 us (21%)
  blocking collectives  137 us (16%)
  local copies, waits for them, and re-layouts  121 us (14%)
  other arithmetic  43.6 us (5%)
  starting transfers between devices  17.1 us (2%)
  between operations  15.5 us (2%)
    psum x1, waiting for transfers between devices, local(): grad_small, loss = lax.psum((flat_grads, loss_local), ('batch', 'expert'))  118 us
    dot_general x32, matrix products, pick_rows(): jnp.dot(one_hot(index, source.shape[0]), source, preferred_element_type=j...  83.5 us
    reduce_scatter x1, waiting for transfers between devices, local(): lax.psum_scatter(d_rows.astype(jnp.bfloat16), 'expert', scatter_dimension...  78.3 us
    dot_general x32, matrix products, add_rows(): lax.dot_general(one_hot(index, extent), split_three(values), (((0,), (0,)...  73 us
    all_gather x1, waiting for transfers between devices, local(): lax.all_gather(inputs, 'expert', axis=0, tiled=True)  45.1 us
    all_gather x1, waiting for transfers between devices, local(): lax.all_gather(d_mixed.reshape(tokens, TASKS * OUT), 'expert', axis=0, ti...  45 us
    psum x1, blocking collectives, local(): counts = jnp.maximum(lax.psum(jnp.sum(mask, 0), ('batch', 'expert')), 1.0)  43.1 us
    psum x1, blocking collectives, local(): grad_small, loss = lax.psum((flat_grads, loss_local), ('batch', 'expert'))  39.4 us
  transfers between devices with their start and end apart: 12, of which 8 were waited for; matrix products, arithmetic and copies ran while one was open for 4% of the time, Pallas kernels for 0%

commit v1 on v0

--- a/solution.py
+++ b/solution.py
@@ -1,6 +1,11 @@
+import collections
+import functools
+
 import jax
 import jax.numpy as jnp
 from jax import lax
+from jax.experimental import pallas as pl
+from jax.experimental.pallas import tpu as pltpu
 from jax.sharding import PartitionSpec as P
 
 FIELDS = 26
@@ -112,7 +117,7 @@
     return (d_first_w, d_second_w, d_first_b, d_second_b, d_inputs)
 
 
-def local(
+def plain(
     dense_feats,
     picks,
     labels,
@@ -334,43 +339,900 @@
     )
 
 
+MESH = pl.DeviceIdType.MESH
+BF = jnp.bfloat16
+F32 = jnp.float32
+NN = (((1,), (0,)), ((), ()))
+NT = (((1,), (1,)), ((), ()))
+KEYS = 256
+CHUNK = 256
+LANES = 128
+ONES = 16
+
+Sizes = collections.namedtuple(
+    "Sizes",
+    (
+        "groups",
+        "experts",
+        "devices",
+        "slots",
+        "rows",
+        "tokens",
+        "first",
+        "second",
+        "pack",
+        "span",
+    ),
+)
+
+
+def sizes_of(mesh, tokens, slots, rows):
+    groups = mesh.shape["batch"]
+    experts = mesh.shape["expert"]
+    first = INPUT // groups
+    second = HID // groups
+    span = tokens * LANES // slots
+    return Sizes(
+        groups,
+        experts,
+        groups * experts,
+        slots,
+        rows,
+        tokens,
+        first,
+        second,
+        first + second // 2,
+        span,
+    )
+
+
+def fits(size):
+    return (
+        size.slots % LANES == 0
+        and size.slots & (size.slots - 1) == 0
+        and size.span == CHUNK
+        and size.second % 32 == 0
+        and size.first % 16 == 0
+        and size.groups % 2 == 0
+        and size.devices % 2 == 0
+        and size.rows % KEYS == 0
+        and size.experts == 4
+    )
+
+
+def mm(left, right, dims=NN, precision=None):
+    return lax.dot_general(left, right, dims, preferred_element_type=F32, precision=precision)
+
+
+def here(size):
+    group = lax.axis_index("batch")
+    expert = lax.axis_index("expert")
+    return group, expert, group * size.experts + expert
+
+
+def place(size, device):
+    return (lax.div(device, size.experts), lax.rem(device, size.experts))
+
+
+def greet(size, me):
+    barrier = pltpu.get_barrier_semaphore()
+
+    def one(step, carry):
+        peer = lax.rem(me + step, size.devices)
+        pl.semaphore_signal(barrier, inc=1, device_id=place(size, peer), device_id_type=MESH)
+        return carry
+
+    lax.fori_loop(1, size.devices, one, 0)
+    return barrier
+
+
+def push(source, target, sent, landed, where):
+    return pltpu.make_async_remote_copy(
+        src_ref=source,
+        dst_ref=target,
+        send_sem=sent,
+        recv_sem=landed,
+        device_id=where,
+        device_id_type=MESH,
+    )
+
+
+def spread(index, extent, width):
+    return lax.broadcasted_iota(jnp.int32, (extent, width), 0) == index
+
+
+def as_low(flag):
+    return jnp.where(flag, 1.0, 0.0).astype(BF)
+
+
+def look_up(cells, key, high, levels):
+    found = mm(cells, as_low(spread(key, KEYS, key.shape[1])))
+    result = found[:EMB]
+    for level in range(1, levels):
+        result = jnp.where(high == level, found[level * EMB : (level + 1) * EMB], result)
+    return result
+
+
+def levels_of(values, high, levels):
+    return jnp.concatenate(
+        [jnp.where(high == level, values, 0.0) for level in range(levels)], 0
+    ).astype(BF)
+
+
+def front(
+    size,
+    requests,
+    mask,
+    table,
+    first,
+    second,
+    asked,
+    got,
+    gathered,
+    totals,
+    message,
+    cells,
+    rows,
+    ask_sent,
+    ask_landed,
+    row_sent,
+    row_landed,
+    z_sent,
+    z_landed,
+    y_sent,
+    y_landed,
+    c_sent,
+    c_landed,
+):
+    group, expert, me = here(size)
+    slots, devices, experts = size.slots, size.devices, size.experts
+    chips = size.groups // 2
+    chip, core = lax.div(group, 2), lax.rem(group, 2)
+    barrier = greet(size, me)
+    valid = mask[...].astype(F32)
+    lane = lax.broadcasted_iota(jnp.int32, (1, LANES), 1)
+    count = jnp.where(
+        lane == 0,
+        jnp.sum(valid[0:1], 1, keepdims=True),
+        jnp.where(lane == 1, jnp.sum(valid[1:2], 1, keepdims=True), 0.0),
+    ).astype(jnp.int32)
+    for part in range(size.groups):
+        for one in range(experts):
+            peer = part * experts + one
+            message[peer, :, :slots] = requests[part, one : one + 1, :]
+            message[peer, :, slots:] = count
+    gathered[group, expert, : size.first, :] = first[...].astype(BF)
+    half = size.second // 2
+    gathered[group, expert, size.first :, :LANES] = second[:half].astype(BF)
+    gathered[group, expert, size.first :, LANES:] = second[half:].astype(BF)
+    blocks = size.rows // KEYS
+    for block in range(blocks):
+        cells[block * EMB : (block + 1) * EMB, :] = table[
+            :, block * KEYS : (block + 1) * KEYS
+        ].astype(BF)
+    pl.semaphore_wait(barrier, devices - 1)
+
+    def ask(step, receive):
+        peer = lax.rem(me + (devices - step if receive else step), devices)
+        return push(
+            message.at[peer],
+            asked.at[peer if receive else me],
+            ask_sent.at[step],
+            ask_landed.at[peer if receive else me],
+            place(size, peer),
+        )
+
+    def answer(step, receive):
+        peer = lax.rem(me + devices - step, devices)
+        return push(
+            rows.at[peer],
+            got.at[me],
+            row_sent.at[step],
+            row_landed.at[me],
+            place(size, peer),
+        )
+
+    def arrival(step):
+        peer = lax.rem(me + step, devices)
+        return push(
+            rows.at[peer],
+            got.at[peer],
+            row_sent.at[step],
+            row_landed.at[peer],
+            place(size, peer),
+        )
+
+    def along_z(step, receive):
+        other = lax.rem(expert + (experts - step if receive else step), experts)
+        block = gathered.at[group, other if receive else expert]
+        return push(
+            block, block, z_sent.at[step], z_landed.at[step], (group, other)
+        )
+
+    def along_y(step, receive):
+        other = lax.rem(chip + (chips - step if receive else step), chips)
+        block = gathered.at[(other if receive else chip) * 2 + core]
+        return push(
+            block, block, y_sent.at[step], y_landed.at[step], (other * 2 + core, expert)
+        )
+
+    def across(step, receive):
+        other = lax.rem(chip + chips - step, chips)
+        block = gathered.at[other * 2 + (1 - core if receive else core)]
+        return push(
+            block, block, c_sent.at[step], c_landed.at[step], (chip * 2 + 1 - core, expert)
+        )
+
+    def start_ask(step, carry):
+        ask(step, False).start()
+        return carry
+
+    lax.fori_loop(1, devices, start_ask, 0)
+    for step in range(1, experts):
+        along_z(step, False).start()
+
+    def serve(peer):
+        index = asked[peer, :, :slots]
+        rows[peer] = look_up(cells[...], index & (KEYS - 1), index >> 8, blocks).astype(BF)
+
+    asked[me] = message[me]
+    serve(me)
+    got[me] = rows[me]
+
+    def serve_one(step, carry):
+        peer = lax.rem(me + devices - step, devices)
+        ask(step, True).wait_recv()
+        serve(peer)
+        answer(step, False).start()
+        return carry
+
+    third = devices // 4
+    lax.fori_loop(1, third, serve_one, 0)
+    for step in range(1, experts):
+        along_z(step, True).wait_recv()
+    for step in range(1, chips):
+        along_y(step, False).start()
+    across(0, False).start()
+    lax.fori_loop(third, devices, serve_one, 0)
+    for step in range(1, chips):
+        along_y(step, True).wait_recv()
+        across(step, False).start()
+    total = jnp.zeros((1, LANES), jnp.int32)
+    for peer in range(devices):
+        total = total + asked[peer, :, slots:]
+    totals[...] = jnp.maximum(total.astype(F32), 1.0)
+
+    def finish(step, carry):
+        arrival(step).wait_recv()
+        ask(step, False).wait_send()
+        answer(step, False).wait_send()
+        return carry
+
+    lax.fori_loop(1, devices, finish, 0)
+    for step in range(1, experts):
+        along_z(step, False).wait_send()
+    for step in range(1, chips):
+        along_y(step, False).wait_send()
+    for step in range(chips):
+        across(step, True).wait_recv()
+        across(step, False).wait_send()
+
+
+def sigmoid(value):
+    return 0.5 + 0.5 * jnp.tanh(0.5 * value)
+
+
+def middle(
+    size,
+    got,
+    picks,
+    dense,
+    labels,
+    mask,
+    totals,
+    gathered,
+    vectors,
+    gate_t,
+    gate_n,
+    tower_n,
+    tower_t,
+    dense_w,
+    out_slots,
+    out_grads,
+    out_bias_one,
+    out_bias_two,
+    out_dense,
+    out_gate,
+    out_tower,
+    out_head,
+    out_loss,
+    columns,
+    first_t,
+    second_n,
+    second_t,
+    wide,
+    feats,
+    slot_cells,
+    chosen,
+    inputs,
+    slope_one,
+    slope_two,
+    hidden,
+    outs,
+    mixes,
+    deltas,
+    d_inputs,
+    slot_sum,
+    sum_first,
+    sum_second,
+    sum_gate,
+    sum_dense,
+    sum_tower,
+    sum_head,
+    loss_sum,
+):
+    experts, slots = size.experts, size.slots
+    levels = size.devices // 2
+    shift = slots.bit_length() - 1
+    half = size.second // 2
+    flipped = jnp.concatenate([vectors[...], jnp.zeros((LANES - 16, LANES), F32)], 0).T
+    for column in range(16):
+        columns[column] = jnp.broadcast_to(flipped[:, column : column + 1], (LANES, LANES))
+    for expert in range(experts):
+        for part in range(size.groups):
+            wide[
+                part * size.first : (part + 1) * size.first, expert * HID : (expert + 1) * HID
+            ] = gathered[part, expert, : size.first, :]
+            base = part * size.second
+            second_n[expert, base : base + half, :] = gathered[part, expert, size.first :, :LANES]
+            second_n[expert, base + half : base + 2 * half, :] = gathered[
+                part, expert, size.first :, LANES:
+            ]
+        first_t[expert] = wide[:, expert * HID : (expert + 1) * HID].T
+        second_t[expert] = second_n[expert].T
+    wide[:, experts * HID :] = gate_n[...]
+    feats[...] = jnp.ones_like(feats)
+    feats[:DENSE, :] = dense[...]
+    inputs[INPUT:, :] = jnp.ones((ONES, CHUNK), BF)
+    for expert in range(experts):
+        hidden[expert, HID:, :] = jnp.ones((ONES, CHUNK), BF)
+    for task in range(TASKS):
+        mixes[task, OUT:, :] = jnp.ones((ONES, CHUNK), BF)
+    deltas[experts * HID :, :] = jnp.zeros((LANES, CHUNK), BF)
+    for total in (sum_first, sum_second, sum_gate, sum_dense, sum_tower, sum_head, loss_sum):
+        total[...] = jnp.zeros_like(total)
+
+    def column(index, begin=0, end=LANES):
+        block = columns[index, begin:end, :]
+        return jnp.concatenate([block] * (CHUNK // LANES), 1)
+
+    def chunk(step, carry):
+        token = pl.multiple_of(step * CHUNK, CHUNK)
+        slot = pl.multiple_of(step * LANES, LANES)
+        here_tokens = pl.ds(token, CHUNK)
+        for owner in range(size.devices):
+            level, lower = owner // 2, owner % 2
+            slot_cells[
+                level * EMB : (level + 1) * EMB, lower * LANES : (lower + 1) * LANES
+            ] = got[owner, :, pl.ds(slot, LANES)]
+
+        def split(field):
+            index = picks[pl.ds(field, 1), here_tokens]
+            owner = index >> shift
+            return (owner & 1) * LANES + (index & (LANES - 1)), owner >> 1
+
+        def pick(field, carry):
+            key, high = split(field)
+            flags = as_low(spread(key, KEYS, CHUNK))
+            chosen[field] = flags
+            found = mm(slot_cells[...], flags)
+            result = found[:EMB]
+            for level in range(1, levels):
+                result = jnp.where(high == level, found[level * EMB : (level + 1) * EMB], result)
+            inputs[pl.ds(pl.multiple_of(field * EMB, EMB), EMB), :] = result.astype(BF)
+            return carry
+
+        lax.fori_loop(0, FIELDS, pick, 0)
+        inputs[FIELDS * EMB : INPUT, :] = mm(
+            dense_w[...], feats[:, here_tokens], precision=HI
+        ).astype(BF)
+        x = inputs[:INPUT, :]
+        logits = mm(gate_t[...], x)[: TASKS * experts] + column(14, 0, TASKS * experts)
+        probs, gates = [], []
+        for task in range(TASKS):
+            line = [logits[task * experts + e : task * experts + e + 1] for e in range(experts)]
+            top = functools.reduce(jnp.maximum, line)
+            powers = [jnp.exp(item - top) for item in line]
+            whole = 1.0 / functools.reduce(jnp.add, powers)
+            probs.append([item * whole for item in powers])
+            gates.append([item.astype(BF).astype(F32) for item in probs[-1]])
+        mixed = [None] * TASKS
+        for expert in range(experts):
+            pre = mm(first_t[expert], x) + jnp.concatenate(
+                [column(2 * expert), column(2 * expert + 1)], 0
+            )
+            sig = sigmoid(pre)
+            act = pre * sig
+            slope_one[expert] = sig + act * (1.0 - sig)
+            hidden[expert, :HID, :] = act.astype(BF)
+            pre = mm(second_t[expert], hidden[expert, :HID, :]) + column(8 + expert)
+            sig = sigmoid(pre)
+            act = pre * sig
+            slope_two[expert] = sig + act * (1.0 - sig)
+            outs[expert] = act
+            for task in range(TASKS):
+                term = gates[task][expert] * act
+                mixed[task] = term if mixed[task] is None else mixed[task] + term
+        d_mixed = []
+        for task in range(TASKS):
+            mixes[task, :OUT, :] = mixed[task].astype(BF)
+            low, high = task * TOWER, (task + 1) * TOWER
+            pre = mm(tower_t[task], mixes[task, :OUT, :]) + column(12, low, high)
+            sig = sigmoid(pre)
+            act = pre * sig
+            head = column(13, low, high)
+            logit = jnp.sum(act * head, 0, keepdims=True) + column(15, task, task + 1)
+            valid = mask[task : task + 1, here_tokens].astype(F32)
+            target = labels[task : task + 1, here_tokens].astype(F32)
+            scale = valid / totals[0:1, task : task + 1]
+            soft = jnp.maximum(logit, 0.0) + jnp.log(1.0 + jnp.exp(-jnp.abs(logit)))
+            loss_sum[...] += scale * (soft - target * logit)
+            d_logit = scale * (sigmoid(logit) - target)
+            d_pre = ((sig + act * (1.0 - sig)) * (d_logit * head)).astype(BF)
+            sum_head[task] += mm(
+                jnp.broadcast_to(d_logit, (8, CHUNK)),
+                jnp.concatenate([act, jnp.ones((8, CHUNK), F32)], 0),
+                NT,
+                HI,
+            )
+            sum_tower[task] += mm(mixes[task], d_pre, NT)
+            d_mixed.append(mm(tower_n[task], d_pre).astype(BF).astype(F32))
+        d_gates = [[None] * experts for task in range(TASKS)]
+        for expert in range(experts):
+            d_out = gates[0][expert] * d_mixed[0] + gates[1][expert] * d_mixed[1]
+            for task in range(TASKS):
+                d_gates[task][expert] = jnp.sum(outs[expert] * d_mixed[task], 0, keepdims=True)
+            d_two = (slope_two[expert] * d_out).astype(BF)
+            sum_second[expert] += mm(hidden[expert], d_two, NT)
+            d_one = (slope_one[expert] * mm(second_n[expert], d_two)).astype(BF)
+            deltas[expert * HID : (expert + 1) * HID, :] = d_one
+            sum_first[expert] += mm(inputs[...], d_one, NT)
+        lines = []
+        for task in range(TASKS):
+            inner = functools.reduce(
+                jnp.add, [probs[task][e] * d_gates[task][e] for e in range(experts)]
+            )
+            lines += [probs[task][e] * (d_gates[task][e] - inner) for e in range(experts)]
+        lines.append(jnp.zeros((16 - TASKS * experts, CHUNK), F32))
+        d_gate = jnp.concatenate(lines, 0).astype(BF)
+        deltas[experts * HID : experts * HID + 16, :] = d_gate
+        sum_gate[...] += mm(inputs[...], d_gate, NT)
+        d_inputs[...] = mm(wide[...], deltas[...])
+        sum_dense[...] += mm(feats[:, here_tokens], d_inputs[FIELDS * EMB :, :], NT, HI)
+        slot_sum[...] = jnp.zeros_like(slot_sum)
+
+        def give(field, carry):
+            key, high = split(field)
+            values = d_inputs[pl.ds(pl.multiple_of(field * EMB, EMB), EMB), :]
+            slot_sum[...] += mm(levels_of(values, high, levels), chosen[field], NT)
+            return carry
+
+        lax.fori_loop(0, FIELDS, give, 0)
+        for owner in range(size.devices):
+            level, lower = owner // 2, owner % 2
+            out_slots[owner, :, pl.ds(slot, LANES)] = slot_sum[
+                level * EMB : (level + 1) * EMB, lower * LANES : (lower + 1) * LANES
+            ].astype(BF)
+        return carry
+
+    lax.fori_loop(0, size.tokens // CHUNK, chunk, 0)
+    for expert in range(experts):
+        for part in range(size.groups):
+            out_grads[part, expert, : size.first, :] = sum_first[
+                expert, part * size.first : (part + 1) * size.first, :
+            ].astype(BF)
+            base = part * size.second
+            out_grads[part, expert, size.first :, :LANES] = sum_second[
+                expert, base : base + half, :
+            ].astype(BF)
+            out_grads[part, expert, size.first :, LANES:] = sum_second[
+                expert, base + half : base + 2 * half, :
+            ].astype(BF)
+        out_bias_one[expert : expert + 1, :] = sum_first[expert, INPUT : INPUT + 1, :]
+        out_bias_two[expert : expert + 1, :] = sum_second[expert, HID : HID + 1, :]
+    out_dense[...] = sum_dense[...]
+    out_gate[...] = sum_gate[...]
+    out_tower[...] = sum_tower[...]
+    out_head[...] = sum_head[...]
+    out_loss[...] = loss_sum[...]
+
+
+def back(
+    size,
+    slots_in,
+    asked,
+    grads,
+    small,
+    table_grad,
+    first_grad,
+    second_grad,
+    small_sum,
+    slots_got,
+    small_got,
+    core_got,
+    core_sum,
+    chip_got,
+    chip_sum,
+    z_got,
+    slot_sent,
+    slot_landed,
+    small_sent,
+    small_landed,
+    whole_sent,
+    whole_landed,
+    c_sent,
+    c_landed,
+    y_sent,
+    y_landed,
+    z_sent,
+    z_landed,
+):
+    group, expert, me = here(size)
+    slots, devices, experts = size.slots, size.devices, size.experts
+    chips = size.groups // 2
+    chip, core = lax.div(group, 2), lax.rem(group, 2)
+    blocks = size.rows // KEYS
+    barrier = greet(size, me)
+    table_grad[...] = jnp.zeros_like(table_grad)
+    pl.semaphore_wait(barrier, devices - 1)
+
+    def across(step, receive):
+        other = lax.rem(chip + step, chips)
+        return push(
+            grads.at[other * 2 + 1 - core],
+            core_got.at[other],
+            c_sent.at[step],
+            c_landed.at[step],
+            (chip * 2 + 1 - core, expert),
+        )
+
+    def along_y(step, receive):
+        other = lax.rem(chip + (chips - step if receive else step), chips)
+        return push(
+            core_sum.at[other],
+            chip_got.at[step],
+            y_sent.at[step],
+            y_landed.at[step],
+            (other * 2 + core, expert),
+        )
+
+    def along_z(step, receive):
+        other = lax.rem(expert + (experts - step if receive else step), experts)
+        return push(
+            chip_sum.at[other], z_got.at[step], z_sent.at[step], z_landed.at[step], (group, other)
+        )
+
+    def to_all(source, target, sent, landed, step, receive, mine=False):
+        peer = lax.rem(me + (devices - step if receive else step), devices)
+        return push(
+            source.at[me if mine else peer],
+            target.at[peer if receive else me],
+            sent.at[step],
+            landed.at[peer if receive else me],
+            place(size, peer),
+        )
+
+    def send_slots(step, receive):
+        return to_all(slots_in, slots_got, slot_sent, slot_landed, step, receive)
+
+    def send_small(step, receive):
+        return to_all(small, small_got, small_sent, small_landed, step, receive)
+
+    def send_whole(step, receive):
+        return to_all(small_sum, small_sum, whole_sent, whole_landed, step, receive, True)
+
+    for step in range(1, chips + 1):
+        across(step % chips, False).start()
+
+    def start_small(step, carry):
+        send_small(step, False).start()
+        return carry
+
+    lax.fori_loop(1, devices, start_small, 0)
+
+    def start_slots(step, carry):
+        send_slots(step, False).start()
+        return carry
+
+    lax.fori_loop(1, devices, start_slots, 0)
+    for step in range(1, chips + 1):
+        other = lax.rem(chip + step, chips)
+        across(step % chips, True).wait_recv()
+        core_sum[other] = (
+            grads[other * 2 + core].astype(F32) + core_got[other].astype(F32)
+        ).astype(BF)
+        if step < chips:
+            along_y(step, False).start()
+    small_got[me] = small[me]
+
+    def add_small(step, total):
+        send_small(step, True).wait_recv()
+        return total + small_got[lax.rem(me + devices - step, devices)]
+
+    small_sum[me] = lax.fori_loop(1, devices, add_small, small_got[me])
+
+    def start_whole(step, carry):
+        send_whole(step, False).start()
+        return carry
+
+    lax.fori_loop(1, devices, start_whole, 0)
+    total = core_sum[chip].astype(F32)
+    for step in range(1, chips):
+        along_y(step, True).wait_recv()
+        total = total + chip_got[step].astype(F32)
+    chip_sum[...] = total.astype(BF)
+    for step in range(1, experts):
+        along_z(step, False).start()
+
+    def gather(peer, values):
+        index = asked[peer, :, :slots]
+        levels = levels_of(values, index >> 8, blocks)
+        spots = as_low(spread(index & (KEYS - 1), KEYS, slots))
+        table_grad[...] += mm(levels, spots, NT)
+
+    gather(me, slots_in[me].astype(F32))
+
+    def gather_one(step, carry):
+        peer = lax.rem(me + devices - step, devices)
+        send_slots(step, True).wait_recv()
+        gather(peer, slots_got[peer].astype(F32))
+        return carry
+
+    lax.fori_loop(1, devices, gather_one, 0)
+    total = chip_sum[expert].astype(F32)
+    for step in range(1, experts):
+        along_z(step, True).wait_recv()
+        total = total + z_got[step].astype(F32)
+    half = size.second // 2
+    first_grad[...] = total[: size.first]
+    second_grad[:half, :] = total[size.first :, :LANES]
+    second_grad[half:, :] = total[size.first :, LANES:]
+
+    def finish(step, carry):
+        send_whole(step, True).wait_recv()
+        send_whole(step, False).wait_send()
+        send_small(step, False).wait_send()
+        send_slots(step, False).wait_send()
+        return carry
+
+    lax.fori_loop(1, devices, finish, 0)
+    for step in range(chips):
+        across(step, False).wait_send()
+    for step in range(1, chips):
+        along_y(step, False).wait_send()
+    for step in range(1, experts):
+        along_z(step, False).wait_send()
+
+
+def update(size, *refs):
+    grads, state, results = refs[:3], refs[3:12], refs[12:]
+    table_grad = grads[0][...]
+    wide = jnp.concatenate(
+        [table_grad[b * EMB : (b + 1) * EMB] for b in range(size.rows // KEYS)], 1
+    )
+    for index, grad in enumerate((wide, grads[1][...], grads[2][...])):
+        rate = 0.3 if index == 0 else 0.15
+        values = [ref[...] for ref in state[3 * index : 3 * index + 3]]
+        for ref, value in zip(results[3 * index : 3 * index + 3], adamw(*values, grad, rate)):
+            ref[...] = value
+
+
+def shape(dims, dtype=F32):
+    return jax.ShapeDtypeStruct(dims, dtype)
+
+
+def call(kernel, outs, scratch, remote=None):
+    vmem = pl.BlockSpec(memory_space=pltpu.VMEM)
+    params = dict(vmem_limit_bytes=56 * 2**20)
+    if remote is not None:
+        params.update(collective_id=remote, has_side_effects=True)
+    return lambda *args: pl.pallas_call(
+        kernel,
+        out_shape=outs,
+        in_specs=[vmem] * len(args),
+        out_specs=[vmem] * len(outs),
+        scratch_shapes=scratch,
+        compiler_params=pltpu.CompilerParams(**params),
+    )(*args)
+
+
+def pads(array, dims):
+    return jnp.pad(array, [(0, want - have) for want, have in zip(dims, array.shape)])
+
+
+def local(
+    size,
+    dense_feats,
+    picks,
+    labels,
+    label_mask,
+    requests,
+    table,
+    table_m,
+    table_v,
+    first_w,
+    first_m,
+    first_v,
+    second_w,
+    second_m,
+    second_v,
+    small,
+    small_m,
+    small_v,
+):
+    devices, experts, groups = size.devices, size.experts, size.groups
+    chips = groups // 2
+    dma = pltpu.SemaphoreType.DMA
+    vm = pltpu.VMEM
+    message = size.slots + LANES
+    asked, got, gathered, totals = call(
+        functools.partial(front, size),
+        [
+            shape((devices, 1, message), jnp.int32),
+            shape((devices, EMB, size.slots), BF),
+            shape((groups, experts, size.pack, HID), BF),
+            shape((1, LANES)),
+        ],
+        [
+            vm((devices, 1, message), jnp.int32),
+            vm((size.rows // KEYS * EMB, KEYS), BF),
+            vm((devices, EMB, size.slots), BF),
+        ]
+        + [dma((devices,))] * 4
+        + [dma((experts,))] * 2
+        + [dma((chips,))] * 4,
+        0,
+    )(requests[0], label_mask.T, table.T, first_w[0], second_w[0])
+    bias_one, bias_two, dense_w, gate_w, tower_w, head_w = unpack(small, experts)
+    vectors = jnp.concatenate(
+        [
+            bias_one.reshape(8, LANES),
+            bias_two,
+            tower_w[:, OUT].reshape(1, LANES),
+            head_w[:, :TOWER].reshape(1, LANES),
+            pads(gate_w[INPUT][None], (1, LANES)),
+            pads(head_w[:, TOWER][None], (1, LANES)),
+        ],
+        0,
+    )
+    gate_low = gate_w[:INPUT].astype(BF)
+    tower_low = tower_w[:, :OUT].astype(BF)
+    outs = call(
+        functools.partial(middle, size),
+        [
+            shape((devices, EMB, size.slots), BF),
+            shape((groups, experts, size.pack, HID), BF),
+            shape((experts, HID)),
+            shape((experts, OUT)),
+            shape((16, DOUT)),
+            shape((INPUT + ONES, 16)),
+            shape((TASKS, OUT + ONES, TOWER)),
+            shape((TASKS, 8, TOWER + 8)),
+            shape((1, CHUNK)),
+        ],
+        [
+            vm((16, LANES, LANES), F32),
+            vm((experts, HID, INPUT), BF),
+            vm((experts, HID, OUT), BF),
+            vm((experts, OUT, HID), BF),
+            vm((INPUT, experts * HID + LANES), BF),
+            vm((16, size.tokens), F32),
+            vm((devices // 2 * EMB, KEYS), BF),
+            vm((FIELDS, KEYS, CHUNK), BF),
+            vm((INPUT + ONES, CHUNK), BF),
+            vm((experts, HID, CHUNK), F32),
+            vm((experts, OUT, CHUNK), F32),
+            vm((experts, HID + ONES, CHUNK), BF),
+            vm((experts, OUT, CHUNK), F32),
+            vm((TASKS, OUT + ONES, CHUNK), BF),
+            vm((experts * HID + LANES, CHUNK), BF),
+            vm((INPUT, CHUNK), F32),
+            vm((devices // 2 * EMB, KEYS), F32),
+            vm((experts, INPUT + ONES, HID), F32),
+            vm((experts, HID + ONES, OUT), F32),
+            vm((INPUT + ONES, 16), F32),
+            vm((16, DOUT), F32),
+            vm((TASKS, OUT + ONES, TOWER), F32),
+            vm((TASKS, 8, TOWER + 8), F32),
+            vm((1, CHUNK), F32),
+        ],
+    )(
+        got,
+        picks.T,
+        dense_feats.T,
+        labels.T,
+        label_mask.T,
+        totals,
+        gathered,
+        vectors,
+        pads(gate_low.T, (16, INPUT)),
+        pads(gate_low, (INPUT, LANES)),
+        tower_low,
+        tower_low.transpose(0, 2, 1),
+        pads(dense_w.T, (DOUT, 16)),
+    )
+    slot_grads, grads, d_bias_one, d_bias_two, d_dense, d_gate, d_tower, d_head, loss = outs
+    flat = jnp.concatenate(
+        [
+            d_bias_one.reshape(-1),
+            d_bias_two.reshape(-1),
+            d_dense[: DENSE + 1].reshape(-1),
+            d_gate[: INPUT + 1, : TASKS * experts].reshape(-1),
+            d_tower[:, : OUT + 1].reshape(-1),
+            d_head[:, 0, : TOWER + 1].reshape(-1),
+            jnp.sum(loss).reshape(1),
+        ]
+    )
+    count = flat.shape[0] - 1
+    lines = -(-(count + 1) // (devices * 8 * LANES)) * 8
+    flat = jnp.pad(flat, (0, devices * lines * LANES - count - 1)).reshape(devices, lines, LANES)
+    table_grad, first_grad, second_grad, flat = call(
+        functools.partial(back, size),
+        [
+            shape((size.rows // KEYS * EMB, KEYS)),
+            shape((size.first, HID)),
+            shape((size.second, OUT)),
+            shape((devices, lines, LANES)),
+        ],
+        [
+            vm((devices, EMB, size.slots), BF),
+            vm((devices, lines, LANES), F32),
+            vm((chips, experts, size.pack, HID), BF),
+            vm((chips, experts, size.pack, HID), BF),
+            vm((chips, experts, size.pack, HID), BF),
+            vm((experts, size.pack, HID), BF),
+            vm((experts, size.pack, HID), BF),
+        ]
+        + [dma((devices,))] * 6
+        + [dma((chips,))] * 4
+        + [dma((experts,))] * 2,
+        1,
+    )(slot_grads, asked, grads, flat)
+    tables = (table.T, table_m.T, table_v.T)
+    firsts = (first_w[0], first_m[0], first_v[0])
+    seconds = (second_w[0], second_m[0], second_v[0])
+    new = call(
+        functools.partial(update, size),
+        [shape(a.shape) for a in tables + firsts + seconds],
+        [],
+    )(table_grad, first_grad, second_grad, *tables, *firsts, *seconds)
+    flat = flat.reshape(-1)
+    new_small = adamw(small, small_m, small_v, flat[:count], 0.15)
+    return (
+        (flat[count],)
+        + tuple(a.T for a in new[:3])
+        + tuple(a[None] for a in new[3:])
+        + tuple(new_small)
+    )
+
+
 def solution(mesh):
-    return jax.shard_map(
-        local,
-        mesh=mesh,
-        in_specs=(
-            P(("batch", "expert"), None),
-            P(("batch", "expert"), None),
-            P(("batch", "expert"), None),
-            P(("batch", "expert"), None),
-            P(("batch", "expert"), None, None, None),
-            P(("batch", "expert"), None),
-            P(("batch", "expert"), None),
-            P(("batch", "expert"), None),
-            P("expert", "batch", None),
-            P("expert", "batch", None),
-            P("expert", "batch", None),
-            P("expert", "batch", None),
-            P("expert", "batch", None),
-            P("expert", "batch", None),
-            P(),
-            P(),
-            P(),
-        ),
-        out_specs=(
-            P(),
-            P(("batch", "expert"), None),
-            P(("batch", "expert"), None),
-            P(("batch", "expert"), None),
-            P("expert", "batch", None),
-            P("expert", "batch", None),
-            P("expert", "batch", None),
-            P("expert", "batch", None),
-            P("expert", "batch", None),
-            P("expert", "batch", None),
-            P(),
-            P(),
-            P(),
-        ),
-        check_vma=False,
-    )
+    both = P(("batch", "expert"), None)
+    shard = P("expert", "batch", None)
+    ins = (both,) * 4 + (P(("batch", "expert"), None, None, None),) + (both,) * 3
+    ins = ins + (shard,) * 6 + (P(),) * 3
+
+    def step(*args):
+        devices = mesh.shape["batch"] * mesh.shape["expert"]
+        size = sizes_of(
+            mesh, args[0].shape[0] // devices, args[4].shape[-1], args[5].shape[0] // devices
+        )
+        return jax.shard_map(
+            functools.partial(local, size) if fits(size) else plain,
+            mesh=mesh,
+            in_specs=ins,
+            out_specs=(P(),) + (both,) * 3 + (shard,) * 6 + (P(),) * 3,
+            check_vma=False,
+        )(*args)
+
+    return step

time: 868 us -> 157 us (0.18); the launches traced: 858 us -> 156 us
  waiting for transfers between devices: 339 us -> 0 us
  matrix products: 184 us -> 0 us
  blocking collectives: 137 us -> 0 us
  Pallas kernels: 0 us -> 135 us
  local copies, waits for them, and re-layouts: 121 us -> 17.5 us
  other arithmetic: 43.6 us -> 2.94 us
  starting transfers between devices: 17.1 us -> 0 us
  between operations: 15.5 us -> 0.77 us
    dot_general x80 -> x0, matrix products: 184 us -> none  [the longest x32 83.5 us: pick_rows(): jnp.dot(one_hot(index, source.shape[0]), source, preferred_element_type=j...]
    pallas_call x0 -> x4, Pallas kernels: none -> 135 us  [call(): pl.pallas_call(kernel, out_shape=outs, in_specs=[vmem] * len(args), out_s...]
    psum x1 -> x0, waiting for transfers between devices: 118 us -> none  [local(): grad_small, loss = lax.psum((flat_grads, loss_local), ('batch', 'expert'))]
    all_gather x2 -> x0, waiting for transfers between devices: 90.1 us -> none  [the longest x1 45.1 us: local(): lax.all_gather(inputs, 'expert', axis=0, tiled=True)]
    psum x2 -> x0, blocking collectives: 82.5 us -> none  [the longest x1 43.1 us: local(): counts = jnp.maximum(lax.psum(jnp.sum(mask, 0), ('batch', 'expert')), 1.0)]
    reduce_scatter x4 -> x0, waiting for transfers between devices: 78.3 us -> none  [the longest x1 78.3 us: local(): lax.psum_scatter(d_rows.astype(jnp.bfloat16), 'expert', scatter_dimension...]
    reshape x16 -> x5, local copies, waits for them, and re-layouts: 36.1 us -> 1.75 us  [the longest x1 0.77 us: local(): d_dense[:DENSE + 1].reshape(-1)]
    all_gather x3 -> x0, blocking collectives: 31.7 us -> none  [the longest x1 14.1 us: local(): lax.all_gather(gates.reshape(tokens, TASKS * experts), 'expert', axis=0,...]
  transfers between devices with their start and end apart: 12 -> 0, of which waited for: 8 -> 0; matrix products, arithmetic and copies ran while one was open for 4% -> 0% of each run, Pallas kernels for 0% -> 0%
where the time goes in v1:
time: 157 us; the launch traced here: 156 us
  Pallas kernels  135 us (86%)
  local copies, waits for them, and re-layouts  17.5 us (11%)
  other arithmetic  2.94 us (2%)
    pallas_call x4, Pallas kernels, call(): pl.pallas_call(kernel, out_shape=outs, in_specs=[vmem] * len(args), out_s...  135 us

profile of v1, /device:TPU:0, one launch (start us, length us, event | category | flops | bytes accessed | tf_op | source)
XLA Modules:
  0.0 156.2 jit_solution(8934603500379473663)
XLA Ops:
  0.6 0.8 slice_bitcast_fusion.2
  1.4 0.8 slice.66
  2.2 0.1 reshape.73
  2.3 0.1 reshape.74
  2.4 0.2 slice_reduce_fusion.2
  2.5 0.7 slice_bitcast_fusion.1
  3.2 0.7 slice_bitcast_fusion
  3.9 0.8 slice.94
  4.7 0.7 slice.73
  5.4 0.1 reshape.75
  5.5 0.1 copy.39
  5.6 0.6 pad.28.dense_w
  6.2 1.0 slice.64
  7.2 0.1 reshape.72
  7.3 0.1 copy.41
  7.4 0.0 copy-start.1
  7.5 0.1 reshape_squeeze.6
  7.5 1.2 concatenate.6.vectors
  8.7 0.7 copy.40.tower_n
  9.5 0.2 convert_element_type.17
  9.7 0.1 copy.37
  9.7 0.7 pad.27.gate_n
  10.4 0.6 pad.26.gate_t
  11.0 31.4 %shard_map.264 = (s32[32,1,640]{2,1,0:T(1,128)}, bf16[32,16,512]{2,1,0:T(8,128)(2,1)}, bf16[8,4,80,256]{3,2,1,0:T(8,128)(2,1)}, f32[1,128]{1,0:T(1,128)}) custom-call(s32[8,4,512]{2,1,0:T(4,128)} %bitcast.56, s32[2,1024]{1,0:T(2,128)} %bitcast.60, f32[16,4096]{1,0:T(8,128)} %bitcast.43, f32[64,256]{1,0:T(8,128)} %bitcast.48, f32[32,128]{1,0:T(8,128)} %bitcast.54), custom_call_target="tpu_custom_call" | custom-call | tf_op jit(solution)/shard_map/pallas_call | solution.py:1039
  42.4 0.0 copy-done.1
  42.5 66.7 %shard_map.265 = (bf16[32,16,512]{2,1,0:T(8,128)(2,1)}, bf16[8,4,80,256]{3,2,1,0:T(8,128)(2,1)}, f32[4,256]{1,0:T(4,128)}, f32[4,128]{1,0:T(4,128)}, f32[16,96]{...) custom-call(bf16[32,16,512]{2,1,0:T(8,128)(2,1)} %get-tuple-element.39.got, ...), custom_call_target="tpu_custom_call" | custom-call | tf_op jit(solution)/shard_map/pallas_call | solution.py:1039
  109.1 1.3 reduce_sum.9
  110.4 0.7 slice_reduce_fusion.1
  111.2 0.1 reshape_squeeze.7
  111.2 0.7 copy.42
  111.9 0.8 reshape.78
  112.7 0.9 slice.76
  113.6 0.1 reshape.80
  113.7 1.0 slice.75
  114.7 0.1 reshape.79
  114.8 0.0 copy-done.4
  114.8 0.0 copy-start
  114.9 0.0 copy-start.2
  114.9 0.0 copy-start.3
  114.9 0.8 concatenate.7
  115.7 0.7 pad_bitcast_fusion.small
  116.4 34.5 %shard_map.266 = (f32[256,256]{1,0:T(8,128)}, f32[64,256]{1,0:T(8,128)}, f32[32,128]{1,0:T(8,128)}, f32[32,8,128]{2,1,0:T(8,128)}) custom-call(bf16[32,16,512]{2,1,0:T(8,128)(2,1)} %get-tuple-element.42.slots_in, s32[32,1,640]{2,1,0:T(1,128)} %get-tuple-element.43.asked, bf16[8,4,80,256]{3,2,1,0:T(8,128)(2,1)} %get-tuple-element.44.grads, ...), custom_call_target="tpu_custom_call" | custom-call | tf_op jit(solution)/shard_map/pallas_call | solution.py:1039
  150.9 1.3 slice.83
  152.1 0.0 copy-done
  152.1 0.0 copy-done.2
  152.1 0.0 copy-done.3
  152.1 1.6 %multiply_subtract_fusion = (f32[23626]{0:T(1024)}, f32[23626]{0:T(1024)}, f32[23626]{0:T(1024)}) fusion(f32[23626]{0:T(1024)S(1)} %copy-done, f32[32768]{0:T(1024)} %bitcast.53, f32[23626]{0:T(1024)S(1)} %copy-done.2, f32[23626]{0:T(1024)S(1)} %copy-done.3), kind=kLoop, calls=%fused_computation.3 | loop fusion | flops 354390 | bytes 661528 | tf_op jit(solution)/shard_map/sub | solution.py:52
  153.8 2.4 %shard_map.267 = (f32[16,4096]{1,0:T(8,128)}, f32[16,4096]{1,0:T(8,128)}, f32[16,4096]{1,0:T(8,128)}, f32[64,256]{1,0:T(8,128)}, f32[64,256]{1,0:T(8,128)}, /*in...) custom-call(f32[256,256]{1,0:T(8,128)} %get-tuple-element.53.refs_0_, ...), custom_call_target="tpu_custom_call" | custom-call | tf_op jit(solution)/shard_map/pallas_call | solution.py:1039
  (5 shorter events, 0.0 us)
Async XLA Ops:
  7.4 35.0 %copy-start.1 = (bf16[2,128,64]{1,2,0:T(8,128)(2,1)}, bf16[2,128,64]{1,2,0:T(8,128)(2,1)S(1)}, u32[]{:S(2)}) copy-start(bf16[2,128,64]{1,2,0:T(8,128)(2,1)S(1)} %copy.41) | copy-start | bytes 98308
  109.1 5.7 %copy-start.4 = (f32[4,128]{1,0:T(4,128)S(1)}, f32[4,128]{1,0:T(4,128)}, u32[]{:S(2)}) copy-start(f32[4,128]{1,0:T(4,128)} %get-tuple-element.46) | copy-start | bytes 6148
  114.8 37.3 %copy-start = (f32[23626]{0:T(1024)S(1)}, f32[23626]{0:T(1024)}, u32[]{:S(2)}) copy-start(f32[23626]{0:T(1024)} %param.31) | copy-start | bytes 283516
  114.9 37.3 %copy-start.2 = (f32[23626]{0:T(1024)S(1)}, f32[23626]{0:T(1024)}, u32[]{:S(2)}) copy-start(f32[23626]{0:T(1024)} %param.32) | copy-start | bytes 283516
  114.9 37.3 %copy-start.3 = (f32[23626]{0:T(1024)S(1)}, f32[23626]{0:T(1024)}, u32[]{:S(2)}) copy-start(f32[23626]{0:T(1024)} %param.33) | copy-start | bytes 283516

commit v2 on v1

--- a/solution.py
+++ b/solution.py
@@ -459,194 +459,93 @@
     ).astype(BF)
 
 
-def front(
+def sigmoid(value):
+    return 0.5 + 0.5 * jnp.tanh(0.5 * value)
+
+
+def lanes_of(rows=1):
+    return lax.broadcasted_iota(jnp.int32, (rows, LANES), 1)
+
+
+def turn(values, shift):
+    shift = shift % LANES
+    return pltpu.roll(values, shift, 1) if shift else values
+
+
+def take(flat, offset, count):
+    row, shift = offset // LANES, offset % LANES
+    if shift == 0:
+        return flat[row : row + count, :]
+    return jnp.where(
+        lanes_of(count) < LANES - shift,
+        turn(flat[row : row + count, :], -shift),
+        turn(flat[row + 1 : row + 1 + count, :], -shift),
+    )
+
+
+def put(flat, offset, values):
+    row, shift = offset // LANES, offset % LANES
+    count = values.shape[0]
+    moved = turn(values, shift)
+    if shift == 0:
+        flat[row : row + count, :] += moved
+        return
+    flat[row : row + count, :] += jnp.where(lanes_of(count) >= shift, moved, 0.0)
+    flat[row + 1 : row + 1 + count, :] += jnp.where(lanes_of(count) < shift, moved, 0.0)
+
+
+def offsets(experts):
+    sizes = [
+        experts * HID,
+        experts * OUT,
+        (DENSE + 1) * DOUT,
+        (INPUT + 1) * TASKS * experts,
+        TASKS * (OUT + 1) * TOWER,
+        TASKS * (TOWER + 1),
+    ]
+    return [sum(sizes[:index]) for index in range(len(sizes) + 1)]
+
+
+def step_kernel(
     size,
     requests,
+    picks,
+    dense,
+    labels,
     mask,
     table,
     first,
     second,
+    small,
+    table_grad,
+    first_grad,
+    second_grad,
+    small_sum,
+    message,
     asked,
-    got,
-    gathered,
-    totals,
-    message,
     cells,
     rows,
-    ask_sent,
-    ask_landed,
-    row_sent,
-    row_landed,
-    z_sent,
-    z_landed,
-    y_sent,
-    y_landed,
-    c_sent,
-    c_landed,
-):
-    group, expert, me = here(size)
-    slots, devices, experts = size.slots, size.devices, size.experts
-    chips = size.groups // 2
-    chip, core = lax.div(group, 2), lax.rem(group, 2)
-    barrier = greet(size, me)
-    valid = mask[...].astype(F32)
-    lane = lax.broadcasted_iota(jnp.int32, (1, LANES), 1)
-    count = jnp.where(
-        lane == 0,
-        jnp.sum(valid[0:1], 1, keepdims=True),
-        jnp.where(lane == 1, jnp.sum(valid[1:2], 1, keepdims=True), 0.0),
-    ).astype(jnp.int32)
-    for part in range(size.groups):
-        for one in range(experts):
-            peer = part * experts + one
-            message[peer, :, :slots] = requests[part, one : one + 1, :]
-            message[peer, :, slots:] = count
-    gathered[group, expert, : size.first, :] = first[...].astype(BF)
-    half = size.second // 2
-    gathered[group, expert, size.first :, :LANES] = second[:half].astype(BF)
-    gathered[group, expert, size.first :, LANES:] = second[half:].astype(BF)
-    blocks = size.rows // KEYS
-    for block in range(blocks):
-        cells[block * EMB : (block + 1) * EMB, :] = table[
-            :, block * KEYS : (block + 1) * KEYS
-        ].astype(BF)
-    pl.semaphore_wait(barrier, devices - 1)
-
-    def ask(step, receive):
-        peer = lax.rem(me + (devices - step if receive else step), devices)
-        return push(
-            message.at[peer],
-            asked.at[peer if receive else me],
-            ask_sent.at[step],
-            ask_landed.at[peer if receive else me],
-            place(size, peer),
-        )
-
-    def answer(step, receive):
-        peer = lax.rem(me + devices - step, devices)
-        return push(
-            rows.at[peer],
-            got.at[me],
-            row_sent.at[step],
-            row_landed.at[me],
-            place(size, peer),
-        )
-
-    def arrival(step):
-        peer = lax.rem(me + step, devices)
-        return push(
-            rows.at[peer],
-            got.at[peer],
-            row_sent.at[step],
-            row_landed.at[peer],
-            place(size, peer),
-        )
-
-    def along_z(step, receive):
-        other = lax.rem(expert + (experts - step if receive else step), experts)
-        block = gathered.at[group, other if receive else expert]
-        return push(
-            block, block, z_sent.at[step], z_landed.at[step], (group, other)
-        )
-
-    def along_y(step, receive):
-        other = lax.rem(chip + (chips - step if receive else step), chips)
-        block = gathered.at[(other if receive else chip) * 2 + core]
-        return push(
-            block, block, y_sent.at[step], y_landed.at[step], (other * 2 + core, expert)
-        )
-
-    def across(step, receive):
-        other = lax.rem(chip + chips - step, chips)
-        block = gathered.at[other * 2 + (1 - core if receive else core)]
-        return push(
-            block, block, c_sent.at[step], c_landed.at[step], (chip * 2 + 1 - core, expert)
-        )
-
-    def start_ask(step, carry):
-        ask(step, False).start()
-        return carry
-
-    lax.fori_loop(1, devices, start_ask, 0)
-    for step in range(1, experts):
-        along_z(step, False).start()
-
-    def serve(peer):
-        index = asked[peer, :, :slots]
-        rows[peer] = look_up(cells[...], index & (KEYS - 1), index >> 8, blocks).astype(BF)
-
-    asked[me] = message[me]
-    serve(me)
-    got[me] = rows[me]
-
-    def serve_one(step, carry):
-        peer = lax.rem(me + devices - step, devices)
-        ask(step, True).wait_recv()
-        serve(peer)
-        answer(step, False).start()
-        return carry
-
-    third = devices // 4
-    lax.fori_loop(1, third, serve_one, 0)
-    for step in range(1, experts):
-        along_z(step, True).wait_recv()
-    for step in range(1, chips):
-        along_y(step, False).start()
-    across(0, False).start()
-    lax.fori_loop(third, devices, serve_one, 0)
-    for step in range(1, chips):
-        along_y(step, True).wait_recv()
-        across(step, False).start()
-    total = jnp.zeros((1, LANES), jnp.int32)
-    for peer in range(devices):
-        total = total + asked[peer, :, slots:]
-    totals[...] = jnp.maximum(total.astype(F32), 1.0)
-
-    def finish(step, carry):
-        arrival(step).wait_recv()
-        ask(step, False).wait_send()
-        answer(step, False).wait_send()
-        return carry
-
-    lax.fori_loop(1, devices, finish, 0)
-    for step in range(1, experts):
-        along_z(step, False).wait_send()
-    for step in range(1, chips):
-        along_y(step, False).wait_send()
-    for step in range(chips):
-        across(step, True).wait_recv()
-        across(step, False).wait_send()
-
-
-def sigmoid(value):
-    return 0.5 + 0.5 * jnp.tanh(0.5 * value)
-
-
-def middle(
-    size,
     got,
-    picks,
-    dense,
-    labels,
-    mask,
-    totals,
+    slots_out,
+    slots_got,
     gathered,
+    grads,
+    core_got,
+    core_sum,
+    chip_got,
+    chip_sum,
+    z_got,
     vectors,
+    columns,
+    gate_rows,
     gate_t,
-    gate_n,
+    tower_rows,
     tower_n,
     tower_t,
+    dense_rows,
     dense_w,
-    out_slots,
-    out_grads,
-    out_bias_one,
-    out_bias_two,
-    out_dense,
-    out_gate,
-    out_tower,
-    out_head,
-    out_loss,
-    columns,
+    small_part,
+    small_got,
     first_t,
     second_n,
     second_t,
@@ -670,14 +569,285 @@
     sum_tower,
     sum_head,
     loss_sum,
+    ask_sent,
+    ask_landed,
+    row_sent,
+    row_landed,
+    slot_sent,
+    slot_landed,
+    small_sent,
+    small_landed,
+    whole_sent,
+    whole_landed,
+    gz_sent,
+    gz_landed,
+    gy_sent,
+    gy_landed,
+    gc_sent,
+    gc_landed,
+    sz_sent,
+    sz_landed,
+    sy_sent,
+    sy_landed,
+    sc_sent,
+    sc_landed,
 ):
-    experts, slots = size.experts, size.slots
-    levels = size.devices // 2
+    group, expert_here, me = here(size)
+    slots, devices, experts = size.slots, size.devices, size.experts
+    chips = size.groups // 2
+    chip, core = lax.div(group, 2), lax.rem(group, 2)
+    blocks = size.rows // KEYS
+    half = size.second // 2
+    levels = devices // 2
     shift = slots.bit_length() - 1
-    half = size.second // 2
-    flipped = jnp.concatenate([vectors[...], jnp.zeros((LANES - 16, LANES), F32)], 0).T
+    chunks = size.tokens // CHUNK
+    gates_wide = TASKS * experts
+    at_one, at_two, at_dense, at_gate, at_tower, at_head, at_loss = offsets(experts)
+    lane = lanes_of()
+    barrier = greet(size, me)
+
+    def own_lines(device):
+        count = small_got.shape[1]
+        return pl.ds(pl.multiple_of(device * count, count), count)
+
+    def to_all(source, target, sent, landed, step, receive):
+        peer = lax.rem(me + (devices - step if receive else step), devices)
+        return push(
+            source(peer),
+            target(peer if receive else me),
+            sent.at[step],
+            landed.at[peer if receive else me],
+            place(size, peer),
+        )
+
+    def ask(step, receive):
+        return to_all(
+            lambda p: message.at[p], lambda p: asked.at[p], ask_sent, ask_landed, step, receive
+        )
+
+    def answer(part, step, receive):
+        peer = lax.rem(me + (step if receive else devices - step), devices)
+        return push(
+            rows.at[part, peer],
+            got.at[part, peer if receive else me],
+            row_sent.at[part, step],
+            row_landed.at[part, peer if receive else me],
+            place(size, peer),
+        )
+
+    def give_slots(part, step, receive):
+        return to_all(
+            lambda p: slots_out.at[part, p],
+            lambda p: slots_got.at[part, p],
+            slot_sent.at[part],
+            slot_landed.at[part],
+            step,
+            receive,
+        )
+
+    def give_small(step, receive):
+        return to_all(
+            lambda p: small_part.at[own_lines(p), :],
+            lambda p: small_got.at[p],
+            small_sent,
+            small_landed,
+            step,
+            receive,
+        )
+
+    def give_whole(step, receive):
+        return to_all(
+            lambda p: small_sum.at[own_lines(me), :],
+            lambda p: small_sum.at[own_lines(p), :],
+            whole_sent,
+            whole_landed,
+            step,
+            receive,
+        )
+
+    def turned(index, count, step, receive):
+        return lax.rem(index + (count - step if receive else step), count)
+
+    def weights_z(step, receive):
+        other = turned(expert_here, experts, step, receive)
+        block = gathered.at[group, other if receive else expert_here]
+        return push(block, block, gz_sent.at[step], gz_landed.at[step], (group, other))
+
+    def weights_y(step, receive):
+        other = turned(chip, chips, step, receive)
+        block = gathered.at[(other if receive else chip) * 2 + core]
+        return push(
+            block, block, gy_sent.at[step], gy_landed.at[step], (other * 2 + core, expert_here)
+        )
+
+    def weights_c(step, receive):
+        other = turned(chip, chips, step, True)
+        block = gathered.at[other * 2 + (1 - core if receive else core)]
+        return push(
+            block, block, gc_sent.at[step], gc_landed.at[step], (chip * 2 + 1 - core, expert_here)
+        )
+
+    def sums_c(step):
+        other = turned(chip, chips, step, False)
+        return push(
+            grads.at[other * 2 + 1 - core],
+            core_got.at[other],
+            sc_sent.at[step],
+            sc_landed.at[step],
+            (chip * 2 + 1 - core, expert_here),
+        )
+
+    def sums_y(step, receive):
+        other = turned(chip, chips, step, receive)
+        return push(
+            core_sum.at[other],
+            chip_got.at[step],
+            sy_sent.at[step],
+            sy_landed.at[step],
+            (other * 2 + core, expert_here),
+        )
+
+    def sums_z(step, receive):
+        other = turned(expert_here, experts, step, receive)
+        return push(
+            chip_sum.at[other],
+            z_got.at[step],
+            sz_sent.at[step],
+            sz_landed.at[step],
+            (group, other),
+        )
+
+    def loop(begin, end, body, unroll=1):
+        def one(step, carry):
+            body(step)
+            return carry
+
+        lax.fori_loop(begin, end, one, 0, unroll=unroll)
+
+    valid = mask[...].astype(F32)
+    count = jnp.where(
+        lane == 0,
+        jnp.sum(valid[0:1], 1, keepdims=True),
+        jnp.where(lane == 1, jnp.sum(valid[1:2], 1, keepdims=True), 0.0),
+    ).astype(jnp.int32)
+    for part in range(size.groups):
+        for one in range(experts):
+            peer = part * experts + one
+            message[peer, :, :slots] = requests[part, one : one + 1, :]
+            message[peer, :, slots:] = count
+    gathered[group, expert_here, : size.first, :] = first[...].astype(BF)
+    gathered[group, expert_here, size.first :, :LANES] = second[:half].astype(BF)
+    gathered[group, expert_here, size.first :, LANES:] = second[half:].astype(BF)
+    for block in range(blocks):
+        cells[block * EMB : (block + 1) * EMB, :] = table[
+            :, block * KEYS : (block + 1) * KEYS
+        ].astype(BF)
+    pl.semaphore_wait(barrier, devices - 1)
+    loop(1, devices, lambda step: ask(step, False).start())
+    for step in range(1, experts):
+        weights_z(step, False).start()
+
+    vectors[...] = jnp.zeros_like(vectors)
+    vectors[: at_dense // LANES, :] = small[: at_dense // LANES, :]
+    lines = take(small, at_tower, TASKS * (OUT + 1) * TOWER // LANES)
+    count_rows = lines.shape[0]
+    tower_rows[pl.ds(0, count_rows, stride=2), :] = lines
+    tower_rows[pl.ds(1, count_rows, stride=2), :] = turn(lines, TOWER)
+    for task in range(TASKS):
+        base = task * (OUT + 1)
+        block = tower_rows[base : base + OUT, :]
+        tower_n[task] = block[:, :TOWER].astype(BF)
+        tower_t[task] = block.T[:TOWER].astype(BF)
+    last = [tower_rows[k * (OUT + 1) + OUT : (k + 1) * (OUT + 1), :] for k in range(TASKS)]
+    vectors[12:13, :] = jnp.where(lane < TOWER, last[0], turn(last[1], TOWER))
+    heads = [take(small, at_head, 1)]
+    end = at_head + TOWER + 1
+    heads.append(turn(small[end // LANES : end // LANES + 1, :], -(end % LANES)))
+    vectors[13:14, :] = jnp.where(lane < TOWER, heads[0], turn(heads[1], TOWER))
+    vectors[15:16, :] = jnp.where(lane == 0, turn(heads[0], -TOWER), turn(heads[1], 1 - TOWER))
+    per_line = LANES // gates_wide
+    lines = take(small, at_gate, INPUT // per_line + 1)
+    for spot in range(per_line):
+        gate_rows[pl.ds(spot, lines.shape[0], stride=per_line), :] = jnp.where(
+            lanes_of(lines.shape[0]) < gates_wide, turn(lines, -spot * gates_wide), 0.0
+        )
+    for block in range(INPUT // LANES):
+        piece = gate_rows[block * LANES : (block + 1) * LANES, :]
+        gate_t[:, block * LANES : (block + 1) * LANES] = piece.T[:16].astype(BF)
+        wide[block * LANES : (block + 1) * LANES, experts * HID :] = piece.astype(BF)
+    vectors[14:15, :] = gate_rows[INPUT : INPUT + 1, :]
+    dense_rows[...] = jnp.zeros_like(dense_rows)
+    for line in range(DENSE + 1):
+        dense_rows[line : line + 1, :] = take(small, at_dense + line * DOUT, 1)
+    dense_w[...] = dense_rows[...].T[:DOUT, :16]
+    flipped = vectors[...].T
     for column in range(16):
         columns[column] = jnp.broadcast_to(flipped[:, column : column + 1], (LANES, LANES))
+    feats[...] = jnp.ones_like(feats)
+    feats[:DENSE, :] = dense[...]
+    inputs[INPUT:, :] = jnp.ones((ONES, CHUNK), BF)
+    for expert in range(experts):
+        hidden[expert, HID:, :] = jnp.ones((ONES, CHUNK), BF)
+    for task in range(TASKS):
+        mixes[task, OUT:, :] = jnp.ones((ONES, CHUNK), BF)
+    deltas[experts * HID :, :] = jnp.zeros((LANES, CHUNK), BF)
+    for total in (
+        sum_first,
+        sum_second,
+        sum_gate,
+        sum_dense,
+        sum_tower,
+        sum_head,
+        loss_sum,
+        small_part,
+        table_grad,
+    ):
+        total[...] = jnp.zeros_like(total)
+
+    asked[me] = message[me]
+    batch = 4
+
+    def serve(part, first_round):
+        columns_here = pl.ds(part * LANES, LANES)
+
+        def some(turn_no, own):
+            steps = [turn_no * batch + i for i in range(batch)]
+            peers = [lax.rem(me + devices - step, devices) for step in steps]
+            if first_round:
+                for i, step in enumerate(steps):
+                    if not (own and i == 0):
+                        ask(step, True).wait_recv()
+            index = jnp.concatenate([asked[peer, :, columns_here] for peer in peers], 1)
+            found = look_up(cells[...], index & (KEYS - 1), index >> 8, blocks).astype(BF)
+            for i, peer in enumerate(peers):
+                piece = found[:, i * LANES : (i + 1) * LANES]
+                if own and i == 0:
+                    got[part, peer] = piece
+                else:
+                    rows[part, peer] = piece
+                    answer(part, steps[i], False).start()
+
+        some(0, True)
+        loop(1, devices // batch, lambda turn_no: some(turn_no, False))
+
+    serve(0, True)
+    for step in range(1, experts):
+        weights_z(step, True).wait_recv()
+    for step in range(1, chips):
+        weights_y(step, False).start()
+    weights_c(0, False).start()
+    total = jnp.zeros((1, LANES), jnp.int32)
+    for peer in range(devices):
+        total = total + asked[peer, :, slots:]
+    totals = jnp.maximum(total.astype(F32), 1.0)
+    for part in range(1, chunks):
+        serve(part, False)
+        if part == chunks - 2:
+            for step in range(1, chips):
+                weights_y(step, True).wait_recv()
+                weights_c(step, False).start()
+    for step in range(chips):
+        weights_c(step, True).wait_recv()
     for expert in range(experts):
         for part in range(size.groups):
             wide[
@@ -690,38 +860,26 @@
             ]
         first_t[expert] = wide[:, expert * HID : (expert + 1) * HID].T
         second_t[expert] = second_n[expert].T
-    wide[:, experts * HID :] = gate_n[...]
-    feats[...] = jnp.ones_like(feats)
-    feats[:DENSE, :] = dense[...]
-    inputs[INPUT:, :] = jnp.ones((ONES, CHUNK), BF)
-    for expert in range(experts):
-        hidden[expert, HID:, :] = jnp.ones((ONES, CHUNK), BF)
-    for task in range(TASKS):
-        mixes[task, OUT:, :] = jnp.ones((ONES, CHUNK), BF)
-    deltas[experts * HID :, :] = jnp.zeros((LANES, CHUNK), BF)
-    for total in (sum_first, sum_second, sum_gate, sum_dense, sum_tower, sum_head, loss_sum):
-        total[...] = jnp.zeros_like(total)
 
     def column(index, begin=0, end=LANES):
         block = columns[index, begin:end, :]
         return jnp.concatenate([block] * (CHUNK // LANES), 1)
 
-    def chunk(step, carry):
-        token = pl.multiple_of(step * CHUNK, CHUNK)
-        slot = pl.multiple_of(step * LANES, LANES)
-        here_tokens = pl.ds(token, CHUNK)
-        for owner in range(size.devices):
+    def chunk(step):
+        here_tokens = pl.ds(pl.multiple_of(step * CHUNK, CHUNK), CHUNK)
+        loop(1, devices, lambda hop: answer(step, hop, True).wait_recv())
+        for owner in range(devices):
             level, lower = owner // 2, owner % 2
             slot_cells[
                 level * EMB : (level + 1) * EMB, lower * LANES : (lower + 1) * LANES
-            ] = got[owner, :, pl.ds(slot, LANES)]
+            ] = got[step, owner]
 
         def split(field):
             index = picks[pl.ds(field, 1), here_tokens]
             owner = index >> shift
             return (owner & 1) * LANES + (index & (LANES - 1)), owner >> 1
 
-        def pick(field, carry):
+        def pick(field):
             key, high = split(field)
             flags = as_low(spread(key, KEYS, CHUNK))
             chosen[field] = flags
@@ -730,14 +888,13 @@
             for level in range(1, levels):
                 result = jnp.where(high == level, found[level * EMB : (level + 1) * EMB], result)
             inputs[pl.ds(pl.multiple_of(field * EMB, EMB), EMB), :] = result.astype(BF)
-            return carry
-
-        lax.fori_loop(0, FIELDS, pick, 0)
+
+        loop(0, FIELDS, pick, 13)
         inputs[FIELDS * EMB : INPUT, :] = mm(
             dense_w[...], feats[:, here_tokens], precision=HI
         ).astype(BF)
         x = inputs[:INPUT, :]
-        logits = mm(gate_t[...], x)[: TASKS * experts] + column(14, 0, TASKS * experts)
+        logits = mm(gate_t[...], x)[:gates_wide] + column(14, 0, gates_wide)
         probs, gates = [], []
         for task in range(TASKS):
             line = [logits[task * experts + e : task * experts + e + 1] for e in range(experts)]
@@ -772,16 +929,17 @@
             act = pre * sig
             head = column(13, low, high)
             logit = jnp.sum(act * head, 0, keepdims=True) + column(15, task, task + 1)
-            valid = mask[task : task + 1, here_tokens].astype(F32)
+            scale = mask[task : task + 1, here_tokens].astype(F32) / totals[:, task : task + 1]
             target = labels[task : task + 1, here_tokens].astype(F32)
-            scale = valid / totals[0:1, task : task + 1]
             soft = jnp.maximum(logit, 0.0) + jnp.log(1.0 + jnp.exp(-jnp.abs(logit)))
             loss_sum[...] += scale * (soft - target * logit)
             d_logit = scale * (sigmoid(logit) - target)
             d_pre = ((sig + act * (1.0 - sig)) * (d_logit * head)).astype(BF)
             sum_head[task] += mm(
                 jnp.broadcast_to(d_logit, (8, CHUNK)),
-                jnp.concatenate([act, jnp.ones((8, CHUNK), F32)], 0),
+                jnp.concatenate(
+                    [act, jnp.ones((8, CHUNK), F32), jnp.zeros((LANES - TOWER - 8, CHUNK), F32)], 0
+                ),
                 NT,
                 HI,
             )
@@ -803,215 +961,157 @@
                 jnp.add, [probs[task][e] * d_gates[task][e] for e in range(experts)]
             )
             lines += [probs[task][e] * (d_gates[task][e] - inner) for e in range(experts)]
-        lines.append(jnp.zeros((16 - TASKS * experts, CHUNK), F32))
-        d_gate = jnp.concatenate(lines, 0).astype(BF)
-        deltas[experts * HID : experts * HID + 16, :] = d_gate
-        sum_gate[...] += mm(inputs[...], d_gate, NT)
+        lines.append(jnp.zeros((16 - gates_wide, CHUNK), F32))
+        deltas[experts * HID : experts * HID + 16, :] = jnp.concatenate(lines, 0).astype(BF)
+        sum_gate[...] += mm(inputs[...], deltas[experts * HID :, :], NT)
         d_inputs[...] = mm(wide[...], deltas[...])
-        sum_dense[...] += mm(feats[:, here_tokens], d_inputs[FIELDS * EMB :, :], NT, HI)
+        sum_dense[...] += mm(feats[:, here_tokens], d_inputs[INPUT - LANES :, :], NT, HI)
         slot_sum[...] = jnp.zeros_like(slot_sum)
 
-        def give(field, carry):
+        def give(field):
             key, high = split(field)
             values = d_inputs[pl.ds(pl.multiple_of(field * EMB, EMB), EMB), :]
             slot_sum[...] += mm(levels_of(values, high, levels), chosen[field], NT)
-            return carry
-
-        lax.fori_loop(0, FIELDS, give, 0)
-        for owner in range(size.devices):
+
+        loop(0, FIELDS, give, 13)
+        for owner in range(devices):
             level, lower = owner // 2, owner % 2
-            out_slots[owner, :, pl.ds(slot, LANES)] = slot_sum[
+            slots_out[step, owner] = slot_sum[
                 level * EMB : (level + 1) * EMB, lower * LANES : (lower + 1) * LANES
             ].astype(BF)
-        return carry
-
-    lax.fori_loop(0, size.tokens // CHUNK, chunk, 0)
-    for expert in range(experts):
-        for part in range(size.groups):
-            out_grads[part, expert, : size.first, :] = sum_first[
+        loop(1, devices, lambda hop: give_slots(step, hop, False).start())
+        slots_got[step, me] = slots_out[step, me]
+
+    loop(0, chunks, chunk)
+
+    for part in range(size.groups):
+        base = part * size.second
+        for expert in range(experts):
+            grads[part, expert, : size.first, :] = sum_first[
                 expert, part * size.first : (part + 1) * size.first, :
             ].astype(BF)
-            base = part * size.second
-            out_grads[part, expert, size.first :, :LANES] = sum_second[
+            grads[part, expert, size.first :, :LANES] = sum_second[
                 expert, base : base + half, :
             ].astype(BF)
-            out_grads[part, expert, size.first :, LANES:] = sum_second[
+            grads[part, expert, size.first :, LANES:] = sum_second[
                 expert, base + half : base + 2 * half, :
             ].astype(BF)
-        out_bias_one[expert : expert + 1, :] = sum_first[expert, INPUT : INPUT + 1, :]
-        out_bias_two[expert : expert + 1, :] = sum_second[expert, HID : HID + 1, :]
-    out_dense[...] = sum_dense[...]
-    out_gate[...] = sum_gate[...]
-    out_tower[...] = sum_tower[...]
-    out_head[...] = sum_head[...]
-    out_loss[...] = loss_sum[...]
-
-
-def back(
-    size,
-    slots_in,
-    asked,
-    grads,
-    small,
-    table_grad,
-    first_grad,
-    second_grad,
-    small_sum,
-    slots_got,
-    small_got,
-    core_got,
-    core_sum,
-    chip_got,
-    chip_sum,
-    z_got,
-    slot_sent,
-    slot_landed,
-    small_sent,
-    small_landed,
-    whole_sent,
-    whole_landed,
-    c_sent,
-    c_landed,
-    y_sent,
-    y_landed,
-    z_sent,
-    z_landed,
-):
-    group, expert, me = here(size)
-    slots, devices, experts = size.slots, size.devices, size.experts
-    chips = size.groups // 2
-    chip, core = lax.div(group, 2), lax.rem(group, 2)
-    blocks = size.rows // KEYS
-    barrier = greet(size, me)
-    table_grad[...] = jnp.zeros_like(table_grad)
-    pl.semaphore_wait(barrier, devices - 1)
-
-    def across(step, receive):
-        other = lax.rem(chip + step, chips)
-        return push(
-            grads.at[other * 2 + 1 - core],
-            core_got.at[other],
-            c_sent.at[step],
-            c_landed.at[step],
-            (chip * 2 + 1 - core, expert),
-        )
-
-    def along_y(step, receive):
-        other = lax.rem(chip + (chips - step if receive else step), chips)
-        return push(
-            core_sum.at[other],
-            chip_got.at[step],
-            y_sent.at[step],
-            y_landed.at[step],
-            (other * 2 + core, expert),
-        )
-
-    def along_z(step, receive):
-        other = lax.rem(expert + (experts - step if receive else step), experts)
-        return push(
-            chip_sum.at[other], z_got.at[step], z_sent.at[step], z_landed.at[step], (group, other)
-        )
-
-    def to_all(source, target, sent, landed, step, receive, mine=False):
-        peer = lax.rem(me + (devices - step if receive else step), devices)
-        return push(
-            source.at[me if mine else peer],
-            target.at[peer if receive else me],
-            sent.at[step],
-            landed.at[peer if receive else me],
-            place(size, peer),
-        )
-
-    def send_slots(step, receive):
-        return to_all(slots_in, slots_got, slot_sent, slot_landed, step, receive)
-
-    def send_small(step, receive):
-        return to_all(small, small_got, small_sent, small_landed, step, receive)
-
-    def send_whole(step, receive):
-        return to_all(small_sum, small_sum, whole_sent, whole_landed, step, receive, True)
-
     for step in range(1, chips + 1):
-        across(step % chips, False).start()
-
-    def start_small(step, carry):
-        send_small(step, False).start()
-        return carry
-
-    lax.fori_loop(1, devices, start_small, 0)
-
-    def start_slots(step, carry):
-        send_slots(step, False).start()
-        return carry
-
-    lax.fori_loop(1, devices, start_slots, 0)
+        sums_c(step % chips).start()
+    for expert in range(experts):
+        per = HID // LANES
+        for piece in range(per):
+            line = expert * per + piece
+            small_part[line : line + 1, :] = sum_first[
+                expert, INPUT : INPUT + 1, piece * LANES : (piece + 1) * LANES
+            ]
+        line = experts * per + expert
+        small_part[line : line + 1, :] = sum_second[expert, HID : HID + 1, :]
+    for line in range(DENSE + 1):
+        values = jnp.where(lane < DOUT, turn(sum_dense[line : line + 1, :], DOUT - LANES), 0.0)
+        put(small_part, at_dense + line * DOUT, values)
+    lines = INPUT // per_line + 1
+    packed = jnp.zeros((lines, LANES), F32)
+    for spot in range(per_line):
+        packed = packed + turn(sum_gate[pl.ds(spot, lines, stride=per_line), :], spot * gates_wide)
+    inside = lax.broadcasted_iota(jnp.int32, (lines, LANES), 0) < lines - 1
+    put(
+        small_part,
+        at_gate,
+        jnp.where(inside | (lanes_of(lines) < gates_wide), packed, 0.0),
+    )
+    tower_rows[...] = jnp.zeros_like(tower_rows)
+    for task in range(TASKS):
+        base = task * (OUT + 1)
+        tower_rows[base : base + OUT + 1, :TOWER] = sum_tower[task, : OUT + 1, :]
+    put(
+        small_part,
+        at_tower,
+        tower_rows[pl.ds(0, count_rows, stride=2), :]
+        + turn(tower_rows[pl.ds(1, count_rows, stride=2), :], TOWER),
+    )
+    for task in range(TASKS):
+        put(
+            small_part,
+            at_head + task * (TOWER + 1),
+            jnp.where(lane < TOWER + 1, sum_head[task, 0:1, :], 0.0),
+        )
+    whole_loss = jnp.sum(loss_sum[...], 1, keepdims=True)
+    put(small_part, at_loss, jnp.where(lane == 0, whole_loss, 0.0))
+    loop(1, devices, lambda step: give_small(step, False).start())
+
+    def collect(part):
+        columns_here = pl.ds(part * LANES, LANES)
+
+        def some(turn_no, own):
+            steps = [turn_no * batch + i for i in range(batch)]
+            peers = [lax.rem(me + devices - step, devices) for step in steps]
+            for i, step in enumerate(steps):
+                if not (own and i == 0):
+                    give_slots(part, step, True).wait_recv()
+            index = jnp.concatenate([asked[peer, :, columns_here] for peer in peers], 1)
+            values = jnp.concatenate([slots_got[part, peer] for peer in peers], 1).astype(F32)
+            spots = as_low(spread(index & (KEYS - 1), KEYS, batch * LANES))
+            table_grad[...] += mm(levels_of(values, index >> 8, blocks), spots, NT)
+
+        some(0, True)
+        loop(1, devices // batch, lambda turn_no: some(turn_no, False), devices // batch - 1)
+
+    collect(0)
     for step in range(1, chips + 1):
-        other = lax.rem(chip + step, chips)
-        across(step % chips, True).wait_recv()
+        other = turned(chip, chips, step % chips, False)
+        sums_c(step % chips).wait_recv()
         core_sum[other] = (
             grads[other * 2 + core].astype(F32) + core_got[other].astype(F32)
         ).astype(BF)
         if step < chips:
-            along_y(step, False).start()
-    small_got[me] = small[me]
+            sums_y(step, False).start()
+    collect(1)
+    small_got[me] = small_part[own_lines(me), :]
 
     def add_small(step, total):
-        send_small(step, True).wait_recv()
+        give_small(step, True).wait_recv()
         return total + small_got[lax.rem(me + devices - step, devices)]
 
-    small_sum[me] = lax.fori_loop(1, devices, add_small, small_got[me])
-
-    def start_whole(step, carry):
-        send_whole(step, False).start()
-        return carry
-
-    lax.fori_loop(1, devices, start_whole, 0)
+    small_sum[own_lines(me), :] = lax.fori_loop(1, devices, add_small, small_got[me])
+    loop(1, devices, lambda step: give_whole(step, False).start())
+    collect(2)
     total = core_sum[chip].astype(F32)
     for step in range(1, chips):
-        along_y(step, True).wait_recv()
+        sums_y(step, True).wait_recv()
         total = total + chip_got[step].astype(F32)
     chip_sum[...] = total.astype(BF)
     for step in range(1, experts):
-        along_z(step, False).start()
-
-    def gather(peer, values):
-        index = asked[peer, :, :slots]
-        levels = levels_of(values, index >> 8, blocks)
-        spots = as_low(spread(index & (KEYS - 1), KEYS, slots))
-        table_grad[...] += mm(levels, spots, NT)
-
-    gather(me, slots_in[me].astype(F32))
-
-    def gather_one(step, carry):
-        peer = lax.rem(me + devices - step, devices)
-        send_slots(step, True).wait_recv()
-        gather(peer, slots_got[peer].astype(F32))
-        return carry
-
-    lax.fori_loop(1, devices, gather_one, 0)
-    total = chip_sum[expert].astype(F32)
+        sums_z(step, False).start()
+    for part in range(3, chunks):
+        collect(part)
+    total = chip_sum[expert_here].astype(F32)
     for step in range(1, experts):
-        along_z(step, True).wait_recv()
+        sums_z(step, True).wait_recv()
         total = total + z_got[step].astype(F32)
-    half = size.second // 2
     first_grad[...] = total[: size.first]
     second_grad[:half, :] = total[size.first :, :LANES]
     second_grad[half:, :] = total[size.first :, LANES:]
 
-    def finish(step, carry):
-        send_whole(step, True).wait_recv()
-        send_whole(step, False).wait_send()
-        send_small(step, False).wait_send()
-        send_slots(step, False).wait_send()
-        return carry
-
-    lax.fori_loop(1, devices, finish, 0)
+    def finish(step):
+        give_whole(step, True).wait_recv()
+        ask(step, False).wait_send()
+        for part in range(chunks):
+            answer(part, step, False).wait_send()
+            give_slots(part, step, False).wait_send()
+        give_small(step, False).wait_send()
+        give_whole(step, False).wait_send()
+
+    loop(1, devices, finish)
     for step in range(chips):
-        across(step, False).wait_send()
+        weights_c(step, False).wait_send()
+        sums_c(step).wait_send()
     for step in range(1, chips):
-        along_y(step, False).wait_send()
+        weights_y(step, False).wait_send()
+        sums_y(step, False).wait_send()
     for step in range(1, experts):
-        along_z(step, False).wait_send()
+        weights_z(step, False).wait_send()
+        sums_z(step, False).wait_send()
 
 
 def update(size, *refs):
@@ -1044,10 +1144,6 @@
         scratch_shapes=scratch,
         compiler_params=pltpu.CompilerParams(**params),
     )(*args)
-
-
-def pads(array, dims):
-    return jnp.pad(array, [(0, want - have) for want, have in zip(dims, array.shape)])
 
 
 def local(
@@ -1072,56 +1168,44 @@
 ):
     devices, experts, groups = size.devices, size.experts, size.groups
     chips = groups // 2
+    chunks = size.tokens // CHUNK
     dma = pltpu.SemaphoreType.DMA
     vm = pltpu.VMEM
     message = size.slots + LANES
-    asked, got, gathered, totals = call(
-        functools.partial(front, size),
+    count = small.shape[0]
+    lines = -(-(count + 1) // (devices * 8 * LANES)) * 8
+    flat_lines = -(-count // LANES)
+    exchange = vm((chunks, devices, EMB, LANES), BF)
+    weights = vm((groups, experts, size.pack, HID), BF)
+    of_chips = vm((chips, experts, size.pack, HID), BF)
+    of_chip = vm((experts, size.pack, HID), BF)
+    table_grad, first_grad, second_grad, flat = call(
+        functools.partial(step_kernel, size),
         [
-            shape((devices, 1, message), jnp.int32),
-            shape((devices, EMB, size.slots), BF),
-            shape((groups, experts, size.pack, HID), BF),
-            shape((1, LANES)),
+            shape((size.rows // KEYS * EMB, KEYS)),
+            shape((size.first, HID)),
+            shape((size.second, OUT)),
+            shape((devices * lines, LANES)),
         ],
         [
             vm((devices, 1, message), jnp.int32),
+            vm((devices, 1, message), jnp.int32),
             vm((size.rows // KEYS * EMB, KEYS), BF),
-            vm((devices, EMB, size.slots), BF),
         ]
-        + [dma((devices,))] * 4
-        + [dma((experts,))] * 2
-        + [dma((chips,))] * 4,
-        0,
-    )(requests[0], label_mask.T, table.T, first_w[0], second_w[0])
-    bias_one, bias_two, dense_w, gate_w, tower_w, head_w = unpack(small, experts)
-    vectors = jnp.concatenate(
-        [
-            bias_one.reshape(8, LANES),
-            bias_two,
-            tower_w[:, OUT].reshape(1, LANES),
-            head_w[:, :TOWER].reshape(1, LANES),
-            pads(gate_w[INPUT][None], (1, LANES)),
-            pads(head_w[:, TOWER][None], (1, LANES)),
-        ],
-        0,
-    )
-    gate_low = gate_w[:INPUT].astype(BF)
-    tower_low = tower_w[:, :OUT].astype(BF)
-    outs = call(
-        functools.partial(middle, size),
-        [
-            shape((devices, EMB, size.slots), BF),
-            shape((groups, experts, size.pack, HID), BF),
-            shape((experts, HID)),
-            shape((experts, OUT)),
-            shape((16, DOUT)),
-            shape((INPUT + ONES, 16)),
-            shape((TASKS, OUT + ONES, TOWER)),
-            shape((TASKS, 8, TOWER + 8)),
-            shape((1, CHUNK)),
-        ],
-        [
+        + [exchange] * 4
+        + [weights, weights, of_chips, of_chips, of_chips, of_chip, of_chip]
+        + [
+            vm((LANES, LANES), F32),
             vm((16, LANES, LANES), F32),
+            vm((INPUT + ONES, LANES), F32),
+            vm((16, INPUT), BF),
+            vm((TASKS * (OUT + 1) + 6, LANES), F32),
+            vm((TASKS, OUT, TOWER), BF),
+            vm((TASKS, TOWER, OUT), BF),
+            vm((LANES, LANES), F32),
+            vm((DOUT, 16), F32),
+            vm((devices * lines, LANES), F32),
+            vm((devices, lines, LANES), F32),
             vm((experts, HID, INPUT), BF),
             vm((experts, HID, OUT), BF),
             vm((experts, OUT, HID), BF),
@@ -1140,64 +1224,31 @@
             vm((devices // 2 * EMB, KEYS), F32),
             vm((experts, INPUT + ONES, HID), F32),
             vm((experts, HID + ONES, OUT), F32),
-            vm((INPUT + ONES, 16), F32),
-            vm((16, DOUT), F32),
+            vm((INPUT + ONES, LANES), F32),
+            vm((16, LANES), F32),
             vm((TASKS, OUT + ONES, TOWER), F32),
-            vm((TASKS, 8, TOWER + 8), F32),
+            vm((TASKS, 8, LANES), F32),
             vm((1, CHUNK), F32),
-        ],
+        ]
+        + [dma((devices,))] * 2
+        + [dma((chunks, devices))] * 4
+        + [dma((devices,))] * 4
+        + [dma((experts,))] * 2
+        + [dma((chips,))] * 4
+        + [dma((experts,))] * 2
+        + [dma((chips,))] * 4,
+        0,
     )(
-        got,
+        requests[0],
         picks.T,
         dense_feats.T,
         labels.T,
         label_mask.T,
-        totals,
-        gathered,
-        vectors,
-        pads(gate_low.T, (16, INPUT)),
-        pads(gate_low, (INPUT, LANES)),
-        tower_low,
-        tower_low.transpose(0, 2, 1),
-        pads(dense_w.T, (DOUT, 16)),
-    )
-    slot_grads, grads, d_bias_one, d_bias_two, d_dense, d_gate, d_tower, d_head, loss = outs
-    flat = jnp.concatenate(
-        [
-            d_bias_one.reshape(-1),
-            d_bias_two.reshape(-1),
-            d_dense[: DENSE + 1].reshape(-1),
-            d_gate[: INPUT + 1, : TASKS * experts].reshape(-1),
-            d_tower[:, : OUT + 1].reshape(-1),
-            d_head[:, 0, : TOWER + 1].reshape(-1),
-            jnp.sum(loss).reshape(1),
-        ]
-    )
-    count = flat.shape[0] - 1
-    lines = -(-(count + 1) // (devices * 8 * LANES)) * 8
-    flat = jnp.pad(flat, (0, devices * lines * LANES - count - 1)).reshape(devices, lines, LANES)
-    table_grad, first_grad, second_grad, flat = call(
-        functools.partial(back, size),
-        [
-            shape((size.rows // KEYS * EMB, KEYS)),
-            shape((size.first, HID)),
-            shape((size.second, OUT)),
-            shape((devices, lines, LANES)),
-        ],
-        [
-            vm((devices, EMB, size.slots), BF),
-            vm((devices, lines, LANES), F32),
-            vm((chips, experts, size.pack, HID), BF),
-            vm((chips, experts, size.pack, HID), BF),
-            vm((chips, experts, size.pack, HID), BF),
-            vm((experts, size.pack, HID), BF),
-            vm((experts, size.pack, HID), BF),
-        ]
-        + [dma((devices,))] * 6
-        + [dma((chips,))] * 4
-        + [dma((experts,))] * 2,
-        1,
-    )(slot_grads, asked, grads, flat)
+        table.T,
+        first_w[0],
+        second_w[0],
+        jnp.pad(small, (0, flat_lines * LANES - count)).reshape(flat_lines, LANES),
+    )
     tables = (table.T, table_m.T, table_v.T)
     firsts = (first_w[0], first_m[0], first_v[0])
     seconds = (second_w[0], second_m[0], second_v[0])

time: 157 us -> 95.7 us (0.61)
  Pallas kernels: 135 us -> 91.9 us
  local copies, waits for them, and re-layouts: 17.5 us -> 2.15 us
  other arithmetic: 2.94 us -> 0.75 us
    pallas_call x4 -> x2, Pallas kernels: 135 us -> 91.9 us  [call(): pl.pallas_call(kernel, out_shape=outs, in_specs=[vmem] * len(args), out_s...]
    slice x12 -> x0, local copies, waits for them, and re-layouts: 7.56 us -> none  [the longest x3 2.45 us: unpack(): parts.append(flat[offset:offset + length].reshape(shape))]
    concatenate x2 -> x0, local copies, waits for them, and re-layouts: 2 us -> none  [the longest x1 1.2 us: local(): jnp.concatenate([bias_one.reshape(8, LANES), bias_two, tower_w[:, OUT].re...]
    pad x5 -> x0, local copies, waits for them, and re-layouts: 1.95 us -> none  [pads(): jnp.pad(array, [(0, want - have) for want, have in zip(dims, array.shape)])]
where the time goes in v2:
time: 95.7 us; the launch traced here: 95.5 us
  Pallas kernels  91.9 us (96%)
  local copies, waits for them, and re-layouts  2.15 us (2%)
    pallas_call x2, Pallas kernels, call(): pl.pallas_call(kernel, out_shape=outs, in_specs=[vmem] * len(args), out_s...  91.9 us

profile of v2, /device:TPU:0, one launch (start us, length us, event | category | flops | bytes accessed | tf_op | source)
XLA Modules:
  0.0 95.5 jit_solution(8917669932130006722)
XLA Ops:
  0.6 1.5 %pad_bitcast_fusion.small = f32[185,128]{1,0:T(8,128)} fusion(f32[23626]{0:T(1024)} %param.31), kind=kLoop, calls=%fused_computation.4 | loop fusion | bytes 189224 | tf_op jit(solution)/shard_map/reshape | solution.py:1250
  2.2 89.4 %shard_map.264 = (f32[256,256]{1,0:T(8,128)}, f32[64,256]{1,0:T(8,128)}, f32[32,128]{1,0:T(8,128)}, f32[256,128]{1,0:T(8,128)}) custom-call(s32[8,4,512]{2,1,0:T(4,128)} %bitcast.38, s32[26,1024]{1,0:T(8,128)} %bitcast.33, f32[13,1024]{1,0:T(8,128)} %bitcast.39, s32[2,1024]{1,0:T(2,128)} %bitcast.44, s32[2,1024]{1,0:T(2,128)} %bitcast.45, ...), custom_call_target="tpu_custom_call" | custom-call | tf_op jit(solution)/shard_map/pallas_call | solution.py:1139
  91.6 0.0 copy-start
  91.6 0.0 copy-start.1
  91.6 0.0 copy-start.2
  91.6 0.0 copy-start.3
  91.6 2.5 %shard_map.265 = (f32[16,4096]{1,0:T(8,128)}, f32[16,4096]{1,0:T(8,128)}, f32[16,4096]{1,0:T(8,128)}, f32[64,256]{1,0:T(8,128)}, f32[64,256]{1,0:T(8,128)}, /*in...) custom-call(f32[256,256]{1,0:T(8,128)} %get-tuple-element.27.refs_0_, ...), custom_call_target="tpu_custom_call" | custom-call | tf_op jit(solution)/shard_map/pallas_call | solution.py:1139
  94.2 0.0 copy-done
  94.2 0.0 copy-done.1
  94.2 0.0 copy-done.2
  94.2 0.0 copy-done.3
  94.2 0.7 multiply_subtract_fusion
  94.9 0.6 slice.8
Async XLA Ops:
  91.6 2.6 %copy-start = (f32[23626]{0:T(1024)S(1)}, f32[23626]{0:T(1024)}, u32[]{:S(2)}) copy-start(f32[23626]{0:T(1024)} %param.31) | copy-start | bytes 283516
  91.6 2.6 %copy-start.1 = (f32[23626]{0:T(1024)S(1)}, f32[23626]{0:T(1024)}, u32[]{:S(2)}) copy-start(f32[23626]{0:T(1024)} %param.32) | copy-start | bytes 283516
  91.6 2.6 %copy-start.2 = (f32[23626]{0:T(1024)S(1)}, f32[23626]{0:T(1024)}, u32[]{:S(2)}) copy-start(f32[23626]{0:T(1024)} %param.33) | copy-start | bytes 283516
  91.6 2.6 %copy-start.3 = (f32[256,128]{1,0:T(8,128)S(1)}, f32[256,128]{1,0:T(8,128)}, u32[]{:S(2)}) copy-start(f32[256,128]{1,0:T(8,128)} %get-tuple-element.26) | copy-start | bytes 393220

commit v3 on v2

--- a/solution.py
+++ b/solution.py
@@ -615,8 +615,8 @@
         return push(
             source(peer),
             target(peer if receive else me),
-            sent.at[step],
-            landed.at[peer if receive else me],
+            sent,
+            landed,
             place(size, peer),
         )
 
@@ -630,8 +630,8 @@
         return push(
             rows.at[part, peer],
             got.at[part, peer if receive else me],
-            row_sent.at[part, step],
-            row_landed.at[part, peer if receive else me],
+            row_sent,
+            row_landed.at[part],
             place(size, peer),
         )
 
@@ -639,7 +639,7 @@
         return to_all(
             lambda p: slots_out.at[part, p],
             lambda p: slots_got.at[part, p],
-            slot_sent.at[part],
+            slot_sent,
             slot_landed.at[part],
             step,
             receive,
@@ -671,20 +671,20 @@
     def weights_z(step, receive):
         other = turned(expert_here, experts, step, receive)
         block = gathered.at[group, other if receive else expert_here]
-        return push(block, block, gz_sent.at[step], gz_landed.at[step], (group, other))
+        return push(block, block, gz_sent, gz_landed, (group, other))
 
     def weights_y(step, receive):
         other = turned(chip, chips, step, receive)
         block = gathered.at[(other if receive else chip) * 2 + core]
         return push(
-            block, block, gy_sent.at[step], gy_landed.at[step], (other * 2 + core, expert_here)
+            block, block, gy_sent, gy_landed, (other * 2 + core, expert_here)
         )
 
     def weights_c(step, receive):
         other = turned(chip, chips, step, True)
         block = gathered.at[other * 2 + (1 - core if receive else core)]
         return push(
-            block, block, gc_sent.at[step], gc_landed.at[step], (chip * 2 + 1 - core, expert_here)
+            block, block, gc_sent, gc_landed, (chip * 2 + 1 - core, expert_here)
         )
 
     def sums_c(step):
@@ -692,8 +692,8 @@
         return push(
             grads.at[other * 2 + 1 - core],
             core_got.at[other],
-            sc_sent.at[step],
-            sc_landed.at[step],
+            sc_sent,
+            sc_landed,
             (chip * 2 + 1 - core, expert_here),
         )
 
@@ -702,8 +702,8 @@
         return push(
             core_sum.at[other],
             chip_got.at[step],
-            sy_sent.at[step],
-            sy_landed.at[step],
+            sy_sent,
+            sy_landed,
             (other * 2 + core, expert_here),
         )
 
@@ -712,10 +712,17 @@
         return push(
             chip_sum.at[other],
             z_got.at[step],
-            sz_sent.at[step],
-            sz_landed.at[step],
+            sz_sent,
+            sz_landed,
             (group, other),
         )
+
+    def wait(semaphore, block):
+        pltpu.make_async_copy(block, block, semaphore).wait()
+
+    others = pl.ds(0, devices - 1)
+    other_chips = pl.ds(0, chips - 1)
+    other_experts = pl.ds(0, experts - 1)
 
     def loop(begin, end, body, unroll=1):
         def one(step, carry):
@@ -807,16 +814,12 @@
     asked[me] = message[me]
     batch = 4
 
-    def serve(part, first_round):
+    def serve(part):
         columns_here = pl.ds(part * LANES, LANES)
 
         def some(turn_no, own):
             steps = [turn_no * batch + i for i in range(batch)]
             peers = [lax.rem(me + devices - step, devices) for step in steps]
-            if first_round:
-                for i, step in enumerate(steps):
-                    if not (own and i == 0):
-                        ask(step, True).wait_recv()
             index = jnp.concatenate([asked[peer, :, columns_here] for peer in peers], 1)
             found = look_up(cells[...], index & (KEYS - 1), index >> 8, blocks).astype(BF)
             for i, peer in enumerate(peers):
@@ -828,11 +831,11 @@
                     answer(part, steps[i], False).start()
 
         some(0, True)
-        loop(1, devices // batch, lambda turn_no: some(turn_no, False))
-
-    serve(0, True)
-    for step in range(1, experts):
-        weights_z(step, True).wait_recv()
+        loop(1, devices // batch, lambda turn_no: some(turn_no, False), devices // batch - 1)
+
+    wait(ask_landed, asked.at[others])
+    serve(0)
+    wait(gz_landed, gathered.at[0, other_experts])
     for step in range(1, chips):
         weights_y(step, False).start()
     weights_c(0, False).start()
@@ -841,25 +844,11 @@
         total = total + asked[peer, :, slots:]
     totals = jnp.maximum(total.astype(F32), 1.0)
     for part in range(1, chunks):
-        serve(part, False)
+        serve(part)
         if part == chunks - 2:
+            wait(gy_landed, gathered.at[other_chips])
             for step in range(1, chips):
-                weights_y(step, True).wait_recv()
                 weights_c(step, False).start()
-    for step in range(chips):
-        weights_c(step, True).wait_recv()
-    for expert in range(experts):
-        for part in range(size.groups):
-            wide[
-                part * size.first : (part + 1) * size.first, expert * HID : (expert + 1) * HID
-            ] = gathered[part, expert, : size.first, :]
-            base = part * size.second
-            second_n[expert, base : base + half, :] = gathered[part, expert, size.first :, :LANES]
-            second_n[expert, base + half : base + 2 * half, :] = gathered[
-                part, expert, size.first :, LANES:
-            ]
-        first_t[expert] = wide[:, expert * HID : (expert + 1) * HID].T
-        second_t[expert] = second_n[expert].T
 
     def column(index, begin=0, end=LANES):
         block = columns[index, begin:end, :]
@@ -867,7 +856,7 @@
 
     def chunk(step):
         here_tokens = pl.ds(pl.multiple_of(step * CHUNK, CHUNK), CHUNK)
-        loop(1, devices, lambda hop: answer(step, hop, True).wait_recv())
+        wait(row_landed.at[step], got.at[step, others])
         for owner in range(devices):
             level, lower = owner // 2, owner % 2
             slot_cells[
@@ -890,6 +879,23 @@
             inputs[pl.ds(pl.multiple_of(field * EMB, EMB), EMB), :] = result.astype(BF)
 
         loop(0, FIELDS, pick, 13)
+
+        @pl.when(step == 0)
+        def weights_ready():
+            wait(gc_landed, gathered.at[pl.ds(0, chips)])
+            for expert in range(experts):
+                for part in range(size.groups):
+                    wide[
+                        part * size.first : (part + 1) * size.first, expert * HID : (expert + 1) * HID
+                    ] = gathered[part, expert, : size.first, :]
+                    base = part * size.second
+                    second_n[expert, base : base + half, :] = gathered[part, expert, size.first :, :LANES]
+                    second_n[expert, base + half : base + 2 * half, :] = gathered[
+                        part, expert, size.first :, LANES:
+                    ]
+                first_t[expert] = wide[:, expert * HID : (expert + 1) * HID].T
+                second_t[expert] = second_n[expert].T
+
         inputs[FIELDS * EMB : INPUT, :] = mm(
             dense_w[...], feats[:, here_tokens], precision=HI
         ).astype(BF)
@@ -966,6 +972,65 @@
         sum_gate[...] += mm(inputs[...], deltas[experts * HID :, :], NT)
         d_inputs[...] = mm(wide[...], deltas[...])
         sum_dense[...] += mm(feats[:, here_tokens], d_inputs[INPUT - LANES :, :], NT, HI)
+
+        @pl.when(step == chunks - 1)
+        def sums_ready():
+            for part in range(size.groups):
+                base = part * size.second
+                for expert in range(experts):
+                    grads[part, expert, : size.first, :] = sum_first[
+                        expert, part * size.first : (part + 1) * size.first, :
+                    ].astype(BF)
+                    grads[part, expert, size.first :, :LANES] = sum_second[
+                        expert, base : base + half, :
+                    ].astype(BF)
+                    grads[part, expert, size.first :, LANES:] = sum_second[
+                        expert, base + half : base + 2 * half, :
+                    ].astype(BF)
+            for step in range(1, chips + 1):
+                sums_c(step % chips).start()
+            for expert in range(experts):
+                per = HID // LANES
+                for piece in range(per):
+                    line = expert * per + piece
+                    small_part[line : line + 1, :] = sum_first[
+                        expert, INPUT : INPUT + 1, piece * LANES : (piece + 1) * LANES
+                    ]
+                line = experts * per + expert
+                small_part[line : line + 1, :] = sum_second[expert, HID : HID + 1, :]
+            for line in range(DENSE + 1):
+                values = jnp.where(lane < DOUT, turn(sum_dense[line : line + 1, :], DOUT - LANES), 0.0)
+                put(small_part, at_dense + line * DOUT, values)
+            lines = INPUT // per_line + 1
+            packed = jnp.zeros((lines, LANES), F32)
+            for spot in range(per_line):
+                packed = packed + turn(sum_gate[pl.ds(spot, lines, stride=per_line), :], spot * gates_wide)
+            inside = lax.broadcasted_iota(jnp.int32, (lines, LANES), 0) < lines - 1
+            put(
+                small_part,
+                at_gate,
+                jnp.where(inside | (lanes_of(lines) < gates_wide), packed, 0.0),
+            )
+            tower_rows[...] = jnp.zeros_like(tower_rows)
+            for task in range(TASKS):
+                base = task * (OUT + 1)
+                tower_rows[base : base + OUT + 1, :TOWER] = sum_tower[task, : OUT + 1, :]
+            put(
+                small_part,
+                at_tower,
+                tower_rows[pl.ds(0, count_rows, stride=2), :]
+                + turn(tower_rows[pl.ds(1, count_rows, stride=2), :], TOWER),
+            )
+            for task in range(TASKS):
+                put(
+                    small_part,
+                    at_head + task * (TOWER + 1),
+                    jnp.where(lane < TOWER + 1, sum_head[task, 0:1, :], 0.0),
+                )
+            whole_loss = jnp.sum(loss_sum[...], 1, keepdims=True)
+            put(small_part, at_loss, jnp.where(lane == 0, whole_loss, 0.0))
+            loop(1, devices, lambda step: give_small(step, False).start())
+
         slot_sum[...] = jnp.zeros_like(slot_sum)
 
         def give(field):
@@ -984,134 +1049,64 @@
 
     loop(0, chunks, chunk)
 
-    for part in range(size.groups):
-        base = part * size.second
-        for expert in range(experts):
-            grads[part, expert, : size.first, :] = sum_first[
-                expert, part * size.first : (part + 1) * size.first, :
-            ].astype(BF)
-            grads[part, expert, size.first :, :LANES] = sum_second[
-                expert, base : base + half, :
-            ].astype(BF)
-            grads[part, expert, size.first :, LANES:] = sum_second[
-                expert, base + half : base + 2 * half, :
-            ].astype(BF)
-    for step in range(1, chips + 1):
-        sums_c(step % chips).start()
-    for expert in range(experts):
-        per = HID // LANES
-        for piece in range(per):
-            line = expert * per + piece
-            small_part[line : line + 1, :] = sum_first[
-                expert, INPUT : INPUT + 1, piece * LANES : (piece + 1) * LANES
-            ]
-        line = experts * per + expert
-        small_part[line : line + 1, :] = sum_second[expert, HID : HID + 1, :]
-    for line in range(DENSE + 1):
-        values = jnp.where(lane < DOUT, turn(sum_dense[line : line + 1, :], DOUT - LANES), 0.0)
-        put(small_part, at_dense + line * DOUT, values)
-    lines = INPUT // per_line + 1
-    packed = jnp.zeros((lines, LANES), F32)
-    for spot in range(per_line):
-        packed = packed + turn(sum_gate[pl.ds(spot, lines, stride=per_line), :], spot * gates_wide)
-    inside = lax.broadcasted_iota(jnp.int32, (lines, LANES), 0) < lines - 1
-    put(
-        small_part,
-        at_gate,
-        jnp.where(inside | (lanes_of(lines) < gates_wide), packed, 0.0),
-    )
-    tower_rows[...] = jnp.zeros_like(tower_rows)
-    for task in range(TASKS):
-        base = task * (OUT + 1)
-        tower_rows[base : base + OUT + 1, :TOWER] = sum_tower[task, : OUT + 1, :]
-    put(
-        small_part,
-        at_tower,
-        tower_rows[pl.ds(0, count_rows, stride=2), :]
-        + turn(tower_rows[pl.ds(1, count_rows, stride=2), :], TOWER),
-    )
-    for task in range(TASKS):
-        put(
-            small_part,
-            at_head + task * (TOWER + 1),
-            jnp.where(lane < TOWER + 1, sum_head[task, 0:1, :], 0.0),
-        )
-    whole_loss = jnp.sum(loss_sum[...], 1, keepdims=True)
-    put(small_part, at_loss, jnp.where(lane == 0, whole_loss, 0.0))
-    loop(1, devices, lambda step: give_small(step, False).start())
-
     def collect(part):
         columns_here = pl.ds(part * LANES, LANES)
-
-        def some(turn_no, own):
+        wait(slot_landed.at[part], slots_got.at[part, others])
+
+        def some(turn_no):
             steps = [turn_no * batch + i for i in range(batch)]
             peers = [lax.rem(me + devices - step, devices) for step in steps]
-            for i, step in enumerate(steps):
-                if not (own and i == 0):
-                    give_slots(part, step, True).wait_recv()
             index = jnp.concatenate([asked[peer, :, columns_here] for peer in peers], 1)
             values = jnp.concatenate([slots_got[part, peer] for peer in peers], 1).astype(F32)
             spots = as_low(spread(index & (KEYS - 1), KEYS, batch * LANES))
             table_grad[...] += mm(levels_of(values, index >> 8, blocks), spots, NT)
 
-        some(0, True)
-        loop(1, devices // batch, lambda turn_no: some(turn_no, False), devices // batch - 1)
-
-    collect(0)
+        loop(0, devices // batch, some, devices // batch)
+
+    wait(sc_landed, core_got)
     for step in range(1, chips + 1):
         other = turned(chip, chips, step % chips, False)
-        sums_c(step % chips).wait_recv()
         core_sum[other] = (
             grads[other * 2 + core].astype(F32) + core_got[other].astype(F32)
         ).astype(BF)
         if step < chips:
             sums_y(step, False).start()
-    collect(1)
+    collect(0)
+    wait(small_landed, small_got.at[others])
     small_got[me] = small_part[own_lines(me), :]
-
-    def add_small(step, total):
-        give_small(step, True).wait_recv()
-        return total + small_got[lax.rem(me + devices - step, devices)]
-
-    small_sum[own_lines(me), :] = lax.fori_loop(1, devices, add_small, small_got[me])
+    small_sum[own_lines(me), :] = jnp.sum(small_got[...], 0)
     loop(1, devices, lambda step: give_whole(step, False).start())
-    collect(2)
+    for part in range(1, chunks - 1):
+        collect(part)
+    wait(sy_landed, chip_got.at[other_chips])
     total = core_sum[chip].astype(F32)
     for step in range(1, chips):
-        sums_y(step, True).wait_recv()
         total = total + chip_got[step].astype(F32)
     chip_sum[...] = total.astype(BF)
     for step in range(1, experts):
         sums_z(step, False).start()
-    for part in range(3, chunks):
-        collect(part)
+    collect(chunks - 1)
+    wait(sz_landed, z_got.at[other_experts])
     total = chip_sum[expert_here].astype(F32)
     for step in range(1, experts):
-        sums_z(step, True).wait_recv()
         total = total + z_got[step].astype(F32)
     first_grad[...] = total[: size.first]
     second_grad[:half, :] = total[size.first :, :LANES]
     second_grad[half:, :] = total[size.first :, LANES:]
 
-    def finish(step):
-        give_whole(step, True).wait_recv()
-        ask(step, False).wait_send()
-        for part in range(chunks):
-            answer(part, step, False).wait_send()
-            give_slots(part, step, False).wait_send()
-        give_small(step, False).wait_send()
-        give_whole(step, False).wait_send()
-
-    loop(1, devices, finish)
-    for step in range(chips):
-        weights_c(step, False).wait_send()
-        sums_c(step).wait_send()
-    for step in range(1, chips):
-        weights_y(step, False).wait_send()
-        sums_y(step, False).wait_send()
-    for step in range(1, experts):
-        weights_z(step, False).wait_send()
-        sums_z(step, False).wait_send()
+    other_lines = pl.ds(0, (devices - 1) * small_got.shape[1])
+    wait(whole_landed, small_sum.at[other_lines, :])
+    wait(whole_sent, small_sum.at[other_lines, :])
+    wait(small_sent, small_part.at[other_lines, :])
+    wait(ask_sent, message.at[others])
+    wait(row_sent, rows.at[:, others])
+    wait(slot_sent, slots_out.at[:, others])
+    wait(gz_sent, gathered.at[0, other_experts])
+    wait(gy_sent, gathered.at[other_chips])
+    wait(gc_sent, gathered.at[pl.ds(0, chips)])
+    wait(sc_sent, core_got)
+    wait(sy_sent, core_sum.at[other_chips])
+    wait(sz_sent, chip_sum.at[other_experts])
 
 
 def update(size, *refs):
@@ -1230,13 +1225,8 @@
             vm((TASKS, 8, LANES), F32),
             vm((1, CHUNK), F32),
         ]
-        + [dma((devices,))] * 2
-        + [dma((chunks, devices))] * 4
-        + [dma((devices,))] * 4
-        + [dma((experts,))] * 2
-        + [dma((chips,))] * 4
-        + [dma((experts,))] * 2
-        + [dma((chips,))] * 4,
+        + [dma, dma, dma, dma((chunks,)), dma, dma((chunks,))]
+        + [dma] * 16,
         0,
     )(
         requests[0],

time: 95.7 us -> 86.7 us (0.906)
  Pallas kernels: 91.9 us -> 82.9 us
    pallas_call x2, Pallas kernels: 91.9 us -> 82.9 us  [call(): pl.pallas_call(kernel, out_shape=outs, in_specs=[vmem] * len(args), out_s...]
where the time goes in v3:
time: 86.7 us; the launch traced here: 86.5 us
  Pallas kernels  82.9 us (96%)
  local copies, waits for them, and re-layouts  2.15 us (2%)
    pallas_call x2, Pallas kernels, call(): pl.pallas_call(kernel, out_shape=outs, in_specs=[vmem] * len(args), out_s...  82.9 us

profile of v3, /device:TPU:0, one launch (start us, length us, event | category | flops | bytes accessed | tf_op | source)
XLA Modules:
  0.0 86.5 jit_solution(10866038481619220611)
XLA Ops:
  0.6 1.5 %pad_bitcast_fusion.small = f32[185,128]{1,0:T(8,128)} fusion(f32[23626]{0:T(1024)} %param.31), kind=kLoop, calls=%fused_computation.4 | loop fusion | bytes 189224 | tf_op jit(solution)/shard_map/reshape | solution.py:1240
  2.2 80.4 %shard_map.264 = (f32[256,256]{1,0:T(8,128)}, f32[64,256]{1,0:T(8,128)}, f32[32,128]{1,0:T(8,128)}, f32[256,128]{1,0:T(8,128)}) custom-call(s32[8,4,512]{2,1,0:T(4,128)} %bitcast.38, s32[26,1024]{1,0:T(8,128)} %bitcast.33, f32[13,1024]{1,0:T(8,128)} %bitcast.39, s32[2,1024]{1,0:T(2,128)} %bitcast.44, s32[2,1024]{1,0:T(2,128)} %bitcast.45, ...), custom_call_target="tpu_custom_call" | custom-call | tf_op jit(solution)/shard_map/pallas_call | solution.py:1134
  82.6 0.0 copy-start
  82.6 0.0 copy-start.1
  82.6 0.0 copy-start.2
  82.6 0.0 copy-start.3
  82.6 2.5 %shard_map.265 = (f32[16,4096]{1,0:T(8,128)}, f32[16,4096]{1,0:T(8,128)}, f32[16,4096]{1,0:T(8,128)}, f32[64,256]{1,0:T(8,128)}, f32[64,256]{1,0:T(8,128)}, /*in...) custom-call(f32[256,256]{1,0:T(8,128)} %get-tuple-element.27.refs_0_, ...), custom_call_target="tpu_custom_call" | custom-call | tf_op jit(solution)/shard_map/pallas_call | solution.py:1134
  85.2 0.0 copy-done
  85.2 0.0 copy-done.1
  85.2 0.0 copy-done.2
  85.2 0.0 copy-done.3
  85.2 0.7 multiply_subtract_fusion
  86.0 0.6 slice.8
Async XLA Ops:
  82.6 2.6 %copy-start = (f32[23626]{0:T(1024)S(1)}, f32[23626]{0:T(1024)}, u32[]{:S(2)}) copy-start(f32[23626]{0:T(1024)} %param.31) | copy-start | bytes 283516
  82.6 2.6 %copy-start.1 = (f32[23626]{0:T(1024)S(1)}, f32[23626]{0:T(1024)}, u32[]{:S(2)}) copy-start(f32[23626]{0:T(1024)} %param.32) | copy-start | bytes 283516
  82.6 2.6 %copy-start.2 = (f32[23626]{0:T(1024)S(1)}, f32[23626]{0:T(1024)}, u32[]{:S(2)}) copy-start(f32[23626]{0:T(1024)} %param.33) | copy-start | bytes 283516
  82.6 2.6 %copy-start.3 = (f32[256,128]{1,0:T(8,128)S(1)}, f32[256,128]{1,0:T(8,128)}, u32[]{:S(2)}) copy-start(f32[256,128]{1,0:T(8,128)} %get-tuple-element.26) | copy-start | bytes 393220

commit v4 on v3

--- a/solution.py
+++ b/solution.py
@@ -544,6 +544,7 @@
     tower_t,
     dense_rows,
     dense_w,
+    dense_low,
     small_part,
     small_got,
     first_t,
@@ -551,17 +552,24 @@
     second_t,
     wide,
     feats,
-    slot_cells,
-    chosen,
-    inputs,
+    feats_low,
+    slot_cells_a,
+    slot_cells_b,
+    chosen_a,
+    chosen_b,
+    chosen_c,
+    inputs_a,
+    inputs_b,
     slope_one,
     slope_two,
     hidden,
     outs,
     mixes,
     deltas,
-    d_inputs,
-    slot_sum,
+    d_inputs_a,
+    d_inputs_b,
+    slot_sum_a,
+    slot_sum_b,
     sum_first,
     sum_second,
     sum_gate,
@@ -605,6 +613,11 @@
     at_one, at_two, at_dense, at_gate, at_tower, at_head, at_loss = offsets(experts)
     lane = lanes_of()
     barrier = greet(size, me)
+    slot_cells = (slot_cells_a, slot_cells_b)
+    chosen = (chosen_a, chosen_b, chosen_c)
+    inputs = (inputs_a, inputs_b)
+    d_inputs = (d_inputs_a, d_inputs_b)
+    slot_sum = (slot_sum_a, slot_sum_b)
 
     def own_lines(device):
         count = small_got.shape[1]
@@ -668,21 +681,21 @@
     def turned(index, count, step, receive):
         return lax.rem(index + (count - step if receive else step), count)
 
-    def weights_z(step, receive):
-        other = turned(expert_here, experts, step, receive)
-        block = gathered.at[group, other if receive else expert_here]
-        return push(block, block, gz_sent, gz_landed, (group, other))
-
-    def weights_y(step, receive):
-        other = turned(chip, chips, step, receive)
-        block = gathered.at[(other if receive else chip) * 2 + core]
+    def weights_z(step):
+        other = turned(expert_here, experts, step, False)
+        block = gathered.at[group, expert_here]
+        return push(block, block, gz_sent, gz_landed.at[step], (group, other))
+
+    def weights_y(step, source):
+        other = turned(chip, chips, step, False)
+        block = gathered.at[group, source]
         return push(
             block, block, gy_sent, gy_landed, (other * 2 + core, expert_here)
         )
 
-    def weights_c(step, receive):
+    def weights_c(step):
         other = turned(chip, chips, step, True)
-        block = gathered.at[other * 2 + (1 - core if receive else core)]
+        block = gathered.at[other * 2 + core]
         return push(
             block, block, gc_sent, gc_landed, (chip * 2 + 1 - core, expert_here)
         )
@@ -750,9 +763,11 @@
             :, block * KEYS : (block + 1) * KEYS
         ].astype(BF)
     pl.semaphore_wait(barrier, devices - 1)
+    for step in range(1, experts):
+        weights_z(step).start()
+    for step in range(1, chips):
+        weights_y(step, expert_here).start()
     loop(1, devices, lambda step: ask(step, False).start())
-    for step in range(1, experts):
-        weights_z(step, False).start()
 
     vectors[...] = jnp.zeros_like(vectors)
     vectors[: at_dense // LANES, :] = small[: at_dense // LANES, :]
@@ -792,23 +807,18 @@
         columns[column] = jnp.broadcast_to(flipped[:, column : column + 1], (LANES, LANES))
     feats[...] = jnp.ones_like(feats)
     feats[:DENSE, :] = dense[...]
-    inputs[INPUT:, :] = jnp.ones((ONES, CHUNK), BF)
+    upper = feats[...].astype(BF)
+    feats_low[:16, :] = upper
+    feats_low[16:, :] = (feats[...] - upper.astype(F32)).astype(BF)
+    dense_low[...] = mm(dense_w[...], feats[...], precision=HI).astype(BF)
+    for buffer in inputs:
+        buffer[INPUT:, :] = jnp.ones((ONES, CHUNK), BF)
     for expert in range(experts):
         hidden[expert, HID:, :] = jnp.ones((ONES, CHUNK), BF)
     for task in range(TASKS):
         mixes[task, OUT:, :] = jnp.ones((ONES, CHUNK), BF)
     deltas[experts * HID :, :] = jnp.zeros((LANES, CHUNK), BF)
-    for total in (
-        sum_first,
-        sum_second,
-        sum_gate,
-        sum_dense,
-        sum_tower,
-        sum_head,
-        loss_sum,
-        small_part,
-        table_grad,
-    ):
+    for total in (sum_gate, loss_sum, small_part, table_grad):
         total[...] = jnp.zeros_like(total)
 
     asked[me] = message[me]
@@ -834,72 +844,97 @@
         loop(1, devices // batch, lambda turn_no: some(turn_no, False), devices // batch - 1)
 
     wait(ask_landed, asked.at[others])
+    for step in range(1, experts):
+        source = turned(expert_here, experts, step, True)
+        wait(gz_landed.at[step], gathered.at[group, source])
+        for hop in range(1, chips):
+            weights_y(hop, source).start()
+    weights_c(0).start()
     serve(0)
-    wait(gz_landed, gathered.at[0, other_experts])
-    for step in range(1, chips):
-        weights_y(step, False).start()
-    weights_c(0, False).start()
     total = jnp.zeros((1, LANES), jnp.int32)
     for peer in range(devices):
         total = total + asked[peer, :, slots:]
     totals = jnp.maximum(total.astype(F32), 1.0)
-    for part in range(1, chunks):
+    for part in range(1, chunks - 1):
         serve(part)
-        if part == chunks - 2:
-            wait(gy_landed, gathered.at[other_chips])
-            for step in range(1, chips):
-                weights_c(step, False).start()
+    wait(gy_landed, gathered.at[other_chips])
+    for step in range(1, chips):
+        weights_c(step).start()
+    serve(chunks - 1)
 
     def column(index, begin=0, end=LANES):
         block = columns[index, begin:end, :]
         return jnp.concatenate([block] * (CHUNK // LANES), 1)
 
-    def chunk(step):
-        here_tokens = pl.ds(pl.multiple_of(step * CHUNK, CHUNK), CHUNK)
-        wait(row_landed.at[step], got.at[step, others])
+    def tokens_of(part):
+        return slice(part * CHUNK, (part + 1) * CHUNK)
+
+    def split(part, field):
+        index = picks[field : field + 1, tokens_of(part)]
+        owner = index >> shift
+        return (owner & 1) * LANES + (index & (LANES - 1)), owner >> 1
+
+    def fetch(part):
+        wait(row_landed.at[part], got.at[part, others])
         for owner in range(devices):
             level, lower = owner // 2, owner % 2
-            slot_cells[
+            slot_cells[part % 2][
                 level * EMB : (level + 1) * EMB, lower * LANES : (lower + 1) * LANES
-            ] = got[step, owner]
-
-        def split(field):
-            index = picks[pl.ds(field, 1), here_tokens]
-            owner = index >> shift
-            return (owner & 1) * LANES + (index & (LANES - 1)), owner >> 1
-
-        def pick(field):
-            key, high = split(field)
-            flags = as_low(spread(key, KEYS, CHUNK))
-            chosen[field] = flags
-            found = mm(slot_cells[...], flags)
-            result = found[:EMB]
-            for level in range(1, levels):
-                result = jnp.where(high == level, found[level * EMB : (level + 1) * EMB], result)
-            inputs[pl.ds(pl.multiple_of(field * EMB, EMB), EMB), :] = result.astype(BF)
-
-        loop(0, FIELDS, pick, 13)
-
-        @pl.when(step == 0)
-        def weights_ready():
-            wait(gc_landed, gathered.at[pl.ds(0, chips)])
-            for expert in range(experts):
-                for part in range(size.groups):
-                    wide[
-                        part * size.first : (part + 1) * size.first, expert * HID : (expert + 1) * HID
-                    ] = gathered[part, expert, : size.first, :]
-                    base = part * size.second
-                    second_n[expert, base : base + half, :] = gathered[part, expert, size.first :, :LANES]
-                    second_n[expert, base + half : base + 2 * half, :] = gathered[
-                        part, expert, size.first :, LANES:
-                    ]
-                first_t[expert] = wide[:, expert * HID : (expert + 1) * HID].T
-                second_t[expert] = second_n[expert].T
-
-        inputs[FIELDS * EMB : INPUT, :] = mm(
-            dense_w[...], feats[:, here_tokens], precision=HI
-        ).astype(BF)
-        x = inputs[:INPUT, :]
+            ] = got[part, owner]
+        inputs[part % 2][FIELDS * EMB : INPUT, :] = dense_low[:, tokens_of(part)]
+
+    def pick(part, field):
+        key, high = split(part, field)
+        flags = as_low(spread(key, KEYS, CHUNK))
+        chosen[part % 3][field] = flags
+        found = mm(slot_cells[part % 2][...], flags)
+        result = found[:EMB]
+        for level in range(1, levels):
+            result = jnp.where(high == level, found[level * EMB : (level + 1) * EMB], result)
+        inputs[part % 2][field * EMB : (field + 1) * EMB, :] = result.astype(BF)
+
+    def give(part, field, first_time):
+        places, flags = [], []
+        for one in (field, field + 1):
+            key, high = split(part, one)
+            values = d_inputs[part % 2][one * EMB : (one + 1) * EMB, :]
+            places.append(levels_of(values, high, levels))
+            flags.append(chosen[part % 3][one])
+        sums = mm(jnp.concatenate(places, 1), jnp.concatenate(flags, 1), NT)
+        if first_time:
+            slot_sum[part % 2][...] = sums
+        else:
+            slot_sum[part % 2][...] += sums
+
+    def picks_of(part):
+        return [functools.partial(pick, part, field) for field in range(FIELDS)]
+
+    def gives_of(part):
+        return [
+            functools.partial(give, part, field, field == 0) for field in range(0, FIELDS, 2)
+        ]
+
+    def send_slots(part):
+        for owner in range(devices):
+            level, lower = owner // 2, owner % 2
+            slots_out[part, owner] = slot_sum[part % 2][
+                level * EMB : (level + 1) * EMB, lower * LANES : (lower + 1) * LANES
+            ].astype(BF)
+        loop(1, devices, lambda hop: give_slots(part, hop, False).start())
+        slots_got[part, me] = slots_out[part, me]
+
+    def train(part):
+        here_tokens = tokens_of(part)
+        first_time = part == 0
+        whole_x = inputs[part % 2]
+
+        def add(total, value):
+            if first_time:
+                total[...] = value
+            else:
+                total[...] += value
+
+        x = whole_x[:INPUT, :]
         logits = mm(gate_t[...], x)[:gates_wide] + column(14, 0, gates_wide)
         probs, gates = [], []
         for task in range(TASKS):
@@ -909,6 +944,7 @@
             whole = 1.0 / functools.reduce(jnp.add, powers)
             probs.append([item * whole for item in powers])
             gates.append([item.astype(BF).astype(F32) for item in probs[-1]])
+        yield
         mixed = [None] * TASKS
         for expert in range(experts):
             pre = mm(first_t[expert], x) + jnp.concatenate(
@@ -917,8 +953,10 @@
             sig = sigmoid(pre)
             act = pre * sig
             slope_one[expert] = sig + act * (1.0 - sig)
-            hidden[expert, :HID, :] = act.astype(BF)
-            pre = mm(second_t[expert], hidden[expert, :HID, :]) + column(8 + expert)
+            low = act.astype(BF)
+            hidden[expert, :HID, :] = low
+            yield
+            pre = mm(second_t[expert], low) + column(8 + expert)
             sig = sigmoid(pre)
             act = pre * sig
             slope_two[expert] = sig + act * (1.0 - sig)
@@ -926,11 +964,13 @@
             for task in range(TASKS):
                 term = gates[task][expert] * act
                 mixed[task] = term if mixed[task] is None else mixed[task] + term
+            yield
         d_mixed = []
         for task in range(TASKS):
-            mixes[task, :OUT, :] = mixed[task].astype(BF)
+            mix = mixed[task].astype(BF)
+            mixes[task, :OUT, :] = mix
             low, high = task * TOWER, (task + 1) * TOWER
-            pre = mm(tower_t[task], mixes[task, :OUT, :]) + column(12, low, high)
+            pre = mm(tower_t[task], mix) + column(12, low, high)
             sig = sigmoid(pre)
             act = pre * sig
             head = column(13, low, high)
@@ -940,27 +980,41 @@
             soft = jnp.maximum(logit, 0.0) + jnp.log(1.0 + jnp.exp(-jnp.abs(logit)))
             loss_sum[...] += scale * (soft - target * logit)
             d_logit = scale * (sigmoid(logit) - target)
+            yield
             d_pre = ((sig + act * (1.0 - sig)) * (d_logit * head)).astype(BF)
-            sum_head[task] += mm(
-                jnp.broadcast_to(d_logit, (8, CHUNK)),
-                jnp.concatenate(
-                    [act, jnp.ones((8, CHUNK), F32), jnp.zeros((LANES - TOWER - 8, CHUNK), F32)], 0
-                ),
-                NT,
-                HI,
+            d_upper = d_logit.astype(BF).astype(F32)
+            d_both = jnp.concatenate(
+                [
+                    jnp.broadcast_to(d_upper, (8, CHUNK)),
+                    jnp.broadcast_to(d_logit - d_upper, (8, CHUNK)),
+                ],
+                0,
+            ).astype(BF)
+            upper = act.astype(BF)
+            rest = (act - upper.astype(F32)).astype(BF)
+            ones = jnp.ones((16, CHUNK), BF)
+            zeros = jnp.zeros((LANES - TOWER - 16, CHUNK), BF)
+            both = mm(d_both, jnp.concatenate([upper, ones, zeros], 0), NT) + mm(
+                d_both, jnp.concatenate([rest, zeros, jnp.zeros((16, CHUNK), BF)], 0), NT
             )
-            sum_tower[task] += mm(mixes[task], d_pre, NT)
+            add(sum_head.at[task], both[:8] + both[8:])
+            add(sum_tower.at[task], mm(mixes[task], d_pre, NT))
             d_mixed.append(mm(tower_n[task], d_pre).astype(BF).astype(F32))
+            yield
         d_gates = [[None] * experts for task in range(TASKS)]
         for expert in range(experts):
             d_out = gates[0][expert] * d_mixed[0] + gates[1][expert] * d_mixed[1]
+            out = outs[expert]
             for task in range(TASKS):
-                d_gates[task][expert] = jnp.sum(outs[expert] * d_mixed[task], 0, keepdims=True)
+                d_gates[task][expert] = jnp.sum(out * d_mixed[task], 0, keepdims=True)
             d_two = (slope_two[expert] * d_out).astype(BF)
-            sum_second[expert] += mm(hidden[expert], d_two, NT)
-            d_one = (slope_one[expert] * mm(second_n[expert], d_two)).astype(BF)
+            d_hidden = mm(second_n[expert], d_two)
+            add(sum_second.at[expert], mm(hidden[expert], d_two, NT))
+            yield
+            d_one = (slope_one[expert] * d_hidden).astype(BF)
             deltas[expert * HID : (expert + 1) * HID, :] = d_one
-            sum_first[expert] += mm(inputs[...], d_one, NT)
+            add(sum_first.at[expert], mm(whole_x[...], d_one, NT))
+            yield
         lines = []
         for task in range(TASKS):
             inner = functools.reduce(
@@ -968,86 +1022,127 @@
             )
             lines += [probs[task][e] * (d_gates[task][e] - inner) for e in range(experts)]
         lines.append(jnp.zeros((16 - gates_wide, CHUNK), F32))
-        deltas[experts * HID : experts * HID + 16, :] = jnp.concatenate(lines, 0).astype(BF)
-        sum_gate[...] += mm(inputs[...], deltas[experts * HID :, :], NT)
-        d_inputs[...] = mm(wide[...], deltas[...])
-        sum_dense[...] += mm(feats[:, here_tokens], d_inputs[INPUT - LANES :, :], NT, HI)
-
-        @pl.when(step == chunks - 1)
-        def sums_ready():
-            for part in range(size.groups):
-                base = part * size.second
-                for expert in range(experts):
-                    grads[part, expert, : size.first, :] = sum_first[
-                        expert, part * size.first : (part + 1) * size.first, :
-                    ].astype(BF)
-                    grads[part, expert, size.first :, :LANES] = sum_second[
-                        expert, base : base + half, :
-                    ].astype(BF)
-                    grads[part, expert, size.first :, LANES:] = sum_second[
-                        expert, base + half : base + 2 * half, :
-                    ].astype(BF)
-            for step in range(1, chips + 1):
-                sums_c(step % chips).start()
-            for expert in range(experts):
-                per = HID // LANES
-                for piece in range(per):
-                    line = expert * per + piece
-                    small_part[line : line + 1, :] = sum_first[
-                        expert, INPUT : INPUT + 1, piece * LANES : (piece + 1) * LANES
-                    ]
-                line = experts * per + expert
-                small_part[line : line + 1, :] = sum_second[expert, HID : HID + 1, :]
-            for line in range(DENSE + 1):
-                values = jnp.where(lane < DOUT, turn(sum_dense[line : line + 1, :], DOUT - LANES), 0.0)
-                put(small_part, at_dense + line * DOUT, values)
-            lines = INPUT // per_line + 1
-            packed = jnp.zeros((lines, LANES), F32)
-            for spot in range(per_line):
-                packed = packed + turn(sum_gate[pl.ds(spot, lines, stride=per_line), :], spot * gates_wide)
-            inside = lax.broadcasted_iota(jnp.int32, (lines, LANES), 0) < lines - 1
-            put(
-                small_part,
-                at_gate,
-                jnp.where(inside | (lanes_of(lines) < gates_wide), packed, 0.0),
-            )
-            tower_rows[...] = jnp.zeros_like(tower_rows)
-            for task in range(TASKS):
-                base = task * (OUT + 1)
-                tower_rows[base : base + OUT + 1, :TOWER] = sum_tower[task, : OUT + 1, :]
-            put(
-                small_part,
-                at_tower,
-                tower_rows[pl.ds(0, count_rows, stride=2), :]
-                + turn(tower_rows[pl.ds(1, count_rows, stride=2), :], TOWER),
-            )
-            for task in range(TASKS):
-                put(
-                    small_part,
-                    at_head + task * (TOWER + 1),
-                    jnp.where(lane < TOWER + 1, sum_head[task, 0:1, :], 0.0),
-                )
-            whole_loss = jnp.sum(loss_sum[...], 1, keepdims=True)
-            put(small_part, at_loss, jnp.where(lane == 0, whole_loss, 0.0))
-            loop(1, devices, lambda step: give_small(step, False).start())
-
-        slot_sum[...] = jnp.zeros_like(slot_sum)
-
-        def give(field):
-            key, high = split(field)
-            values = d_inputs[pl.ds(pl.multiple_of(field * EMB, EMB), EMB), :]
-            slot_sum[...] += mm(levels_of(values, high, levels), chosen[field], NT)
-
-        loop(0, FIELDS, give, 13)
-        for owner in range(devices):
-            level, lower = owner // 2, owner % 2
-            slots_out[step, owner] = slot_sum[
-                level * EMB : (level + 1) * EMB, lower * LANES : (lower + 1) * LANES
+        d_gate = jnp.concatenate(lines, 0).astype(BF)
+        deltas[experts * HID : experts * HID + 16, :] = d_gate
+        add(sum_gate.at[:, : INPUT + ONES], mm(d_gate, whole_x[...], NT))
+        yield
+        d_x = mm(wide[...], deltas[...])
+        d_inputs[part % 2][...] = d_x
+        d_dense = d_x[INPUT - LANES :, :]
+        upper = d_dense.astype(BF)
+        rest = (d_dense - upper.astype(F32)).astype(BF)
+        both = mm(feats_low[:, here_tokens], upper, NT)
+        add(sum_dense, both[:16] + both[16:] + mm(feats_low[:16, here_tokens], rest, NT))
+        yield
+
+    stops = 2 + 2 * experts + 2 * TASKS + 2 * experts + 1
+
+    def beside(main, jobs):
+        jobs, done = list(jobs), 0
+        for stop, _ in enumerate(main):
+            until = len(jobs) * (stop + 1) // stops
+            for job in jobs[done:until]:
+                job()
+            done = until
+        for job in jobs[done:]:
+            job()
+
+    def mixed_jobs(*lists):
+        spots = [
+            ((index + 0.5) / len(jobs), job) for jobs in lists for index, job in enumerate(jobs)
+        ]
+        return [job for spot, job in sorted(spots, key=lambda pair: pair[0])]
+
+    fetch(0)
+    for job in picks_of(0):
+        job()
+    wait(gc_landed, gathered.at[pl.ds(0, chips)])
+    for expert in range(experts):
+        for part in range(size.groups):
+            wide[
+                part * size.first : (part + 1) * size.first, expert * HID : (expert + 1) * HID
+            ] = gathered[part, expert, : size.first, :]
+            base = part * size.second
+            second_n[expert, base : base + half, :] = gathered[part, expert, size.first :, :LANES]
+            second_n[expert, base + half : base + 2 * half, :] = gathered[
+                part, expert, size.first :, LANES:
+            ]
+        first_t[expert] = wide[:, expert * HID : (expert + 1) * HID].T
+        second_t[expert] = second_n[expert].T
+    for part in range(chunks):
+        jobs = []
+        if part + 1 < chunks:
+            fetch(part + 1)
+            jobs.append(picks_of(part + 1))
+        if part > 0:
+            jobs.append(gives_of(part - 1))
+        beside(train(part), mixed_jobs(*jobs))
+        if part > 0:
+            send_slots(part - 1)
+
+    for part in range(size.groups):
+        base = part * size.second
+        for expert in range(experts):
+            grads[part, expert, : size.first, :] = sum_first[
+                expert, part * size.first : (part + 1) * size.first, :
             ].astype(BF)
-        loop(1, devices, lambda hop: give_slots(step, hop, False).start())
-        slots_got[step, me] = slots_out[step, me]
-
-    loop(0, chunks, chunk)
+            grads[part, expert, size.first :, :LANES] = sum_second[
+                expert, base : base + half, :
+            ].astype(BF)
+            grads[part, expert, size.first :, LANES:] = sum_second[
+                expert, base + half : base + 2 * half, :
+            ].astype(BF)
+    for step in range(1, chips + 1):
+        sums_c(step % chips).start()
+    for expert in range(experts):
+        per = HID // LANES
+        for piece in range(per):
+            line = expert * per + piece
+            small_part[line : line + 1, :] = sum_first[
+                expert, INPUT : INPUT + 1, piece * LANES : (piece + 1) * LANES
+            ]
+        line = experts * per + expert
+        small_part[line : line + 1, :] = sum_second[expert, HID : HID + 1, :]
+    for line in range(DENSE + 1):
+        values = jnp.where(lane < DOUT, turn(sum_dense[line : line + 1, :], DOUT - LANES), 0.0)
+        put(small_part, at_dense + line * DOUT, values)
+    fill = jnp.zeros((LANES - 16, LANES), F32)
+    for block in range(INPUT // LANES):
+        piece = jnp.concatenate([sum_gate[:, block * LANES : (block + 1) * LANES], fill], 0)
+        gate_rows[block * LANES : (block + 1) * LANES, :] = piece.T
+    gate_rows[INPUT:, :] = jnp.concatenate([sum_gate[:, INPUT:], fill], 0).T[:ONES]
+    lines = INPUT // per_line + 1
+    packed = jnp.zeros((lines, LANES), F32)
+    for spot in range(per_line):
+        packed = packed + turn(gate_rows[pl.ds(spot, lines, stride=per_line), :], spot * gates_wide)
+    inside = lax.broadcasted_iota(jnp.int32, (lines, LANES), 0) < lines - 1
+    put(
+        small_part,
+        at_gate,
+        jnp.where(inside | (lanes_of(lines) < gates_wide), packed, 0.0),
+    )
+    tower_rows[...] = jnp.zeros_like(tower_rows)
+    for task in range(TASKS):
+        base = task * (OUT + 1)
+        tower_rows[base : base + OUT + 1, :TOWER] = sum_tower[task, : OUT + 1, :]
+    put(
+        small_part,
+        at_tower,
+        tower_rows[pl.ds(0, count_rows, stride=2), :]
+        + turn(tower_rows[pl.ds(1, count_rows, stride=2), :], TOWER),
+    )
+    for task in range(TASKS):
+        put(
+            small_part,
+            at_head + task * (TOWER + 1),
+            jnp.where(lane < TOWER + 1, sum_head[task, 0:1, :], 0.0),
+        )
+    whole_loss = jnp.sum(loss_sum[...], 1, keepdims=True)
+    put(small_part, at_loss, jnp.where(lane == 0, whole_loss, 0.0))
+    loop(1, devices, lambda step: give_small(step, False).start())
+    for job in gives_of(chunks - 1):
+        job()
+    send_slots(chunks - 1)
 
     def collect(part):
         columns_here = pl.ds(part * LANES, LANES)
@@ -1199,6 +1294,7 @@
             vm((TASKS, TOWER, OUT), BF),
             vm((LANES, LANES), F32),
             vm((DOUT, 16), F32),
+            vm((DOUT, size.tokens), BF),
             vm((devices * lines, LANES), F32),
             vm((devices, lines, LANES), F32),
             vm((experts, HID, INPUT), BF),
@@ -1206,8 +1302,13 @@
             vm((experts, OUT, HID), BF),
             vm((INPUT, experts * HID + LANES), BF),
             vm((16, size.tokens), F32),
+            vm((32, size.tokens), BF),
+            vm((devices // 2 * EMB, KEYS), BF),
             vm((devices // 2 * EMB, KEYS), BF),
             vm((FIELDS, KEYS, CHUNK), BF),
+            vm((FIELDS, KEYS, CHUNK), BF),
+            vm((FIELDS, KEYS, CHUNK), BF),
+            vm((INPUT + ONES, CHUNK), BF),
             vm((INPUT + ONES, CHUNK), BF),
             vm((experts, HID, CHUNK), F32),
             vm((experts, OUT, CHUNK), F32),
@@ -1216,17 +1317,21 @@
             vm((TASKS, OUT + ONES, CHUNK), BF),
             vm((experts * HID + LANES, CHUNK), BF),
             vm((INPUT, CHUNK), F32),
+            vm((INPUT, CHUNK), F32),
+            vm((devices // 2 * EMB, KEYS), F32),
             vm((devices // 2 * EMB, KEYS), F32),
             vm((experts, INPUT + ONES, HID), F32),
             vm((experts, HID + ONES, OUT), F32),
-            vm((INPUT + ONES, LANES), F32),
+            vm((16, INPUT + LANES), F32),
             vm((16, LANES), F32),
             vm((TASKS, OUT + ONES, TOWER), F32),
             vm((TASKS, 8, LANES), F32),
             vm((1, CHUNK), F32),
         ]
         + [dma, dma, dma, dma((chunks,)), dma, dma((chunks,))]
-        + [dma] * 16,
+        + [dma] * 5
+        + [dma((experts,))]
+        + [dma] * 10,
         0,
     )(
         requests[0],

time: 86.7 us -> 78 us (0.90)
  Pallas kernels: 82.9 us -> 74.2 us
    pallas_call x2, Pallas kernels: 82.9 us -> 74.2 us  [call(): pl.pallas_call(kernel, out_shape=outs, in_specs=[vmem] * len(args), out_s...]
where the time goes in v4:
time: 78 us; the launch traced here: 77.8 us
  Pallas kernels  74.2 us (95%)
  local copies, waits for them, and re-layouts  2.15 us (3%)
    pallas_call x2, Pallas kernels, call(): pl.pallas_call(kernel, out_shape=outs, in_specs=[vmem] * len(args), out_s...  74.2 us

profile of v4, /device:TPU:0, one launch (start us, length us, event | category | flops | bytes accessed | tf_op | source)
XLA Modules:
  0.0 77.8 jit_solution(14291968388351807664)
XLA Ops:
  0.6 1.5 %pad_bitcast_fusion.small = f32[185,128]{1,0:T(8,128)} fusion(f32[23626]{0:T(1024)} %param.31), kind=kLoop, calls=%fused_computation.4 | loop fusion | bytes 189224 | tf_op jit(solution)/shard_map/reshape | solution.py:1345
  2.2 71.7 %shard_map.264 = (f32[256,256]{1,0:T(8,128)}, f32[64,256]{1,0:T(8,128)}, f32[32,128]{1,0:T(8,128)}, f32[256,128]{1,0:T(8,128)}) custom-call(s32[8,4,512]{2,1,0:T(4,128)} %bitcast.38, s32[26,1024]{1,0:T(8,128)} %bitcast.33, f32[13,1024]{1,0:T(8,128)} %bitcast.39, s32[2,1024]{1,0:T(2,128)} %bitcast.44, s32[2,1024]{1,0:T(2,128)} %bitcast.45, ...), custom_call_target="tpu_custom_call" | custom-call | tf_op jit(solution)/shard_map/pallas_call | solution.py:1229
  73.9 0.0 copy-start
  73.9 0.0 copy-start.1
  73.9 0.0 copy-start.2
  73.9 0.0 copy-start.3
  73.9 2.5 %shard_map.265 = (f32[16,4096]{1,0:T(8,128)}, f32[16,4096]{1,0:T(8,128)}, f32[16,4096]{1,0:T(8,128)}, f32[64,256]{1,0:T(8,128)}, f32[64,256]{1,0:T(8,128)}, /*in...) custom-call(f32[256,256]{1,0:T(8,128)} %get-tuple-element.27.refs_0_, ...), custom_call_target="tpu_custom_call" | custom-call | tf_op jit(solution)/shard_map/pallas_call | solution.py:1229
  76.5 0.0 copy-done
  76.5 0.0 copy-done.1
  76.5 0.0 copy-done.2
  76.5 0.0 copy-done.3
  76.5 0.7 multiply_subtract_fusion
  77.3 0.6 slice.8
Async XLA Ops:
  73.9 2.6 %copy-start = (f32[23626]{0:T(1024)S(1)}, f32[23626]{0:T(1024)}, u32[]{:S(2)}) copy-start(f32[23626]{0:T(1024)} %param.31) | copy-start | bytes 283516
  73.9 2.6 %copy-start.1 = (f32[23626]{0:T(1024)S(1)}, f32[23626]{0:T(1024)}, u32[]{:S(2)}) copy-start(f32[23626]{0:T(1024)} %param.32) | copy-start | bytes 283516
  73.9 2.6 %copy-start.2 = (f32[23626]{0:T(1024)S(1)}, f32[23626]{0:T(1024)}, u32[]{:S(2)}) copy-start(f32[23626]{0:T(1024)} %param.33) | copy-start | bytes 283516
  73.9 2.6 %copy-start.3 = (f32[256,128]{1,0:T(8,128)S(1)}, f32[256,128]{1,0:T(8,128)}, u32[]{:S(2)}) copy-start(f32[256,128]{1,0:T(8,128)} %get-tuple-element.26) | copy-start | bytes 393220

commit v5 on v4

--- a/solution.py
+++ b/solution.py
@@ -393,7 +393,7 @@
         and size.span == CHUNK
         and size.second % 32 == 0
         and size.first % 16 == 0
-        and size.groups % 2 == 0
+        and size.groups == 8
         and size.devices % 2 == 0
         and size.rows % KEYS == 0
         and size.experts == 4
@@ -590,7 +590,9 @@
     gz_sent,
     gz_landed,
     gy_sent,
+    gx_landed,
     gy_landed,
+    gd_landed,
     gc_sent,
     gc_landed,
     sz_sent,
@@ -681,53 +683,75 @@
     def turned(index, count, step, receive):
         return lax.rem(index + (count - step if receive else step), count)
 
+    def source_at(step):
+        return turned(expert_here, experts, step, True)
+
     def weights_z(step):
         other = turned(expert_here, experts, step, False)
         block = gathered.at[group, expert_here]
         return push(block, block, gz_sent, gz_landed.at[step], (group, other))
 
-    def weights_y(step, source):
-        other = turned(chip, chips, step, False)
-        block = gathered.at[group, source]
-        return push(
-            block, block, gy_sent, gy_landed, (other * 2 + core, expert_here)
-        )
-
-    def weights_c(step):
-        other = turned(chip, chips, step, True)
-        block = gathered.at[other * 2 + core]
+    beside_x = chip + 1 - 2 * lax.rem(chip, 2)
+    beside_y = lax.rem(chip + 2, 4)
+    across_both = lax.rem(beside_x + 2, 4)
+
+    def weights_x(step, owner):
+        block = gathered.at[owner * 2 + core, source_at(step)]
+        landed = (gx_landed if owner is chip else gd_landed).at[step]
+        return push(block, block, gy_sent, landed, (beside_x * 2 + core, expert_here))
+
+    def weights_y(step, owner):
+        block = gathered.at[owner * 2 + core, source_at(step)]
+        landed = (gy_landed if owner is chip else gd_landed).at[step]
+        return push(block, block, gy_sent, landed, (beside_y * 2 + core, expert_here))
+
+    def spread_weights(step):
+        weights_x(step, chip).start()
+        weights_y(step, chip).start()
+
+    def forward_weights(step):
+        wait(gx_landed.at[step], gathered.at[0, 0])
+        wait(gy_landed.at[step], gathered.at[0, 0])
+        if step % 2 == 0:
+            weights_y(step, beside_x).start()
+        else:
+            weights_x(step, beside_y).start()
+
+    def weights_c(owner):
+        block = gathered.at[owner * 2 + core]
         return push(
             block, block, gc_sent, gc_landed, (chip * 2 + 1 - core, expert_here)
         )
 
-    def sums_c(step):
+    def expert_at(turn_no):
+        return turned(expert_here, experts, turn_no + 1, False)
+
+    def sums_c(turn_no, step):
+        expert = expert_at(turn_no)
         other = turned(chip, chips, step, False)
         return push(
-            grads.at[other * 2 + 1 - core],
-            core_got.at[other],
+            grads.at[other * 2 + 1 - core, expert],
+            core_got.at[expert, other],
             sc_sent,
-            sc_landed,
+            sc_landed.at[turn_no],
             (chip * 2 + 1 - core, expert_here),
         )
 
-    def sums_y(step, receive):
-        other = turned(chip, chips, step, receive)
+    def sums_y(turn_no, step):
+        expert = expert_at(turn_no)
+        other = turned(chip, chips, step, False)
         return push(
-            core_sum.at[other],
-            chip_got.at[step],
+            core_sum.at[expert, other],
+            chip_got.at[expert, step],
             sy_sent,
-            sy_landed,
+            sy_landed.at[turn_no],
             (other * 2 + core, expert_here),
         )
 
-    def sums_z(step, receive):
-        other = turned(expert_here, experts, step, receive)
+    def sums_z(turn_no):
+        expert = expert_at(turn_no)
         return push(
-            chip_sum.at[other],
-            z_got.at[step],
-            sz_sent,
-            sz_landed,
-            (group, other),
+            chip_sum.at[expert], z_got.at[turn_no], sz_sent, sz_landed, (group, expert)
         )
 
     def wait(semaphore, block):
@@ -765,8 +789,7 @@
     pl.semaphore_wait(barrier, devices - 1)
     for step in range(1, experts):
         weights_z(step).start()
-    for step in range(1, chips):
-        weights_y(step, expert_here).start()
+    spread_weights(0)
     loop(1, devices, lambda step: ask(step, False).start())
 
     vectors[...] = jnp.zeros_like(vectors)
@@ -838,29 +861,39 @@
                     got[part, peer] = piece
                 else:
                     rows[part, peer] = piece
-                    answer(part, steps[i], False).start()
+                    if part == 0:
+                        answer(part, steps[i], False).start()
 
         some(0, True)
         loop(1, devices // batch, lambda turn_no: some(turn_no, False), devices // batch - 1)
 
+    def send_rows(part):
+        loop(1, devices, lambda step: answer(part, step, False).start())
+
+    forward_weights(0)
     wait(ask_landed, asked.at[others])
     for step in range(1, experts):
-        source = turned(expert_here, experts, step, True)
-        wait(gz_landed.at[step], gathered.at[group, source])
-        for hop in range(1, chips):
-            weights_y(hop, source).start()
-    weights_c(0).start()
-    serve(0)
+        wait(gz_landed.at[step], gathered.at[0, 0])
+        spread_weights(step)
+    weights_c(chip).start()
     total = jnp.zeros((1, LANES), jnp.int32)
     for peer in range(devices):
         total = total + asked[peer, :, slots:]
     totals = jnp.maximum(total.astype(F32), 1.0)
-    for part in range(1, chunks - 1):
+    serve(0)
+    serve(1)
+    for step in range(1, experts):
+        forward_weights(step)
+    weights_c(beside_x).start()
+    weights_c(beside_y).start()
+    send_rows(1)
+    for part in range(2, chunks):
         serve(part)
-    wait(gy_landed, gathered.at[other_chips])
-    for step in range(1, chips):
-        weights_c(step).start()
-    serve(chunks - 1)
+    for step in range(experts):
+        wait(gd_landed.at[step], gathered.at[0, 0])
+    weights_c(across_both).start()
+    for part in range(2, chunks):
+        send_rows(part)
 
     def column(index, begin=0, end=LANES):
         block = columns[index, begin:end, :]
@@ -1077,12 +1110,13 @@
         if part > 0:
             jobs.append(gives_of(part - 1))
         beside(train(part), mixed_jobs(*jobs))
-        if part > 0:
+        if 0 < part < chunks - 1:
             send_slots(part - 1)
 
-    for part in range(size.groups):
-        base = part * size.second
-        for expert in range(experts):
+    for turn_no in range(experts):
+        expert = expert_at(turn_no)
+        for part in range(size.groups):
+            base = part * size.second
             grads[part, expert, : size.first, :] = sum_first[
                 expert, part * size.first : (part + 1) * size.first, :
             ].astype(BF)
@@ -1092,8 +1126,8 @@
             grads[part, expert, size.first :, LANES:] = sum_second[
                 expert, base + half : base + 2 * half, :
             ].astype(BF)
-    for step in range(1, chips + 1):
-        sums_c(step % chips).start()
+        for step in range(1, chips + 1):
+            sums_c(turn_no, step % chips).start()
     for expert in range(experts):
         per = HID // LANES
         for piece in range(per):
@@ -1140,6 +1174,17 @@
     whole_loss = jnp.sum(loss_sum[...], 1, keepdims=True)
     put(small_part, at_loss, jnp.where(lane == 0, whole_loss, 0.0))
     loop(1, devices, lambda step: give_small(step, False).start())
+    for turn_no in range(experts):
+        expert = expert_at(turn_no)
+        wait(sc_landed.at[turn_no], core_got.at[expert])
+        for step in range(1, chips + 1):
+            other = turned(chip, chips, step % chips, False)
+            core_sum[expert, other] = (
+                grads[other * 2 + core, expert].astype(F32) + core_got[expert, other].astype(F32)
+            ).astype(BF)
+            if step < chips:
+                sums_y(turn_no, step).start()
+    send_slots(chunks - 2)
     for job in gives_of(chunks - 1):
         job()
     send_slots(chunks - 1)
@@ -1158,33 +1203,27 @@
 
         loop(0, devices // batch, some, devices // batch)
 
-    wait(sc_landed, core_got)
-    for step in range(1, chips + 1):
-        other = turned(chip, chips, step % chips, False)
-        core_sum[other] = (
-            grads[other * 2 + core].astype(F32) + core_got[other].astype(F32)
-        ).astype(BF)
-        if step < chips:
-            sums_y(step, False).start()
-    collect(0)
-    wait(small_landed, small_got.at[others])
-    small_got[me] = small_part[own_lines(me), :]
-    small_sum[own_lines(me), :] = jnp.sum(small_got[...], 0)
-    loop(1, devices, lambda step: give_whole(step, False).start())
-    for part in range(1, chunks - 1):
+    for part in range(chunks - 2):
         collect(part)
-    wait(sy_landed, chip_got.at[other_chips])
-    total = core_sum[chip].astype(F32)
-    for step in range(1, chips):
-        total = total + chip_got[step].astype(F32)
-    chip_sum[...] = total.astype(BF)
-    for step in range(1, experts):
-        sums_z(step, False).start()
+    for turn_no in range(experts):
+        expert = expert_at(turn_no)
+        wait(sy_landed.at[turn_no], chip_got.at[expert, other_chips])
+        total = core_sum[expert, chip].astype(F32)
+        for step in range(1, chips):
+            total = total + chip_got[expert, step].astype(F32)
+        if turn_no + 1 < experts:
+            chip_sum[expert] = total.astype(BF)
+            sums_z(turn_no).start()
+        if turn_no == 0:
+            wait(small_landed, small_got.at[others])
+            small_got[me] = small_part[own_lines(me), :]
+            small_sum[own_lines(me), :] = jnp.sum(small_got[...], 0)
+            loop(1, devices, lambda step: give_whole(step, False).start())
+    collect(chunks - 2)
     collect(chunks - 1)
     wait(sz_landed, z_got.at[other_experts])
-    total = chip_sum[expert_here].astype(F32)
-    for step in range(1, experts):
-        total = total + z_got[step].astype(F32)
+    for turn_no in range(experts - 1):
+        total = total + z_got[turn_no].astype(F32)
     first_grad[...] = total[: size.first]
     second_grad[:half, :] = total[size.first :, :LANES]
     second_grad[half:, :] = total[size.first :, LANES:]
@@ -1200,7 +1239,7 @@
     wait(gy_sent, gathered.at[other_chips])
     wait(gc_sent, gathered.at[pl.ds(0, chips)])
     wait(sc_sent, core_got)
-    wait(sy_sent, core_sum.at[other_chips])
+    wait(sy_sent, core_sum.at[:, other_chips])
     wait(sz_sent, chip_sum.at[other_experts])
 
 
@@ -1267,7 +1306,7 @@
     flat_lines = -(-count // LANES)
     exchange = vm((chunks, devices, EMB, LANES), BF)
     weights = vm((groups, experts, size.pack, HID), BF)
-    of_chips = vm((chips, experts, size.pack, HID), BF)
+    of_chips = vm((experts, chips, size.pack, HID), BF)
     of_chip = vm((experts, size.pack, HID), BF)
     table_grad, first_grad, second_grad, flat = call(
         functools.partial(step_kernel, size),
@@ -1330,8 +1369,9 @@
         ]
         + [dma, dma, dma, dma((chunks,)), dma, dma((chunks,))]
         + [dma] * 5
-        + [dma((experts,))]
-        + [dma] * 10,
+        + [dma((experts,)), dma, dma((experts,)), dma((experts,)), dma((experts,))]
+        + [dma] * 5
+        + [dma((experts,)), dma, dma((experts,))],
         0,
     )(
         requests[0],

time: 78 us -> 72.5 us (0.929)
  Pallas kernels: 74.2 us -> 68.6 us
    pallas_call x2, Pallas kernels: 74.2 us -> 68.6 us  [call(): pl.pallas_call(kernel, out_shape=outs, in_specs=[vmem] * len(args), out_s...]
where the time goes in v5:
time: 72.5 us; the launch traced here: 72.3 us
  Pallas kernels  68.6 us (95%)
  local copies, waits for them, and re-layouts  2.15 us (3%)
  other arithmetic  0.75 us (1%)
    pallas_call x2, Pallas kernels, call(): pl.pallas_call(kernel, out_shape=outs, in_specs=[vmem] * len(args), out_s...  68.6 us
    reshape x1, local copies, waits for them, and re-layouts, local(): jnp.pad(small, (0, flat_lines * LANES - count)).reshape(flat_lines, LANES)  1.54 us

profile of v5, /device:TPU:0, one launch (start us, length us, event | category | flops | bytes accessed | tf_op | source)
XLA Modules:
  0.0 72.3 jit_solution(15243393585875121376)
XLA Ops:
  0.6 1.5 %pad_bitcast_fusion.small = f32[185,128]{1,0:T(8,128)} fusion(f32[23626]{0:T(1024)} %param.31), kind=kLoop, calls=%fused_computation.4 | loop fusion | bytes 189224 | tf_op jit(solution)/shard_map/reshape | solution.py:1385
  2.2 66.1 %shard_map.264 = (f32[256,256]{1,0:T(8,128)}, f32[64,256]{1,0:T(8,128)}, f32[32,128]{1,0:T(8,128)}, f32[256,128]{1,0:T(8,128)}) custom-call(s32[8,4,512]{2,1,0:T(4,128)} %bitcast.38, s32[26,1024]{1,0:T(8,128)} %bitcast.33, f32[13,1024]{1,0:T(8,128)} %bitcast.39, s32[2,1024]{1,0:T(2,128)} %bitcast.44, s32[2,1024]{1,0:T(2,128)} %bitcast.45, ...), custom_call_target="tpu_custom_call" | custom-call | tf_op jit(solution)/shard_map/pallas_call | solution.py:1268
  68.3 0.0 copy-start
  68.3 0.0 copy-start.1
  68.3 0.0 copy-start.2
  68.3 0.0 copy-start.3
  68.3 2.5 %shard_map.265 = (f32[16,4096]{1,0:T(8,128)}, f32[16,4096]{1,0:T(8,128)}, f32[16,4096]{1,0:T(8,128)}, f32[64,256]{1,0:T(8,128)}, f32[64,256]{1,0:T(8,128)}, /*in...) custom-call(f32[256,256]{1,0:T(8,128)} %get-tuple-element.27.refs_0_, ...), custom_call_target="tpu_custom_call" | custom-call | tf_op jit(solution)/shard_map/pallas_call | solution.py:1268
  70.9 0.0 copy-done
  70.9 0.0 copy-done.1
  70.9 0.0 copy-done.2
  70.9 0.0 copy-done.3
  70.9 0.7 %multiply_subtract_fusion = (f32[23626]{0:T(1024)}, f32[23626]{0:T(1024)}, f32[23626]{0:T(1024)}) fusion(f32[23626]{0:T(1024)S(1)} %copy-done, f32[32768]{0:T(1024)S(1)} %bitcast.34, f32[23626]{0:T(1024)S(1)} %copy-done.1, f32[23626]{0:T(1024)S(1)} %copy-done.2), kind=kLoop, calls=%fused_computation.2 | loop fusion | flops 354390 | bytes 661528 | tf_op jit(solution)/shard_map/sub | solution.py:52
  71.7 0.6 slice.8
Async XLA Ops:
  68.3 2.6 %copy-start = (f32[23626]{0:T(1024)S(1)}, f32[23626]{0:T(1024)}, u32[]{:S(2)}) copy-start(f32[23626]{0:T(1024)} %param.31) | copy-start | bytes 283516
  68.3 2.6 %copy-start.1 = (f32[23626]{0:T(1024)S(1)}, f32[23626]{0:T(1024)}, u32[]{:S(2)}) copy-start(f32[23626]{0:T(1024)} %param.32) | copy-start | bytes 283516
  68.3 2.6 %copy-start.2 = (f32[23626]{0:T(1024)S(1)}, f32[23626]{0:T(1024)}, u32[]{:S(2)}) copy-start(f32[23626]{0:T(1024)} %param.33) | copy-start | bytes 283516
  68.3 2.6 %copy-start.3 = (f32[256,128]{1,0:T(8,128)S(1)}, f32[256,128]{1,0:T(8,128)}, u32[]{:S(2)}) copy-start(f32[256,128]{1,0:T(8,128)} %get-tuple-element.26) | copy-start | bytes 393220

commit v6 on v5

--- a/solution.py
+++ b/solution.py
@@ -438,11 +438,12 @@
 
 
 def spread(index, extent, width):
-    return lax.broadcasted_iota(jnp.int32, (extent, width), 0) == index
+    lines = lax.broadcasted_iota(jnp.int32, (extent, width), 0).astype(F32).astype(BF)
+    return lines == index.astype(F32).astype(BF)
 
 
 def as_low(flag):
-    return jnp.where(flag, 1.0, 0.0).astype(BF)
+    return jnp.where(flag, jnp.ones((), BF), jnp.zeros((), BF))
 
 
 def look_up(cells, key, high, levels):
@@ -1244,7 +1245,9 @@
 
 
 def update(size, *refs):
-    grads, state, results = refs[:3], refs[3:12], refs[12:]
+    grads, state, flat, results, loss = refs[:3], refs[3:12], refs[12], refs[13:22], refs[22]
+    spot = offsets(size.experts)[-1]
+    loss[...] = flat[spot // LANES : spot // LANES + 1, spot % LANES : spot % LANES + 1]
     table_grad = grads[0][...]
     wide = jnp.concatenate(
         [table_grad[b * EMB : (b + 1) * EMB] for b in range(size.rows // KEYS)], 1
@@ -1389,15 +1392,15 @@
     seconds = (second_w[0], second_m[0], second_v[0])
     new = call(
         functools.partial(update, size),
-        [shape(a.shape) for a in tables + firsts + seconds],
+        [shape(a.shape) for a in tables + firsts + seconds] + [shape((1, 1))],
         [],
-    )(table_grad, first_grad, second_grad, *tables, *firsts, *seconds)
+    )(table_grad, first_grad, second_grad, *tables, *firsts, *seconds, flat)
     flat = flat.reshape(-1)
     new_small = adamw(small, small_m, small_v, flat[:count], 0.15)
     return (
-        (flat[count],)
+        (new[9].reshape(()),)
         + tuple(a.T for a in new[:3])
-        + tuple(a[None] for a in new[3:])
+        + tuple(a[None] for a in new[3:9])
         + tuple(new_small)
     )
 

time: 72.5 us -> 71.3 us (0.983)
  no operation moved by 1% of the time
where the time goes in v6:
time: 71.3 us; the launch traced here: 71.1 us
  Pallas kernels  68.1 us (96%)
  local copies, waits for them, and re-layouts  1.56 us (2%)
  other arithmetic  0.75 us (1%)
  between operations  0.72 us (1%)
    pallas_call x2, Pallas kernels, call(): pl.pallas_call(kernel, out_shape=outs, in_specs=[vmem] * len(args), out_s...  68.1 us
    reshape x1, local copies, waits for them, and re-layouts, local(): jnp.pad(small, (0, flat_lines * LANES - count)).reshape(flat_lines, LANES)  1.54 us

profile of v6, /device:TPU:0, one launch (start us, length us, event | category | flops | bytes accessed | tf_op | source)
XLA Modules:
  0.0 71.1 jit_solution(575995999663821106)
XLA Ops:
  0.6 1.5 %pad_bitcast_fusion.small = f32[185,128]{1,0:T(8,128)} fusion(f32[23626]{0:T(1024)} %param.31), kind=kLoop, calls=%fused_computation.4 | loop fusion | bytes 189224 | tf_op jit(solution)/shard_map/reshape | solution.py:1388
  2.2 65.5 %shard_map.264 = (f32[256,256]{1,0:T(8,128)}, f32[64,256]{1,0:T(8,128)}, f32[32,128]{1,0:T(8,128)}, f32[256,128]{1,0:T(8,128)}) custom-call(s32[8,4,512]{2,1,0:T(4,128)} %bitcast.39, s32[26,1024]{1,0:T(8,128)} %bitcast.34, f32[13,1024]{1,0:T(8,128)} %bitcast.40, s32[2,1024]{1,0:T(2,128)} %bitcast.43, s32[2,1024]{1,0:T(2,128)} %bitcast.44, ...), custom_call_target="tpu_custom_call" | custom-call | tf_op jit(solution)/shard_map/pallas_call | solution.py:1271
  67.7 0.0 copy-start
  67.7 0.0 copy-start.1
  67.7 0.0 copy-start.2
  67.7 0.0 copy-start.3
  67.7 2.6 %shard_map.265 = (f32[16,4096]{1,0:T(8,128)}, f32[16,4096]{1,0:T(8,128)}, f32[16,4096]{1,0:T(8,128)}, f32[64,256]{1,0:T(8,128)}, f32[64,256]{1,0:T(8,128)}, /*in...) custom-call(f32[256,256]{1,0:T(8,128)} %get-tuple-element.27.refs_0_, ...), custom_call_target="tpu_custom_call" | custom-call | tf_op jit(solution)/shard_map/pallas_call | solution.py:1271
  70.3 0.0 copy-done
  70.3 0.0 copy-done.1
  70.4 0.0 copy-done.2
  70.4 0.0 copy-done.3
  70.4 0.7 %multiply_subtract_fusion = (f32[23626]{0:T(1024)}, f32[23626]{0:T(1024)}, f32[23626]{0:T(1024)}) fusion(f32[23626]{0:T(1024)S(1)} %copy-done.1, f32[32768]{0:T(1024)S(1)} %bitcast.29, f32[23626]{0:T(1024)S(1)} %copy-done.2, f32[23626]{0:T(1024)S(1)} %copy-done.3), kind=kLoop, calls=%fused_computation.2 | loop fusion | flops 354390 | bytes 661528 | tf_op jit(solution)/shard_map/sub | solution.py:52
Async XLA Ops:
  67.7 2.7 %copy-start = (f32[256,128]{1,0:T(8,128)S(1)}, f32[256,128]{1,0:T(8,128)}, u32[]{:S(2)}) copy-start(f32[256,128]{1,0:T(8,128)} %get-tuple-element.30.refs_12_) | copy-start | bytes 393220
  67.7 2.7 %copy-start.1 = (f32[23626]{0:T(1024)S(1)}, f32[23626]{0:T(1024)}, u32[]{:S(2)}) copy-start(f32[23626]{0:T(1024)} %param.31) | copy-start | bytes 283516
  67.7 2.7 %copy-start.2 = (f32[23626]{0:T(1024)S(1)}, f32[23626]{0:T(1024)}, u32[]{:S(2)}) copy-start(f32[23626]{0:T(1024)} %param.32) | copy-start | bytes 283516
  67.7 2.7 %copy-start.3 = (f32[23626]{0:T(1024)S(1)}, f32[23626]{0:T(1024)}, u32[]{:S(2)}) copy-start(f32[23626]{0:T(1024)} %param.33) | copy-start | bytes 283516

commit v7 on v6

--- a/solution.py
+++ b/solution.py
@@ -788,10 +788,10 @@
             :, block * KEYS : (block + 1) * KEYS
         ].astype(BF)
     pl.semaphore_wait(barrier, devices - 1)
+    loop(1, devices, lambda step: ask(step, False).start())
     for step in range(1, experts):
         weights_z(step).start()
     spread_weights(0)
-    loop(1, devices, lambda step: ask(step, False).start())
 
     vectors[...] = jnp.zeros_like(vectors)
     vectors[: at_dense // LANES, :] = small[: at_dense // LANES, :]

time: 71.3 us -> 69.1 us (0.969)
  Pallas kernels: 68.1 us -> 65.8 us
    pallas_call x2, Pallas kernels: 68.1 us -> 65.8 us  [call(): pl.pallas_call(kernel, out_shape=outs, in_specs=[vmem] * len(args), out_s...]
where the time goes in v7:
time: 69.1 us; the launch traced here: 68.9 us
  Pallas kernels  65.8 us (95%)
  local copies, waits for them, and re-layouts  1.56 us (2%)
  other arithmetic  0.75 us (1%)
  between operations  0.72 us (1%)
    pallas_call x2, Pallas kernels, call(): pl.pallas_call(kernel, out_shape=outs, in_specs=[vmem] * len(args), out_s...  65.8 us
    reshape x1, local copies, waits for them, and re-layouts, local(): jnp.pad(small, (0, flat_lines * LANES - count)).reshape(flat_lines, LANES)  1.54 us

profile of v7, /device:TPU:0, one launch (start us, length us, event | category | flops | bytes accessed | tf_op | source)
XLA Modules:
  0.0 68.9 jit_solution(12540587375425942607)
XLA Ops:
  0.6 1.5 %pad_bitcast_fusion.small = f32[185,128]{1,0:T(8,128)} fusion(f32[23626]{0:T(1024)} %param.31), kind=kLoop, calls=%fused_computation.4 | loop fusion | bytes 189224 | tf_op jit(solution)/shard_map/reshape | solution.py:1388
  2.2 63.2 %shard_map.264 = (f32[256,256]{1,0:T(8,128)}, f32[64,256]{1,0:T(8,128)}, f32[32,128]{1,0:T(8,128)}, f32[256,128]{1,0:T(8,128)}) custom-call(s32[8,4,512]{2,1,0:T(4,128)} %bitcast.39, s32[26,1024]{1,0:T(8,128)} %bitcast.34, f32[13,1024]{1,0:T(8,128)} %bitcast.40, s32[2,1024]{1,0:T(2,128)} %bitcast.43, s32[2,1024]{1,0:T(2,128)} %bitcast.44, ...), custom_call_target="tpu_custom_call" | custom-call | tf_op jit(solution)/shard_map/pallas_call | solution.py:1271
  65.4 0.0 copy-start
  65.4 0.0 copy-start.1
  65.4 0.0 copy-start.2
  65.5 0.0 copy-start.3
  65.5 2.6 %shard_map.265 = (f32[16,4096]{1,0:T(8,128)}, f32[16,4096]{1,0:T(8,128)}, f32[16,4096]{1,0:T(8,128)}, f32[64,256]{1,0:T(8,128)}, f32[64,256]{1,0:T(8,128)}, /*in...) custom-call(f32[256,256]{1,0:T(8,128)} %get-tuple-element.27.refs_0_, ...), custom_call_target="tpu_custom_call" | custom-call | tf_op jit(solution)/shard_map/pallas_call | solution.py:1271
  68.1 0.0 copy-done
  68.1 0.0 copy-done.1
  68.1 0.0 copy-done.2
  68.1 0.0 copy-done.3
  68.1 0.7 %multiply_subtract_fusion = (f32[23626]{0:T(1024)}, f32[23626]{0:T(1024)}, f32[23626]{0:T(1024)}) fusion(f32[23626]{0:T(1024)S(1)} %copy-done.1, f32[32768]{0:T(1024)S(1)} %bitcast.29, f32[23626]{0:T(1024)S(1)} %copy-done.2, f32[23626]{0:T(1024)S(1)} %copy-done.3), kind=kLoop, calls=%fused_computation.2 | loop fusion | flops 354390 | bytes 661528 | tf_op jit(solution)/shard_map/sub | solution.py:52
Async XLA Ops:
  65.4 2.7 %copy-start = (f32[256,128]{1,0:T(8,128)S(1)}, f32[256,128]{1,0:T(8,128)}, u32[]{:S(2)}) copy-start(f32[256,128]{1,0:T(8,128)} %get-tuple-element.30.refs_12_) | copy-start | bytes 393220
  65.4 2.7 %copy-start.1 = (f32[23626]{0:T(1024)S(1)}, f32[23626]{0:T(1024)}, u32[]{:S(2)}) copy-start(f32[23626]{0:T(1024)} %param.31) | copy-start | bytes 283516
  65.4 2.7 %copy-start.2 = (f32[23626]{0:T(1024)S(1)}, f32[23626]{0:T(1024)}, u32[]{:S(2)}) copy-start(f32[23626]{0:T(1024)} %param.32) | copy-start | bytes 283516
  65.5 2.7 %copy-start.3 = (f32[23626]{0:T(1024)S(1)}, f32[23626]{0:T(1024)}, u32[]{:S(2)}) copy-start(f32[23626]{0:T(1024)} %param.33) | copy-start | bytes 283516
